TPU v7x, 32 devices: a whole 2x2x4 slice. The times are simulated.
32 devices in a mesh: rows: 4 (over x, core), cols: 8 (over z, y).
Axes of the slice: x: 2, y: 2, z: 4, core: 2. Of those that a mesh axis runs over, the one named last changes fastest.
Arguments:
- field: bfloat16 [32, 16, 32768], P('cols', 'rows'), may hold values from -6 to 6
- depth_kernel: float32 [7, 7, 32], replicated, may hold values from -0.875 to 0.875
- point_weight: bfloat16 [32, 32], replicated, may hold values from -1 to 1
- point_bias: float32 [32], replicated, may hold values from -3 to 3
- vert_weight: bfloat16 [2, 288, 32], replicated, may hold values from -0.375 to 0.375
- vert_bias: float32 [2, 32], replicated, may hold values from -3 to 3
- exhaust: bfloat16 [16384, 32], P(('rows', 'cols')), may hold values from -6 to 6
- owner: int32 [16384, 1], P(('rows', 'cols')), may hold values from 0 to 7; in each aligned block of 512 rows (0 to 511, 512 to 1023, ...) at most 128 rows name the same one
- cells: int32 [16384], P(('rows', 'cols')), may hold values from 0 to 16383
Outputs:
- advanced: bfloat16 [32, 16, 32768], P(None, 'rows', 'cols')
Inputs may be any that keep to these rules, and one draw needn't show every extreme that they name: `owner`: among the 512 rows of one device, no tile is named by more than 128 rows, a bound that some block reaches.
All inputs are finite; a program needn't handle non-finite values.
Results may differ from a plain program's by a relative error of at most 0.0055.
Values may be sent and summed in bfloat16 or wider, within the bound.
No kernel may reach another device: no remote copies, remote signals or barrier semaphores. Data moves between devices by JAX's collectives and lax.ppermute only.
A program may use at most 128 MiB of HBM per device.

v0:
```python
import jax
import jax.numpy as jnp
from jax import lax
from jax.sharding import PartitionSpec as P

C = 32
X = 1024
Z = 32
YB = 4
KH = 7
KV = 9
LAYERS = 2


def padded_2(block, sides, width):
    for axis, dim in sides:
        count = lax.axis_size(axis)
        forward = [(i, i + 1) for i in range(count - 1)]
        backward = [(target, source) for source, target in forward]
        low = lax.ppermute(
            lax.slice_in_dim(block, block.shape[dim] - width, None, axis=dim), axis, forward
        )
        high = lax.ppermute(lax.slice_in_dim(block, 0, width, axis=dim), axis, backward)
        block = jnp.concatenate([low, block, high], axis=dim)
    return block


def block_matrix(weight):
    return jnp.kron(jnp.eye(128 // C, dtype=jnp.bfloat16), weight)


def horizontal(band, depth_kernel, point_weight, point_bias):
    height = band.shape[1] - 6
    merged = band.shape[2] - 6 * C
    tiled = jnp.tile(depth_kernel, (1, 1, merged // C))
    total = jnp.zeros((band.shape[0], height, merged), jnp.float32)
    for i in range(KH):
        for j in range(KH):
            total = (
                total
                + band[:, i : i + height, j * C : j * C + merged].astype(jnp.float32) * tiled[i, j]
            )
    depth_b = total.astype(jnp.bfloat16).reshape(band.shape[0], height, merged // 128, 128)
    proj = jnp.einsum(
        "zywk,kd->zywd", depth_b, block_matrix(point_weight), preferred_element_type=jnp.float32
    )
    proj = proj.reshape(band.shape[0], height, merged)
    bias_row = jnp.tile(point_bias, merged // C)
    center = band[:, 3 : 3 + height, 3 * C : 3 * C + merged].astype(jnp.float32)
    return (center + jax.nn.gelu(proj + bias_row)).astype(jnp.bfloat16)


def vertical(level_field, vert_weight, vert_bias):
    levels = level_field.shape[0]
    height = level_field.shape[1]
    merged = level_field.shape[2]
    current = level_field.reshape(levels, height, merged // 128, 128)
    result = None
    for layer in range(LAYERS):
        padded = jnp.pad(current, ((4, 4), (0, 0), (0, 0), (0, 0)))
        conv = jnp.zeros(current.shape, jnp.float32)
        for k in range(KV):
            conv = conv + jnp.einsum(
                "zywk,kd->zywd",
                padded[k : k + levels],
                block_matrix(vert_weight[layer, k * C : (k + 1) * C]),
                preferred_element_type=jnp.float32,
            )
        bias_row = jnp.tile(vert_bias[layer], 128 // C)
        result = current.astype(jnp.float32) + jax.nn.gelu(conv + bias_row)
        if layer < LAYERS - 1:
            current = result.astype(jnp.bfloat16)
    return result.reshape(levels, height, merged)


def body(
    field, depth_kernel, point_weight, point_bias, vert_weight, vert_bias, exhaust, owner, cells
):
    columns = lax.axis_size("cols")
    tile_x = X // columns
    rimmed = padded_2(field, (("rows", 1),), 3)
    band = jnp.pad(rimmed, ((0, 0), (0, 0), (3 * C, 3 * C)))
    mixed = horizontal(band, depth_kernel, point_weight, point_bias)
    pre = vertical(
        lax.all_to_all(mixed, "cols", split_axis=2, concat_axis=0, tiled=True),
        vert_weight,
        vert_bias,
    )
    where_to = owner[:, 0]
    got_rows, got_owner, got_cells = (
        lax.all_gather(exhaust, "cols", axis=0, tiled=True),
        lax.all_gather(where_to, "cols", axis=0, tiled=True),
        lax.all_gather(cells, "cols", axis=0, tiled=True),
    )
    valid = got_owner == lax.axis_index("cols")
    tile_cells = Z * YB * tile_x
    target = jnp.where(valid, got_cells, tile_cells)
    source = (
        jnp.zeros((tile_cells, C), jnp.float32)
        .at[target]
        .add(got_rows.astype(jnp.float32), mode="drop")
    )
    source = source.reshape(Z, YB, tile_x * C)
    return (pre + source).astype(jnp.bfloat16)


def solution(mesh):
    placed = (
        P("cols", "rows", None),
        P(),
        P(),
        P(),
        P(),
        P(),
        P(("rows", "cols"), None),
        P(("rows", "cols"), None),
        P(("rows", "cols")),
    )
    return jax.shard_map(
        body, mesh=mesh, in_specs=placed, out_specs=P(None, "rows", "cols"), check_vma=False
    )
```

profile of v0, /device:TPU:2, one launch (start us, length us, event | category | flops | bytes accessed | tf_op | source)
XLA Modules:
  0.0 526.6 jit_solution(301205165318472446)
XLA Ops:
  0.0 2.5 fusion.89
  2.5 0.7 copy.380
  3.3 1.9 collective-permute-start
  5.2 1.6 copy.381
  6.8 3.6 collective-permute-start.1
  10.5 10.2 %tile.14 = f32[7,7,1024,32]{3,2,1,0:T(8,128)} broadcast(f32[7,7,32]{2,1,0:T(8,128)S(1)} %copy-done.57), dimensions={0,1,3} | broadcast | bytes 6428800 | tf_op jit(solution)/shard_map/tile | solution.py:35
  20.6 17.0 %tile.30 = f32[7,7,32768]{2,1,0:T(8,128)} reshape(f32[7,7,1024,32]{3,2,1,0:T(8,128)} %tile.14) | data formatting | bytes 12845056 | tf_op jit(solution)/shard_map/tile | solution.py:35
  37.6 11.2 %fusion.86 = (f32[1,1,32768]{2,1,0:T(1,128)S(1)}, f32[1,1,32768]{2,1,0:T(1,128)S(1)}, f32[1,1,32768]{2,1,0:T(1,128)S(1)}, f32[1,1,32768]{2,1,0:T(1,128)}, f32[1,...) fusion(f32[7,7,32768]{2,1,0:T(8,128)} %tile.30), kind=kLoop, calls=%fused_computation.148 | loop fusion | bytes 4980736 | tf_op jit(solution)/shard_map/slice | solution.py:41
  48.8 11.3 %fusion.87 = (f32[1,1,32768]{2,1,0:T(1,128)}, f32[1,1,32768]{2,1,0:T(1,128)}, f32[1,1,32768]{2,1,0:T(1,128)}, f32[1,1,32768]{2,1,0:T(1,128)}, f32[1,1,32768]{2,1...) fusion(f32[7,7,32768]{2,1,0:T(8,128)} %tile.30), kind=kLoop, calls=%fused_computation.149 | loop fusion | bytes 4980736 | tf_op jit(solution)/shard_map/slice | solution.py:41
  60.1 7.5 %fusion.88 = (f32[1,1,32768]{2,1,0:T(1,128)}, f32[1,1,32768]{2,1,0:T(1,128)}, f32[1,1,32768]{2,1,0:T(1,128)}, f32[1,1,32768]{2,1,0:T(1,128)}, f32[1,1,32768]{2,1...) fusion(f32[7,7,32768]{2,1,0:T(8,128)} %tile.30), kind=kLoop, calls=%fused_computation.150 | loop fusion | bytes 2883584 | tf_op jit(solution)/shard_map/slice | solution.py:41
  67.8 0.7 reshape.183
  68.5 0.8 add.315
  69.4 0.7 copy.336
  70.1 1.8 copy.337
  72.3 4.3 fusion.5
  76.9 55.3 %add_convert_fusion.1 = bf16[4,4,32768]{2,1,0:T(4,128)(2,1)S(1)} fusion(bf16[4,4,32768]{2,1,0:T(4,128)(2,1)S(1)} %copy-done, bf16[4,3,32768]{2,1,0:T(4,128)(2,1)S(1)} %copy.337, bf16[4,3,32768]{2,1,0:T(4,128)(2,1)S(1)} %copy.336, bf16[4,10,32960]{2,1,0:T(8,128)(2,1)S(1)} %fusion.5, f32[32768]{0:T(1024)S(1)} %bitcast.181, f32[32768]{0:T(1024)S(1)} %bitcast.182, ...), kind=kLoop, calls=%fused_computation.62 | loop fusion | flops 86507520 | bytes 54132736 | tf_op jit(solution)/shard_map/convert_element_type | solution.py:43
  132.3 1.9 reshape.164
  134.2 1.6 fusion.83
  135.9 1.9 reshape.165
  137.8 3.4 fusion.20
  141.1 32.0 %copy.340 = bf16[4,4,32768]{1,0,2:T(4,128)(2,1)} copy(bf16[4,4,32768]{2,1,0:T(4,128)(2,1)S(1)} %fusion.20) | data formatting | bytes 2097152 | tf_op jit(solution)/shard_map/convert_element_type | solution.py:50
  173.2 72.0 %reshape.224 = bf16[8,2,32768]{2,1,0:T(2,128)(2,1)} reshape(bf16[32768,4,4]{2,1,0:T(4,128)(2,1)} %bitcast.177) | data formatting | bytes 2097152
  245.2 6.0 %all-to-all-start = ((bf16[8,2,32768]{2,1,0:T(2,128)(2,1)}), bf16[8,2,32768]{2,1,0:T(2,128)(2,1)S(1)}, u32[]{:S(2)}, u32[]{:S(2)}) async-start(bf16[8,2,32768]{2,1,0:T(2,128)(2,1)} %reshape.224), calls=%async_computation | async-start | bytes 2097152 | tf_op jit(solution)/shard_map/all_to_all | solution.py:85
  252.8 1.6 broadcast_multiply_fusion
  254.4 0.7 reshape.189
  255.1 0.7 reshape.188
  255.9 0.7 reshape.187
  256.6 0.7 reshape.186
  257.3 0.7 reshape.185
  258.1 0.7 reshape.184
  258.8 0.7 reshape.190
  259.6 0.7 reshape.191
  260.3 0.7 reshape.192
  261.1 0.8 slice_bitcast_fusion.18
  262.4 0.7 reshape.193
  263.2 0.7 reshape.198
  263.9 0.7 reshape.199
  264.6 0.7 reshape.200
  265.4 0.7 reshape.201
  266.2 32.0 %all_gather.11 = bf16[4096,32]{0,1:T(8,128)(2,1)S(1)} all-gather(bf16[512,32]{0,1:T(8,128)(2,1)} %param.15), channel_id=1, replica_groups=mesh['rows'=4,'cols'=8] {'cols'}, dimensions={0}, use_global_device_ids=true | all-gather | bytes 294912 | tf_op jit(solution)/shard_map/all_gather | solution.py:91
  298.5 26.0 %all-gather = s32[4096,1]{0,1:T(1,128)S(1)} all-gather(s32[512,1]{0,1:T(1,128)S(1)} %copy-done.60), channel_id=2, replica_groups=mesh['rows'=4,'cols'=8] {'cols'}, dimensions={0}, use_global_device_ids=true | all-gather | bytes 18432 | tf_op jit(solution)/shard_map/all_gather | solution.py:92
  324.5 26.0 %all-gather.1 = s32[8,1,512]{2,1,0:T(1,128)S(1)} all-gather(s32[1,1,512]{2,1,0:T(1,128)S(1)} %bitcast.230), channel_id=1, replica_groups=mesh['rows'=4,'cols'=8] {'cols'}, dimensions={0}, use_global_device_ids=true | all-gather | bytes 18432 | tf_op jit(solution)/shard_map/all_gather | solution.py:93
  350.6 26.1 %scatter_custom_fusion = f32[16384,32]{1,0:T(8,128)} fusion(s32[4096]{0:T(1024)S(1)} %compare_select_fusion, f32[4096,32]{1,0:T(8,128)S(1)} %copy.360, f32[]{:T(128)} %constant.14.clone.1), kind=kCustom, calls=%fused_computation.9 | custom fusion | flops 131072 | bytes 2097156 | tf_op jit(solution)/shard_map/scatter-add | solution.py:101
  376.7 6.5 %reshape.168 = f32[32,4,4096]{2,1,0:T(4,128)S(1)} reshape(f32[16384,32]{1,0:T(8,128)} %scatter_custom_fusion) | data formatting | bytes 4194304 | tf_op jit(solution)/shard_map/reshape | solution.py:103
  383.2 74.0 %reshape.225 = bf16[32768,4,4]{2,1,0:T(4,128)(2,1)} reshape(bf16[8,2,32768]{2,1,0:T(2,128)(2,1)S(1)} %all-to-all-done) | data formatting | bytes 2097152
  457.3 45.1 %copy.341 = bf16[4,4,8,4096]{3,1,0,2:T(4,128)(2,1)} copy(bf16[4,4,8,4096]{1,0,3,2:T(4,128)(2,1)} %bitcast.178) | data formatting | bytes 2097152 | tf_op jit(solution)/shard_map/all_to_all | solution.py:85
  502.3 2.3 reshape.166
  504.7 0.4 fusion.71
  505.4 0.4 fusion.73
  506.2 0.4 fusion.75
  506.9 0.4 fusion.77
  507.7 0.4 fusion.79
  508.5 0.4 fusion.81
  509.2 0.4 fusion.69
  510.0 0.4 fusion.67
  510.7 1.7 fusion.36
  512.4 0.4 fusion.56
  512.8 0.4 fusion.58
  513.2 0.4 fusion.60
  513.7 0.4 fusion.62
  515.2 0.4 fusion.54
  517.5 2.8 fusion.44
  520.3 2.9 reshape.167
  523.2 3.2 add_convert_fusion
  (165 shorter events, 8.8 us)
Async XLA Ops:
  2.5 8.0 %copy-start.57 = (f32[7,7,32]{2,1,0:T(8,128)S(1)}, f32[7,7,32]{2,1,0:T(8,128)}, u32[]{:S(2)}) copy-start(f32[7,7,32]{2,1,0:T(8,128)} %param.10) | copy-start | bytes 18820
  3.3 66.1 %collective-permute-start = (bf16[4,3,32768]{2,0,1:T(4,128)(2,1)S(1)}, bf16[4,3,32768]{2,0,1:T(4,128)(2,1)S(1)}, u32[]{:S(2)}, u32[]{:S(2)}) collective-permute-start(bf16[4,3,32768]{2,0,1:T(4,128)(2,1)S(1)} %copy.380), channel_id=1, source_target_pairs={{0,8},{8,16},{16,24},{1,9},{9,17},{17,25},{2,10},{10,18},{18,26},{... | collective-permute-start | bytes 2359304 | tf_op jit(solution)/shard_map/ppermute | solution.py:20
  6.8 63.3 %collective-permute-start.1 = (bf16[4,3,32768]{2,0,1:T(4,128)(2,1)}, bf16[4,3,32768]{2,0,1:T(4,128)(2,1)}, u32[]{:S(2)}, u32[]{:S(2)}) collective-permute-start(bf16[4,3,32768]{2,0,1:T(4,128)(2,1)} %copy.381), channel_id=1, source_target_pairs={{8,0},{16,8},{24,16},{9,1},{17,9},{25,17},{10,2},{18,10},{26,18},{... | collective-permute-start | bytes 2359304 | tf_op jit(solution)/shard_map/ppermute | solution.py:23
  60.1 7.5 %copy-start.58 = (bf16[32,32]{1,0:T(8,128)(2,1)S(1)}, bf16[32,32]{1,0:T(8,128)(2,1)}, u32[]{:S(2)}) copy-start(bf16[32,32]{1,0:T(8,128)(2,1)} %param.11) | copy-start | bytes 6148
  60.1 8.4 %copy-start.62 = (f32[32]{0:T(128)S(1)}, f32[32]{0:T(128)}, u32[]{:S(2)}) copy-start(f32[32]{0:T(128)} %param.12) | copy-start | bytes 388
  67.6 0.9 copy-start.59
  68.5 3.3 copy-start
  71.9 4.7 copy-start.1
  71.9 4.7 copy-start.2
  71.9 4.7 copy-start.3
  71.9 4.7 copy-start.4
  71.9 4.7 copy-start.5
  71.9 4.7 copy-start.6
  72.0 4.7 copy-start.7
  72.0 4.7 copy-start.8
  72.0 4.7 copy-start.9
  72.0 4.7 copy-start.10
  72.0 4.7 copy-start.11
  72.0 4.7 copy-start.12
  72.0 4.7 copy-start.13
  72.0 4.7 copy-start.14
  72.0 4.7 copy-start.15
  72.0 4.7 copy-start.16
  72.1 4.7 copy-start.17
  72.1 4.7 copy-start.18
  72.1 4.7 copy-start.19
  72.1 4.7 copy-start.20
  72.1 4.7 copy-start.21
  72.1 4.7 copy-start.22
  72.1 4.7 copy-start.23
  72.1 4.7 copy-start.24
  72.1 4.7 copy-start.25
  72.1 4.7 copy-start.26
  72.2 4.7 copy-start.27
  72.2 4.7 copy-start.28
  72.2 4.7 copy-start.29
  72.2 4.7 copy-start.30
  72.2 4.7 copy-start.31
  72.2 4.7 copy-start.32
  72.2 4.7 copy-start.33
  72.2 4.7 copy-start.34
  72.2 4.7 copy-start.35
  72.2 4.7 copy-start.36
  72.3 4.7 copy-start.37
  72.3 4.7 copy-start.38
  72.3 4.7 copy-start.39
  132.3 1.9 copy-start.56
  135.9 1.9 copy-start.40
  245.1 6.0 %copy-start.41 = (bf16[2,288,32]{1,2,0:T(8,128)(2,1)S(1)}, bf16[2,288,32]{1,2,0:T(8,128)(2,1)}, u32[]{:S(2)}) copy-start(bf16[2,288,32]{1,2,0:T(8,128)(2,1)} %param.13) | copy-start | bytes 110596
  245.2 138.1 %all-to-all-start = ((bf16[8,2,32768]{2,1,0:T(2,128)(2,1)}), bf16[8,2,32768]{2,1,0:T(2,128)(2,1)S(1)}, u32[]{:S(2)}, u32[]{:S(2)}) async-start(bf16[8,2,32768]{2,1,0:T(2,128)(2,1)} %reshape.224), calls=%async_computation | async-start | bytes 2097152 | tf_op jit(solution)/shard_map/all_to_all | solution.py:85
  261.0 37.5 %copy-start.60 = (s32[512,1]{0,1:T(1,128)S(1)}, s32[512,1]{0,1:T(1,128)}, u32[]{:S(2)}) copy-start(s32[512,1]{0,1:T(1,128)} %param.16) | copy-start | bytes 6148
  261.0 63.5 %copy-start.61 = (s32[512]{0:T(512)S(1)}, s32[512]{0:T(512)}, u32[]{:S(2)}) copy-start(s32[512]{0:T(512)} %param.17) | copy-start | bytes 6148
  502.3 2.3 copy-start.47
  504.7 0.8 copy-start.48
  505.4 0.8 copy-start.49
  506.2 0.8 copy-start.50
  506.9 0.8 copy-start.51
  507.7 0.8 copy-start.52
  508.5 0.8 copy-start.53
  509.2 0.8 copy-start.54
  510.0 0.8 copy-start.55
  513.7 0.8 copy-start.42
  514.4 0.8 copy-start.43
  515.2 0.8 copy-start.44
  (2 other events, 1.5 us)
where the time goes:
time: 527 us
  local copies, waits for them, and re-layouts  323 us (61%)
  other arithmetic  94 us (18%)
  blocking collectives  84 us (16%)
  matrix products  12.7 us (2%)
  starting transfers between devices  11.5 us (2%)
    unnamed x130, local copies, waits for them, and re-layouts  153 us
    convert_element_type x1, other arithmetic, horizontal(): total.astype(jnp.bfloat16)  55.3 us
    all_to_all x1, local copies, waits for them, and re-layouts, body(): lax.all_to_all(mixed, 'cols', split_axis=2, concat_axis=0, tiled=True)  45.1 us
    convert_element_type x1, local copies, waits for them, and re-layouts, horizontal(): return (center + jax.nn.gelu(proj + bias_row)).astype(jnp.bfloat16)  32 us
    all_gather x1, blocking collectives, body(): lax.all_gather(exhaust, 'cols', axis=0, tiled=True)  32 us
    slice x3, local copies, waits for them, and re-layouts, horizontal(): tiled[i, j]  30 us
    another operation x2, local copies, waits for them, and re-layouts, horizontal(): tiled = jnp.tile(depth_kernel, (1, 1, merged // C))  27.1 us
    scatter-add x1, other arithmetic, body(): source = jnp.zeros((tile_cells, C), jnp.float32).at[target].add(got_rows....  26.1 us
  transfers between devices with their start and end apart: 3, of which 0 were waited for; matrix products, arithmetic and copies ran while one was open for 21% of the time, Pallas kernels for 0%

commit v1 on v0

v1 whole, which is shorter than its diff:
```python
import functools

import jax
import jax.numpy as jnp
from jax import lax
from jax.experimental import pallas as pl
from jax.experimental.pallas import tpu as pltpu
from jax.sharding import PartitionSpec as P

C = 32
KH = 7
KV = 9
SEG = 8
SL = SEG * C
HALF = SL // 2
PACK = 48
VMEM = 56 * 1024 * 1024
NT = (((1,), (1,)), ((), ()))
F32 = jnp.float32
BF16 = jnp.bfloat16


def params():
    return pltpu.CompilerParams(vmem_limit_bytes=VMEM)


def cost(flops, moved):
    return pl.CostEstimate(flops=flops, bytes_accessed=moved, transcendentals=0)


def whole(shape):
    return pl.BlockSpec(shape, lambda *_: (0,) * len(shape))


def gelu(x):
    return 0.5 * x * (1.0 + jnp.tanh(0.7978845608028654 * (x + 0.044715 * (x * x * x))))


def swap_matrix(outer, inner):
    size = outer * inner
    row = lax.broadcasted_iota(jnp.int32, (size, size), 0)
    column = lax.broadcasted_iota(jnp.int32, (size, size), 1)
    return (column == (row % outer) * inner + row // outer).astype(BF16)


def segment_kernel(field_ref, own_ref, first_ref, last_ref):
    levels, height, lanes = field_ref.shape
    rows = levels * height
    group = 256 // rows
    swap = swap_matrix(group, rows)
    stacked = []
    for s in range(group):
        piece = field_ref[:, :, s * SL : (s + 1) * SL]
        stacked.append(piece.reshape(rows, SL))
    mixed_up = jnp.concatenate(stacked, axis=0)
    got = jnp.dot(swap, mixed_up, preferred_element_type=F32).astype(BF16)
    for z in range(levels):
        for y in range(height):
            start = (z * height + y) * group
            piece = got[start : start + group]
            own_ref[y, z] = piece
            if y < 3:
                first_ref[y, z] = piece
            if y >= height - 3:
                last_ref[y - (height - 3), z] = piece


def to_segments(field):
    levels, height, lanes = field.shape
    segments = lanes // SL
    rows = levels * height
    if rows % 16 or 256 % rows:
        own = jnp.transpose(field.reshape(levels, height, segments, SL), (1, 0, 2, 3))
        return own, own[:3], own[height - 3 :]
    group = 256 // rows
    out = lambda n: (
        jax.ShapeDtypeStruct((n, levels, segments, SL), BF16),
        pl.BlockSpec((n, levels, group, SL), lambda g: (0, 0, g, 0)),
    )
    shapes, specs = zip(out(height), out(3), out(3))
    return pl.pallas_call(
        segment_kernel,
        grid=(segments // group,),
        in_specs=[pl.BlockSpec((levels, height, group * SL), lambda g: (0, 0, g))],
        out_specs=list(specs),
        out_shape=list(shapes),
        compiler_params=params(),
        cost_estimate=cost(2 * rows * lanes * 256, 8 * rows * lanes),
    )(field)


def weights_kernel(rows_ref, point_ref, vert_ref, across_ref, up_ref):
    blocks = []
    for i in range(KH):
        parts = []
        for xo in range(4):
            parts.append(point_ref[...] * rows_ref[pl.ds(i * 4 + xo, 1), :])
        blocks.append(jnp.concatenate(parts, axis=0).T.astype(BF16))
    zero = jnp.zeros((3 * HALF, HALF), BF16)
    for yi in range(KH + 1):
        for yo in range(2):
            i = yi - yo
            across_ref[yi * 3 * HALF : (yi + 1) * 3 * HALF, yo * HALF : (yo + 1) * HALF] = (
                blocks[i] if 0 <= i < KH else zero
            )
    row = lax.broadcasted_iota(jnp.int32, (KV * HALF, KV * C), 0)
    column = lax.broadcasted_iota(jnp.int32, (KV * HALF, KV * C), 1)
    spread = ((row // HALF == column // C) & (row % C == column % C)).astype(BF16)
    row = lax.broadcasted_iota(jnp.int32, (C, HALF), 0)
    column = lax.broadcasted_iota(jnp.int32, (C, HALF), 1)
    repeat = (row == column % C).astype(BF16)
    row = lax.broadcasted_iota(jnp.int32, (KV * HALF, HALF), 0)
    column = lax.broadcasted_iota(jnp.int32, (KV * HALF, HALF), 1)
    same = (row % HALF) // C == column // C
    zero = jnp.zeros((HALF, HALF), BF16)
    for layer in range(vert_ref.shape[0]):
        tall = lax.dot_general(spread, vert_ref[layer], NT, preferred_element_type=F32).astype(BF16)
        wide = jnp.dot(tall, repeat, preferred_element_type=F32)
        wide = jnp.where(same, wide, 0.0).astype(BF16)
        for zi in range(KV + 1):
            for zo in range(2):
                k = zi - zo
                up_ref[layer, zi * HALF : (zi + 1) * HALF, zo * HALF : (zo + 1) * HALF] = (
                    wide[k * HALF : (k + 1) * HALF] if 0 <= k < KV else zero
                )


def make_weights(depth_kernel, point_weight, vert_weight):
    flat = depth_kernel.reshape(KH, KH * C)
    wide = 3 * HALF
    rows = jnp.stack(
        [
            jnp.pad(flat, ((0, 0), ((xo + 1) * C, wide - KH * C - (xo + 1) * C)))
            for xo in range(4)
        ],
        axis=1,
    ).reshape(KH * 4, wide)
    point = jnp.tile(point_weight.T.astype(F32), (1, wide // C))
    vert = jnp.transpose(vert_weight, (0, 2, 1))
    layers = vert.shape[0]
    return pl.pallas_call(
        weights_kernel,
        out_shape=[
            jax.ShapeDtypeStruct(((KH + 1) * wide, SL), BF16),
            jax.ShapeDtypeStruct((layers, (KV + 1) * HALF, SL), BF16),
        ],
        compiler_params=params(),
        cost_estimate=cost(10**9, 6 * 10**6),
    )(rows, point, vert)


def horizontal_kernel(own_ref, low_ref, high_ref, weight_ref, bias_ref, out_ref):
    height = own_ref.shape[0]
    segments = own_ref.shape[2]
    row = lax.broadcasted_iota(jnp.int32, (segments, HALF), 0)
    lines = [low_ref[y, 0] for y in range(3)]
    lines += [own_ref[y, 0] for y in range(height)]
    lines += [high_ref[y, 0] for y in range(3)]
    left, right = [], []
    for line in lines:
        a0, a1 = line[:, :HALF], line[:, HALF:]
        before = jnp.where(row == 0, 0.0, pltpu.roll(a1.astype(F32), 1, 0)).astype(BF16)
        after = jnp.where(
            row == segments - 1, 0.0, pltpu.roll(a0.astype(F32), segments - 1, 0)
        ).astype(BF16)
        left.append([before, a0, a1])
        right.append([a0, a1, after])
    stacked = []
    for yp in range(height // 2):
        for side in (left, right):
            stacked.append(
                jnp.concatenate(
                    [tile for y in range(2 * yp, 2 * yp + KH + 1) for tile in side[y]], axis=1
                )
            )
    total = jnp.dot(
        jnp.concatenate(stacked, axis=0), weight_ref[...], preferred_element_type=F32
    )
    tiles, _, _, per, _ = out_ref.shape
    for yp in range(height // 2):
        for h in range(2):
            start = (yp * 2 + h) * segments
            for yo in range(2):
                y = 2 * yp + yo
                part = total[start : start + segments, yo * HALF : (yo + 1) * HALF]
                center = lines[y + 3][:, h * HALF : (h + 1) * HALF].astype(F32)
                value = (center + gelu(part + bias_ref[...])).astype(BF16)
                out_ref[:, 0, y, :, h * HALF : (h + 1) * HALF] = value.reshape(tiles, per, HALF)


def horizontal(own, low, high, weight, bias, tiles):
    height, levels, segments, _ = own.shape
    direct = (segments // tiles) % 16 == 0
    parts = tiles if direct else 1
    per = segments // parts
    line = lambda n: pl.BlockSpec((n, 1, segments, SL), lambda z: (0, z, 0, 0))
    out = pl.pallas_call(
        horizontal_kernel,
        grid=(levels,),
        in_specs=[line(height), line(3), line(3), whole(weight.shape), whole(bias.shape)],
        out_specs=pl.BlockSpec((parts, 1, height, per, SL), lambda z: (0, z, 0, 0, 0)),
        out_shape=jax.ShapeDtypeStruct((parts, levels, height, per, SL), BF16),
        compiler_params=params(),
        cost_estimate=cost(
            2 * levels * height * segments * weight.shape[0] * SL // 2, 4 * 10**6
        ),
    )(own, low, high, weight, bias)
    if not direct:
        out = out.reshape(levels, height, tiles, segments // tiles, SL)
        out = jnp.transpose(out, (2, 0, 1, 3, 4))
    return out


def bucket_kernel(rows_ref, owner_ref, cells_ref, out_ref):
    count = rows_ref.shape[1]
    tiles = out_ref.shape[0]
    cap = 2 * count // tiles
    owner, cells = owner_ref[...], cells_ref[...]
    row = lax.broadcasted_iota(jnp.int32, (count, count), 0)
    column = lax.broadcasted_iota(jnp.int32, (count, count), 1)
    before = (row < column).astype(BF16)
    named = (lax.broadcasted_iota(jnp.int32, (tiles, count), 0) == owner).astype(F32)
    rank = jnp.dot(named.astype(BF16), before, preferred_element_type=F32)
    rank = jnp.sum(rank * named, axis=0, keepdims=True).astype(jnp.int32)
    slot = owner * cap + rank
    chosen = lax.broadcasted_iota(jnp.int32, (tiles * cap, count), 0) == slot
    coarse = (cells // HALF).astype(F32)
    fine = (cells % HALF).astype(F32)
    index = lax.broadcasted_iota(jnp.int32, (PACK - C, count), 0)
    places = jnp.where(index == 0, coarse, jnp.where(index == 1, fine, 0.0)).astype(BF16)
    payload = jnp.concatenate([rows_ref[...], places], axis=0)
    out = lax.dot_general(
        payload, chosen.astype(BF16), NT, preferred_element_type=F32
    ).astype(BF16)
    if cap % HALF == 0:
        for t in range(tiles):
            out_ref[t] = out[:, t * cap : (t + 1) * cap]
    else:
        out_ref[...] = jnp.swapaxes(out.reshape(PACK, tiles, cap), 0, 1)


def bucket(exhaust, owner, cells, tiles):
    count = exhaust.shape[0]
    cap = 2 * count // tiles
    return pl.pallas_call(
        bucket_kernel,
        out_shape=jax.ShapeDtypeStruct((tiles, PACK, cap), BF16),
        compiler_params=params(),
        cost_estimate=cost(10**8, 10**6),
    )(exhaust.T, owner.reshape(1, count), cells.reshape(1, count))


def source_kernel(got_ref, out_ref):
    step = out_ref.shape[0]
    slots = got_ref.shape[1]
    got = got_ref[...]
    cells = (got[C : C + 1].astype(F32) * HALF + got[C + 1 : C + 2].astype(F32)).astype(jnp.int32)
    place, within = cells // SEG, cells % SEG
    rows = got[:C]
    lane = lax.broadcasted_iota(jnp.int32, (SL, slots), 0) // C
    spread = jnp.where(lane == within, jnp.concatenate([rows] * SEG, axis=0).astype(F32), 0.0)
    row = lax.broadcasted_iota(jnp.int32, (step, slots), 0) + pl.program_id(0) * step
    chosen = (row == place).astype(BF16)
    out_ref[...] = lax.dot_general(chosen, spread.astype(BF16), NT, preferred_element_type=F32)


def make_source(got, places):
    slots = got.shape[1]
    step = min(512, places)
    return pl.pallas_call(
        source_kernel,
        grid=(places // step,),
        in_specs=[whole(got.shape)],
        out_specs=pl.BlockSpec((step, SL), lambda g: (g, 0)),
        out_shape=jax.ShapeDtypeStruct((places, SL), F32),
        compiler_params=params(),
        cost_estimate=cost(2 * places * slots * SL, 3 * 10**6),
    )(got)


def vertical_kernel(height, field_ref, source_ref, weight_ref, bias_ref, out_ref, held):
    levels, rows, _ = field_ref.shape
    layers = weight_ref.shape[0]
    step = pl.program_id(0)
    zero = jnp.zeros((rows, HALF), BF16)
    tiles = [[field_ref[z, :, h * HALF : (h + 1) * HALF] for h in range(2)] for z in range(levels)]
    for layer in range(layers):
        taps = []
        for k in range(KV + 1):
            column = []
            for zp in range(levels // 2):
                z = 2 * zp + k - KV // 2
                for h in range(2):
                    column.append(tiles[z][h] if 0 <= z < levels else zero)
            taps.append(jnp.concatenate(column, axis=0))
        total = jnp.dot(
            jnp.concatenate(taps, axis=1), weight_ref[layer], preferred_element_type=F32
        )
        following = []
        for z in range(levels):
            following.append([])
            for h in range(2):
                start = ((z // 2) * 2 + h) * rows
                lane = (z % 2) * HALF
                part = total[start : start + rows, lane : lane + HALF]
                value = tiles[z][h].astype(F32) + gelu(part + bias_ref[pl.ds(layer, 1), :])
                if layer == layers - 1:
                    value = value + source_ref[z, :, h * HALF : (h + 1) * HALF]
                following[z].append(value.astype(BF16))
        tiles = following
    for z in range(levels):
        for h in range(2):
            held[step, z, :, h * HALF : (h + 1) * HALF] = tiles[z][h]

    @pl.when(step == pl.num_programs(0) - 1)
    def _():
        steps = held.shape[0]
        across = steps * rows // height
        group = 256 // (steps * rows)
        swap = swap_matrix(group * height, across)
        for g in range(levels // group):
            pieces = [held[n, g * group + z] for z in range(group) for n in range(steps)]
            turned = jnp.dot(
                swap, jnp.concatenate(pieces, axis=0), preferred_element_type=F32
            ).astype(BF16)
            size = group * height
            for s in range(across):
                out_ref[g * group : (g + 1) * group, :, s * SL : (s + 1) * SL] = turned[
                    s * size : (s + 1) * size
                ].reshape(group, height, SL)


def vertical(field, source, weight, bias, height):
    levels, rows, _ = field.shape
    size = 16
    steps = rows // size
    lanes = rows // height * SL
    return pl.pallas_call(
        functools.partial(vertical_kernel, height),
        grid=(steps,),
        in_specs=[
            pl.BlockSpec((levels, size, SL), lambda g: (0, g, 0)),
            pl.BlockSpec((levels, size, SL), lambda g: (0, g, 0)),
            whole(weight.shape),
            whole(bias.shape),
        ],
        out_specs=whole((levels, height, lanes)),
        out_shape=jax.ShapeDtypeStruct((levels, height, lanes), BF16),
        scratch_shapes=[pltpu.VMEM((steps, levels, size, SL), BF16)],
        compiler_params=params(),
        cost_estimate=cost(4 * levels * rows * weight.shape[1] * SL, 6 * 10**6),
    )(field, source, weight, bias)


def body(
    field, depth_kernel, point_weight, point_bias, vert_weight, vert_bias, exhaust, owner, cells
):
    columns, bands = lax.axis_size("cols"), lax.axis_size("rows")
    forward = [(i, i + 1) for i in range(bands - 1)]
    backward = [(target, source) for source, target in forward]
    height = field.shape[1]
    own, first, last = to_segments(field)
    low = lax.ppermute(last, "rows", forward)
    high = lax.ppermute(first, "rows", backward)
    sent = bucket(exhaust, owner, cells, columns)
    got = lax.all_to_all(sent, "cols", split_axis=0, concat_axis=0, tiled=True)
    got = jnp.transpose(got, (1, 0, 2)).reshape(PACK, -1)
    across, up = make_weights(depth_kernel, point_weight, vert_weight)
    mixed = horizontal(
        own, low, high, across, jnp.tile(point_bias, 4).reshape(1, HALF), columns
    )
    tiles, levels, _, per, _ = mixed.shape
    mixed = mixed.reshape(tiles, levels, height * per, SL)
    taken = lax.all_to_all(mixed, "cols", split_axis=0, concat_axis=0, tiled=True)
    taken = taken.reshape(tiles * levels, height * per, SL)
    source = make_source(got, taken.shape[0] * taken.shape[1]).reshape(taken.shape)
    return vertical(taken, source, up, jnp.tile(vert_bias, (1, 4)), height)


def solution(mesh):
    placed = (
        P("cols", "rows", None),
        P(),
        P(),
        P(),
        P(),
        P(),
        P(("rows", "cols"), None),
        P(("rows", "cols"), None),
        P(("rows", "cols")),
    )
    return jax.shard_map(
        body, mesh=mesh, in_specs=placed, out_specs=P(None, "rows", "cols"), check_vma=False
    )
```

time: 527 us -> 77 us (0.15)
  the two profiles are of different devices: /device:TPU:2 before, /device:TPU:0 now
where the time goes in v1:
time: 77 us; the launch traced here: 76.3 us
  Pallas kernels  32.2 us (42%)
  waiting for transfers between devices  21.8 us (28%)
  starting transfers between devices  16.4 us (21%)
  local copies, waits for them, and re-layouts  5.75 us (7%)
    all_to_all x1, waiting for transfers between devices, body(): lax.all_to_all(mixed, 'cols', split_axis=0, concat_axis=0, tiled=True)  21.8 us
    pallas_call x1, Pallas kernels, vertical(): pl.pallas_call(functools.partial(vertical_kernel, height), grid=(steps,),...  9.67 us
    pallas_call x1, Pallas kernels, horizontal(): pl.pallas_call(horizontal_kernel, grid=(levels,), in_specs=[line(height),...  6.95 us
    all_to_all x1, starting transfers between devices, body(): got = lax.all_to_all(sent, 'cols', split_axis=0, concat_axis=0, tiled=True)  6.67 us
    pallas_call x1, Pallas kernels, to_segments(): pl.pallas_call(segment_kernel, grid=(segments // group,), in_specs=[pl.Bl...  6.19 us
    all_to_all x1, starting transfers between devices, body(): lax.all_to_all(mixed, 'cols', split_axis=0, concat_axis=0, tiled=True)  6.01 us
    pallas_call x1, Pallas kernels, make_source(): pl.pallas_call(source_kernel, grid=(places // step,), in_specs=[whole(got...  4 us
    pallas_call x1, Pallas kernels, make_weights(): pl.pallas_call(weights_kernel, out_shape=[jax.ShapeDtypeStruct(((KH + 1)...  3.33 us
  transfers between devices with their start and end apart: 4, of which 1 were waited for; matrix products, arithmetic and copies ran while one was open for 5% of the time, Pallas kernels for 21%

profile of v1, /device:TPU:0, one launch (start us, length us, event | category | flops | bytes accessed | tf_op | source)
XLA Modules:
  0.0 76.3 jit_solution(4724993898460595534)
XLA Ops:
  0.0 0.0 copy-start.1
  0.0 0.0 copy-start.2
  0.0 6.2 %shard_map.91 = (bf16[4,4,128,256]{3,2,1,0:T(8,128)(2,1)}, bf16[3,4,128,256]{3,2,1,0:T(8,128)(2,1)}, bf16[3,4,128,256]{3,2,1,0:T(8,128)(2,1)}) custom-call(bf16[4,4,32768]{2,1,0:T(4,128)(2,1)} %field_ref.1), custom_call_target="tpu_custom_call" | custom-call | flops 268435456 | bytes 4194304 | tf_op jit(solution)/shard_map/pallas_call | solution.py:81
  6.2 2.4 %collective-permute-start = (bf16[3,4,128,256]{3,2,1,0:T(8,128)(2,1)}, bf16[3,4,128,256]{3,2,1,0:T(8,128)(2,1)S(1)}, u32[]{:S(2)}, u32[]{:S(2)}) collective-permute-start(bf16[3,4,128,256]{3,2,1,0:T(8,128)(2,1)} %get-tuple-element.11), channel_id=1, source_target_pairs={{0,8},{8,16},{16,24},{1,9},{9,17},{17,25},{2,10},{10,18},{18,26},{... | collective-permute-start | bytes 2359304 | tf_op jit(solution)/shard_map/ppermute | solution.py:363
  8.6 1.3 %collective-permute-start.1 = (bf16[3,4,128,256]{3,2,1,0:T(8,128)(2,1)}, bf16[3,4,128,256]{3,2,1,0:T(8,128)(2,1)S(1)}, u32[]{:S(2)}, u32[]{:S(2)}) collective-permute-start(bf16[3,4,128,256]{3,2,1,0:T(8,128)(2,1)} %get-tuple-element.12), channel_id=1, source_target_pairs={{8,0},{16,8},{24,16},{9,1},{17,9},{25,17},{10,2},{18,10},{26,18},{... | collective-permute-start | bytes 2359304 | tf_op jit(solution)/shard_map/ppermute | solution.py:364
  9.9 2.1 %shard_map.94 = bf16[8,48,128]{2,1,0:T(8,128)(2,1)} custom-call(bf16[32,512]{1,0:T(8,128)(2,1)} %bitcast.24, s32[1,512]{1,0:T(1,128)} %bitcast.25, s32[1,512]{1,0:T(1,128)} %bitcast.26), custom_call_target="tpu_custom_call" | custom-call | flops 100000000 | bytes 1000000 | tf_op jit(solution)/shard_map/pallas_call | solution.py:245
  12.0 6.7 %all-to-all-start.1 = ((bf16[8,48,128]{2,1,0:T(8,128)(2,1)}), bf16[8,48,128]{2,1,0:T(8,128)(2,1)S(1)}, u32[]{:S(2)}, u32[]{:S(2)}) async-start(bf16[8,48,128]{2,1,0:T(8,128)(2,1)} %shard_map.94), calls=%async_computation.1 | async-start | bytes 196608 | tf_op jit(solution)/shard_map/all_to_all | solution.py:366
  18.7 0.0 copy-done.1
  18.7 0.1 reshape.33
  18.7 0.1 pad_bitcast_fusion.2
  18.9 0.6 reshape.34.rows_ref
  19.6 0.0 copy-done.2
  19.6 0.1 copy.18
  19.7 0.7 tile.11.point_ref
  20.4 0.0 copy-start.4
  20.4 3.3 %shard_map.92 = (bf16[3072,256]{1,0:T(8,128)(2,1)}, bf16[2,1280,256]{2,1,0:T(8,128)(2,1)}) custom-call(f32[28,384]{1,0:T(8,128)} %reshape.34.rows_ref, f32[32,384]{1,0:T(8,128)} %tile.11.point_ref, bf16[2,32,288]{2,1,0:T(8,128)(2,1)} %bitcast.23), custom_call_target="tpu_custom_call" | custom-call | flops 1000000000 | bytes 6000000 | tf_op jit(solution)/shard_map/pallas_call | solution.py:141
  23.7 0.0 copy-done.4
  23.8 0.6 reshape_tile.3.bias_ref
  24.4 0.0 collective-permute-done.low_ref
  24.4 0.0 copy-start.5
  24.4 0.0 collective-permute-done.1.high_ref
  24.4 0.0 copy-start.6
  24.4 0.9 %copy-done.5 = bf16[3,4,128,256]{3,2,1,0:T(8,128)(2,1)} copy-done((bf16[3,4,128,256]{3,2,1,0:T(8,128)(2,1)}, bf16[3,4,128,256]{3,2,1,0:T(8,128)(2,1)S(1)}, u32[]{:S(2)}) %copy-start.5) | copy-done | bytes 786456
  25.3 0.3 copy-done.6
  25.6 6.9 %shard_map.93 = bf16[8,4,4,16,256]{4,3,2,1,0:T(8,128)(2,1)} custom-call(bf16[4,4,128,256]{3,2,1,0:T(8,128)(2,1)} %get-tuple-element.10.own_ref, bf16[3,4,128,256]{3,2,1,0:T(8,128)(2,1)} %copy-done.5, bf16[3,4,128,256]{3,2,1,0:T(8,128)(2,1)} %copy-done.6, bf16[3072,256]{1,0:T(8,128)(2,1)} %get-tuple-element.13.weight_ref, f32[1,128]{1,0:T(1,128)} %reshape_tile.3.bias_ref), custom_call_target="tpu_custom_call" | custom-call | flops 1610612736 | bytes 4000000 | tf_op jit(solution)/shard_map/pallas_call | solution.py:197
  32.5 0.0 copy-start.3
  32.5 0.0 all-to-all-done.1
  32.5 6.0 %all-to-all-start = ((bf16[8,4,64,256]{3,2,1,0:T(8,128)(2,1)}), bf16[8,4,64,256]{3,2,1,0:T(8,128)(2,1)S(1)}, u32[]{:S(2)}, u32[]{:S(2)}) async-start(bf16[8,4,64,256]{3,2,1,0:T(8,128)(2,1)} %bitcast.21), calls=%async_computation | async-start | bytes 2097152 | tf_op jit(solution)/shard_map/all_to_all | solution.py:374
  38.5 0.0 copy-done.3
  38.5 0.7 tile.28.bias_ref
  39.2 0.6 copy_bitcast_fusion.got_ref
  39.9 4.0 %shard_map.95 = f32[2048,256]{1,0:T(8,128)} custom-call(bf16[48,1024]{1,0:T(8,128)(2,1)} %copy_bitcast_fusion.got_ref), custom_call_target="tpu_custom_call" | custom-call | flops 1073741824 | bytes 3000000 | tf_op jit(solution)/shard_map/pallas_call | solution.py:270
  43.9 21.8 %all-to-all-done = bf16[8,4,64,256]{3,2,1,0:T(8,128)(2,1)S(1)} async-done(((bf16[8,4,64,256]{3,2,1,0:T(8,128)(2,1)}), bf16[8,4,64,256]{3,2,1,0:T(8,128)(2,1)S(1)}, u32[]{:S(2)}, u32[]{:S(2)}) %all-to-all-start) | async-done | bytes 1048608 | tf_op jit(solution)/shard_map/all_to_all | solution.py:374
  65.7 0.0 copy-start
  65.7 1.0 %copy-done = bf16[8,4,64,256]{3,2,1,0:T(8,128)(2,1)} copy-done((bf16[8,4,64,256]{3,2,1,0:T(8,128)(2,1)}, bf16[8,4,64,256]{3,2,1,0:T(8,128)(2,1)S(1)}, u32[]{:S(2)}) %copy-start) | copy-done | bytes 1048600
  66.6 9.7 %shard_map.96 = bf16[32,4,4096]{2,1,0:T(4,128)(2,1)} custom-call(bf16[32,64,256]{2,1,0:T(8,128)(2,1)} %bitcast.22, f32[32,64,256]{2,1,0:T(8,128)} %bitcast.27, bf16[2,1280,256]{2,1,0:T(8,128)(2,1)} %get-tuple-element.14.weight_ref, f32[2,128]{1,0:T(2,128)} %tile.28.bias_ref), custom_call_target="tpu_custom_call" | custom-call | flops 2684354560 | bytes 6000000 | tf_op jit(solution)/shard_map/pallas_call | solution.py:338
  (9 shorter events, 0.1 us)
Async XLA Ops:
  0.0 18.7 %copy-start.1 = (f32[7,7,32]{2,1,0:T(8,128)S(1)}, f32[7,7,32]{2,1,0:T(8,128)}, u32[]{:S(2)}) copy-start(f32[7,7,32]{2,1,0:T(8,128)} %param.10) | copy-start | bytes 18820
  0.0 19.6 %copy-start.2 = (bf16[32,32]{1,0:T(8,128)(2,1)S(1)}, bf16[32,32]{1,0:T(8,128)(2,1)}, u32[]{:S(2)}) copy-start(bf16[32,32]{1,0:T(8,128)(2,1)} %param.11) | copy-start | bytes 6148
  6.2 18.2 %collective-permute-start = (bf16[3,4,128,256]{3,2,1,0:T(8,128)(2,1)}, bf16[3,4,128,256]{3,2,1,0:T(8,128)(2,1)S(1)}, u32[]{:S(2)}, u32[]{:S(2)}) collective-permute-start(bf16[3,4,128,256]{3,2,1,0:T(8,128)(2,1)} %get-tuple-element.11), channel_id=1, source_target_pairs={{0,8},{8,16},{16,24},{1,9},{9,17},{17,25},{2,10},{10,18},{18,26},{... | collective-permute-start | bytes 2359304 | tf_op jit(solution)/shard_map/ppermute | solution.py:363
  8.6 15.8 %collective-permute-start.1 = (bf16[3,4,128,256]{3,2,1,0:T(8,128)(2,1)}, bf16[3,4,128,256]{3,2,1,0:T(8,128)(2,1)S(1)}, u32[]{:S(2)}, u32[]{:S(2)}) collective-permute-start(bf16[3,4,128,256]{3,2,1,0:T(8,128)(2,1)} %get-tuple-element.12), channel_id=1, source_target_pairs={{8,0},{16,8},{24,16},{9,1},{17,9},{25,17},{10,2},{18,10},{26,18},{... | collective-permute-start | bytes 2359304 | tf_op jit(solution)/shard_map/ppermute | solution.py:364
  12.0 20.5 %all-to-all-start.1 = ((bf16[8,48,128]{2,1,0:T(8,128)(2,1)}), bf16[8,48,128]{2,1,0:T(8,128)(2,1)S(1)}, u32[]{:S(2)}, u32[]{:S(2)}) async-start(bf16[8,48,128]{2,1,0:T(8,128)(2,1)} %shard_map.94), calls=%async_computation.1 | async-start | bytes 196608 | tf_op jit(solution)/shard_map/all_to_all | solution.py:366
  20.4 3.3 %copy-start.4 = (f32[32]{0:T(128)S(1)}, f32[32]{0:T(128)}, u32[]{:S(2)}) copy-start(f32[32]{0:T(128)} %param.12) | copy-start | bytes 388
  24.4 0.9 %copy-start.5 = (bf16[3,4,128,256]{3,2,1,0:T(8,128)(2,1)}, bf16[3,4,128,256]{3,2,1,0:T(8,128)(2,1)S(1)}, u32[]{:S(2)}) copy-start(bf16[3,4,128,256]{3,2,1,0:T(8,128)(2,1)S(1)} %collective-permute-done.low_ref) | copy-start | bytes 2359300
  24.4 1.1 %copy-start.6 = (bf16[3,4,128,256]{3,2,1,0:T(8,128)(2,1)}, bf16[3,4,128,256]{3,2,1,0:T(8,128)(2,1)S(1)}, u32[]{:S(2)}) copy-start(bf16[3,4,128,256]{3,2,1,0:T(8,128)(2,1)S(1)} %collective-permute-done.1.high_ref) | copy-start | bytes 2359300
  32.5 6.0 %copy-start.3 = (f32[2,32]{1,0:T(2,128)S(1)}, f32[2,32]{1,0:T(2,128)}, u32[]{:S(2)}) copy-start(f32[2,32]{1,0:T(2,128)} %param.14) | copy-start | bytes 772
  32.5 33.1 %all-to-all-start = ((bf16[8,4,64,256]{3,2,1,0:T(8,128)(2,1)}), bf16[8,4,64,256]{3,2,1,0:T(8,128)(2,1)S(1)}, u32[]{:S(2)}, u32[]{:S(2)}) async-start(bf16[8,4,64,256]{3,2,1,0:T(8,128)(2,1)} %bitcast.21), calls=%async_computation | async-start | bytes 2097152 | tf_op jit(solution)/shard_map/all_to_all | solution.py:374
  65.7 1.0 %copy-start = (bf16[8,4,64,256]{3,2,1,0:T(8,128)(2,1)}, bf16[8,4,64,256]{3,2,1,0:T(8,128)(2,1)S(1)}, u32[]{:S(2)}) copy-start(bf16[8,4,64,256]{3,2,1,0:T(8,128)(2,1)S(1)} %all-to-all-done) | copy-start | bytes 3145732

commit v2 on v1

v2 whole, which is shorter than its diff:
```python
import functools

import jax
import jax.numpy as jnp
from jax import lax
from jax.experimental import pallas as pl
from jax.experimental.pallas import tpu as pltpu
from jax.sharding import PartitionSpec as P

C = 32
KH = 7
KV = 9
SEG = 8
SL = SEG * C
HALF = SL // 2
PACK = 48
VMEM = 24 * 1024 * 1024
NT = (((1,), (1,)), ((), ()))
F32 = jnp.float32
BF16 = jnp.bfloat16


def params():
    return pltpu.CompilerParams(vmem_limit_bytes=VMEM)


def cost(flops, moved):
    return pl.CostEstimate(flops=flops, bytes_accessed=moved, transcendentals=0)


def whole(shape):
    return pl.BlockSpec(shape, lambda *_: (0,) * len(shape))


def gelu(x):
    return 0.5 * x * (1.0 + jnp.tanh(0.7978845608028654 * (x + 0.044715 * (x * x * x))))


def swap_matrix(outer, inner):
    size = outer * inner
    row = lax.broadcasted_iota(jnp.int32, (size, size), 0)
    column = lax.broadcasted_iota(jnp.int32, (size, size), 1)
    return (column == (row % outer) * inner + row // outer).astype(BF16)


def segment_kernel(field_ref, own_ref, first_ref, last_ref):
    levels, height, lanes = field_ref.shape
    rows = levels * height
    group = 256 // rows
    swap = swap_matrix(group, rows)
    for g in range(lanes // (group * SL)):
        at = [(g * group + s) * SL for s in range(group)]
        pieces = [field_ref[:, :, n : n + SL].reshape(rows, SL) for n in at]
        got = jnp.dot(
            swap, jnp.concatenate(pieces, axis=0), preferred_element_type=F32
        ).astype(BF16)
        for z in range(levels):
            for y in range(height):
                start = (z * height + y) * group
                piece = got[start : start + group]
                place = slice(g * group, (g + 1) * group)
                own_ref[y, z, place] = piece
                if y < 3:
                    first_ref[y, z, place] = piece
                if y >= height - 3:
                    last_ref[y - (height - 3), z, place] = piece


def to_segments(field):
    levels, height, lanes = field.shape
    segments = lanes // SL
    rows = levels * height
    if rows % 16 or 256 % rows:
        own = jnp.transpose(field.reshape(levels, height, segments, SL), (1, 0, 2, 3))
        return own, own[:3], own[height - 3 :]
    steps = 2
    part = segments // steps
    out = lambda n: (
        jax.ShapeDtypeStruct((n, levels, segments, SL), BF16),
        pl.BlockSpec((n, levels, part, SL), lambda g: (0, 0, g, 0)),
    )
    shapes, specs = zip(out(height), out(3), out(3))
    return pl.pallas_call(
        segment_kernel,
        grid=(steps,),
        in_specs=[pl.BlockSpec((levels, height, part * SL), lambda g: (0, 0, g))],
        out_specs=list(specs),
        out_shape=list(shapes),
        compiler_params=params(),
        cost_estimate=cost(2 * rows * lanes * 256, 8 * rows * lanes),
    )(field)


def across_kernel(depth_ref, point_ref, out_ref):
    point = jnp.concatenate([point_ref[...].astype(F32)] * (HALF // C), axis=1)
    lane = lax.broadcasted_iota(jnp.int32, (C, HALF), 1) // C
    wide = 3 * HALF
    out_ref[...] = jnp.zeros_like(out_ref)
    for i in range(KH):
        columns = jnp.transpose(depth_ref[i])
        scaled = [point * columns[:, j : j + 1] for j in range(KH)]
        for xt in range(wide // C):
            block = jnp.zeros((C, HALF), F32)
            for xo in range(HALF // C):
                j = xt - 1 - xo
                if 0 <= j < KH:
                    block = jnp.where(lane == xo, scaled[j], block)
            block = block.astype(BF16)
            for yo in range(2):
                row = (i + yo) * wide + xt * C
                out_ref[row : row + C, yo * HALF : (yo + 1) * HALF] = block


def across_weights(depth_kernel, point_weight):
    return pl.pallas_call(
        across_kernel,
        out_shape=jax.ShapeDtypeStruct(((KH + 1) * 3 * HALF, SL), BF16),
        compiler_params=params(),
        cost_estimate=cost(1000, 1000),
    )(depth_kernel, point_weight)


def up_kernel(vert_ref, out_ref):
    row = lax.broadcasted_iota(jnp.int32, (KV * HALF, KV * C), 0)
    column = lax.broadcasted_iota(jnp.int32, (KV * HALF, KV * C), 1)
    spread = ((row // HALF == column // C) & (row % C == column % C)).astype(BF16)
    row = lax.broadcasted_iota(jnp.int32, (C, HALF), 0)
    column = lax.broadcasted_iota(jnp.int32, (C, HALF), 1)
    repeat = (row == column % C).astype(BF16)
    row = lax.broadcasted_iota(jnp.int32, (KV * HALF, HALF), 0)
    column = lax.broadcasted_iota(jnp.int32, (KV * HALF, HALF), 1)
    same = (row % HALF) // C == column // C
    zero = jnp.zeros((HALF, HALF), BF16)
    for layer in range(vert_ref.shape[0]):
        tall = lax.dot_general(spread, vert_ref[layer], NT, preferred_element_type=F32).astype(BF16)
        wide = jnp.dot(tall, repeat, preferred_element_type=F32)
        wide = jnp.where(same, wide, 0.0).astype(BF16)
        for zi in range(KV + 1):
            for zo in range(2):
                k = zi - zo
                out_ref[layer, zi * HALF : (zi + 1) * HALF, zo * HALF : (zo + 1) * HALF] = (
                    wide[k * HALF : (k + 1) * HALF] if 0 <= k < KV else zero
                )


def up_weights(vert_weight):
    vert = jnp.transpose(vert_weight, (0, 2, 1))
    return pl.pallas_call(
        up_kernel,
        out_shape=jax.ShapeDtypeStruct((vert.shape[0], (KV + 1) * HALF, SL), BF16),
        compiler_params=params(),
        cost_estimate=cost(1000, 1000),
    )(vert)


def bias_row(row):
    return jnp.concatenate([row] * (HALF // C), axis=1)


def horizontal_kernel(own_ref, low_ref, high_ref, weight_ref, bias_ref, out_ref):
    height = own_ref.shape[0]
    segments = own_ref.shape[2]
    row = lax.broadcasted_iota(jnp.int32, (segments, HALF), 0)
    lines = [low_ref[y, 0] for y in range(3)]
    lines += [own_ref[y, 0] for y in range(height)]
    lines += [high_ref[y, 0] for y in range(3)]
    left, right = [], []
    for line in lines:
        a0, a1 = line[:, :HALF], line[:, HALF:]
        before = jnp.where(row == 0, 0.0, pltpu.roll(a1.astype(F32), 1, 0)).astype(BF16)
        after = jnp.where(
            row == segments - 1, 0.0, pltpu.roll(a0.astype(F32), segments - 1, 0)
        ).astype(BF16)
        left.append([before, a0, a1])
        right.append([a0, a1, after])
    stacked = []
    for yp in range(height // 2):
        for side in (left, right):
            stacked.append(
                jnp.concatenate(
                    [tile for y in range(2 * yp, 2 * yp + KH + 1) for tile in side[y]], axis=1
                )
            )
    total = jnp.dot(
        jnp.concatenate(stacked, axis=0), weight_ref[...], preferred_element_type=F32
    )
    bias = bias_row(bias_ref[...])
    tiles, _, _, per, _ = out_ref.shape
    for yp in range(height // 2):
        for h in range(2):
            start = (yp * 2 + h) * segments
            for yo in range(2):
                y = 2 * yp + yo
                part = total[start : start + segments, yo * HALF : (yo + 1) * HALF]
                center = lines[y + 3][:, h * HALF : (h + 1) * HALF].astype(F32)
                value = (center + gelu(part + bias)).astype(BF16)
                out_ref[:, 0, y, :, h * HALF : (h + 1) * HALF] = value.reshape(tiles, per, HALF)


def horizontal(own, low, high, weight, bias, tiles):
    height, levels, segments, _ = own.shape
    direct = (segments // tiles) % 16 == 0
    parts = tiles if direct else 1
    per = segments // parts
    line = lambda n: pl.BlockSpec((n, 1, segments, SL), lambda z: (0, z, 0, 0))
    out = pl.pallas_call(
        horizontal_kernel,
        grid=(levels,),
        in_specs=[line(height), line(3), line(3), whole(weight.shape), whole(bias.shape)],
        out_specs=pl.BlockSpec((parts, 1, height, per, SL), lambda z: (0, z, 0, 0, 0)),
        out_shape=jax.ShapeDtypeStruct((parts, levels, height, per, SL), BF16),
        compiler_params=params(),
        cost_estimate=cost(
            2 * levels * height * segments * weight.shape[0] * SL // 2, 4 * 10**6
        ),
    )(own, low, high, weight, bias)
    if not direct:
        out = out.reshape(levels, height, tiles, segments // tiles, SL)
        out = jnp.transpose(out, (2, 0, 1, 3, 4))
    return out


def half_kernel(tiles, place_ref, own_ref, low_ref, high_ref, weight_ref, bias_ref, *rest):
    extra_refs, out_refs, done = rest[: -tiles - 1], rest[-tiles - 1 : -1], rest[-1]
    height, levels, segments, _ = own_ref.shape
    size = segments // 2
    start = pl.multiple_of(place_ref[0], size)
    per = size // tiles
    ahead = pl.multiple_of(jnp.maximum(start - 16, 0), 16)
    behind = pl.multiple_of(jnp.minimum(start + size, segments - 16), 16)
    has_ahead = jnp.where(start > 0, 1.0, 0.0)
    has_behind = jnp.where(start + size < segments, 1.0, 0.0)
    bias = bias_row(bias_ref[...])
    refs = [(low_ref, y) for y in range(3)]
    refs += [(own_ref, y) for y in range(height)]
    refs += [(high_ref, y) for y in range(3)]
    stacked, centers = [], []
    for z in range(levels):
        left, right = [], []
        centers.append([])
        for ref, y in refs:
            line = ref[y, z, pl.ds(start, size)]
            a0, a1 = line[:, :HALF], line[:, HALF:]
            edge = ref[y, z, pl.ds(ahead, 16), HALF:].astype(F32) * has_ahead
            before = jnp.concatenate([edge, a1.astype(F32)], axis=0)
            before = pltpu.roll(before, 1, 0)[16:].astype(BF16)
            edge = ref[y, z, pl.ds(behind, 16), :HALF].astype(F32) * has_behind
            after = jnp.concatenate([a0.astype(F32), edge], axis=0)
            after = pltpu.roll(after, size + 15, 0)[:size].astype(BF16)
            left.append([before, a0, a1])
            right.append([a0, a1, after])
            centers[z].append(line)
        for yp in range(height // 2):
            for side in (left, right):
                stacked.append(
                    jnp.concatenate(
                        [tile for y in range(2 * yp, 2 * yp + KH + 1) for tile in side[y]], axis=1
                    )
                )
    total = jnp.dot(jnp.concatenate(stacked, axis=0), weight_ref[...], preferred_element_type=F32)
    for z in range(levels):
        for y in range(height):
            for h in range(2):
                row = ((z * (height // 2) + y // 2) * 2 + h) * size
                lane = (y % 2) * HALF
                part = total[row : row + size, lane : lane + HALF]
                center = centers[z][y + 3][:, h * HALF : (h + 1) * HALF].astype(F32)
                value = (center + gelu(part + bias)).astype(BF16)
                at = (z * height + y) * per
                done[:, at : at + per, h * HALF : (h + 1) * HALF] = value.reshape(tiles, per, HALF)
    rows = levels * height * per
    for slot, out_ref in enumerate(out_refs):
        tile = place_ref[1] ^ slot
        out_ref[:rows] = done[tile]
        for n, extra_ref in enumerate(extra_refs):
            out_ref[rows:, n * HALF : (n + 1) * HALF] = extra_ref[tile]


def half_horizontal(place, own, low, high, weight, bias, tiles, extra=()):
    height, levels, segments, _ = own.shape
    per = segments // (2 * tiles)
    rows = levels * height * per
    full = pl.BlockSpec(memory_space=pltpu.VMEM)
    shape = (rows + (PACK if extra else 0), SL)
    return pl.pallas_call(
        functools.partial(half_kernel, tiles),
        in_specs=[pl.BlockSpec(memory_space=pltpu.SMEM)] + [full] * (5 + len(extra)),
        out_specs=[full] * tiles,
        out_shape=[jax.ShapeDtypeStruct(shape, BF16)] * tiles,
        scratch_shapes=[pltpu.VMEM((tiles, rows, SL), BF16)],
        compiler_params=params(),
        cost_estimate=cost(1000, 1000),
    )(place, own, low, high, weight, bias, *extra)


def bucket_kernel(near_ref, rows_ref, owner_ref, cells_ref, *rest):
    out_refs, held = rest[:-1], rest[-1]
    count = rows_ref.shape[1]
    tiles, _, cap = held.shape
    owner, cells = owner_ref[...], cells_ref[...]
    row = lax.broadcasted_iota(jnp.int32, (count, count), 0)
    column = lax.broadcasted_iota(jnp.int32, (count, count), 1)
    before = (row < column).astype(BF16)
    named = (lax.broadcasted_iota(jnp.int32, (tiles, count), 0) == owner).astype(F32)
    rank = jnp.dot(named.astype(BF16), before, preferred_element_type=F32)
    rank = jnp.sum(rank * named, axis=0, keepdims=True).astype(jnp.int32)
    slot = owner * cap + rank
    chosen = lax.broadcasted_iota(jnp.int32, (tiles * cap, count), 0) == slot
    coarse = (cells // HALF).astype(F32)
    fine = (cells % HALF).astype(F32)
    index = lax.broadcasted_iota(jnp.int32, (PACK - C, count), 0)
    places = jnp.where(index == 0, coarse, jnp.where(index == 1, fine, 0.0)).astype(BF16)
    payload = jnp.concatenate([rows_ref[...], places], axis=0)
    out = lax.dot_general(
        payload, chosen.astype(BF16), NT, preferred_element_type=F32
    ).astype(BF16)
    if cap % HALF == 0:
        for t in range(tiles):
            held[t] = out[:, t * cap : (t + 1) * cap]
    else:
        held[...] = jnp.swapaxes(out.reshape(PACK, tiles, cap), 0, 1)
    size = tiles // len(out_refs)
    for n, out_ref in enumerate(out_refs):
        out_ref[...] = held[pl.ds((near_ref[0] ^ n) * size, size)]


def bucket(near, exhaust, owner, cells, tiles, parts):
    count = exhaust.shape[0]
    cap = 2 * count // tiles
    full = pl.BlockSpec(memory_space=pltpu.VMEM)
    return pl.pallas_call(
        bucket_kernel,
        in_specs=[pl.BlockSpec(memory_space=pltpu.SMEM)] + [full] * 3,
        out_specs=[full] * parts,
        out_shape=[jax.ShapeDtypeStruct((tiles // parts, PACK, cap), BF16)] * parts,
        scratch_shapes=[pltpu.VMEM((tiles, PACK, cap), BF16)],
        compiler_params=params(),
        cost_estimate=cost(1000, 1000),
    )(near, exhaust.T, owner.reshape(1, count), cells.reshape(1, count))


def source_kernel(*refs):
    got_refs, out_ref = refs[:-1], refs[-1]
    places = out_ref.shape[0]
    got = jnp.concatenate([ref[ref.shape[0] - PACK :] for ref in got_refs], axis=1)
    slots = got.shape[1]
    cells = (got[C : C + 1].astype(F32) * HALF + got[C + 1 : C + 2].astype(F32)).astype(jnp.int32)
    place, within = cells // SEG, cells % SEG
    lane = lax.broadcasted_iota(jnp.int32, (SL, slots), 0) // C
    spread = jnp.where(lane == within, jnp.concatenate([got[:C]] * SEG, axis=0).astype(F32), 0.0)
    row = lax.broadcasted_iota(jnp.int32, (places, slots), 0)
    chosen = (row == place).astype(BF16)
    out_ref[...] = lax.dot_general(chosen, spread.astype(BF16), NT, preferred_element_type=F32)


def make_source(got, places):
    full = pl.BlockSpec(memory_space=pltpu.VMEM)
    return pl.pallas_call(
        source_kernel,
        in_specs=[full] * len(got),
        out_specs=full,
        out_shape=jax.ShapeDtypeStruct((places, SL), F32),
        compiler_params=params(),
        cost_estimate=cost(1000, 1000),
    )(*got)


def vertical_kernel(height, me_ref, *refs):
    count = len(refs) - 5
    piece_refs = refs[:count]
    source_ref, weight_ref, bias_ref, out_ref, held = refs[count:]
    levels, rows, _ = held.shape
    per = levels // count
    for d, piece_ref in enumerate(piece_refs):
        for z in range(per):
            held[(me_ref[0] ^ d) * per + z] = piece_ref[z * rows : (z + 1) * rows]
    bias = bias_row(bias_ref[...])
    layers = weight_ref.shape[0]
    zero = jnp.zeros((rows, HALF), BF16)
    tiles = [[held[z, :, h * HALF : (h + 1) * HALF] for h in range(2)] for z in range(levels)]
    for layer in range(layers):
        taps = []
        for k in range(KV + 1):
            column = []
            for zp in range(levels // 2):
                z = 2 * zp + k - KV // 2
                for h in range(2):
                    column.append(tiles[z][h] if 0 <= z < levels else zero)
            taps.append(jnp.concatenate(column, axis=0))
        total = jnp.dot(
            jnp.concatenate(taps, axis=1), weight_ref[layer], preferred_element_type=F32
        )
        following = []
        for z in range(levels):
            following.append([])
            for h in range(2):
                start = ((z // 2) * 2 + h) * rows
                lane = (z % 2) * HALF
                part = total[start : start + rows, lane : lane + HALF]
                value = tiles[z][h].astype(F32) + gelu(part + bias[layer : layer + 1])
                if layer == layers - 1:
                    value = value + source_ref[z, :, h * HALF : (h + 1) * HALF]
                following[z].append(value.astype(BF16))
        tiles = following
    across = rows // height
    group = 256 // rows
    swap = swap_matrix(group * height, across)
    size = group * height
    for g in range(levels // group):
        pieces = [jnp.concatenate(tiles[g * group + z], axis=1) for z in range(group)]
        turned = jnp.dot(
            swap, jnp.concatenate(pieces, axis=0), preferred_element_type=F32
        ).astype(BF16)
        for s in range(across):
            out_ref[g * group : (g + 1) * group, :, s * SL : (s + 1) * SL] = turned[
                s * size : (s + 1) * size
            ].reshape(group, height, SL)


def vertical(me, pieces, source, weight, bias, height):
    levels, rows, _ = source.shape
    lanes = rows // height * SL
    full = pl.BlockSpec(memory_space=pltpu.VMEM)
    return pl.pallas_call(
        functools.partial(vertical_kernel, height),
        in_specs=[pl.BlockSpec(memory_space=pltpu.SMEM)] + [full] * (len(pieces) + 3),
        out_specs=full,
        out_shape=jax.ShapeDtypeStruct((levels, height, lanes), BF16),
        scratch_shapes=[pltpu.VMEM((levels, rows, SL), BF16)],
        compiler_params=params(),
        cost_estimate=cost(4 * levels * rows * weight.shape[1] * SL, 6 * 10**6),
    )(me, *pieces, source, weight, bias)


def exchange(block, distance):
    count = lax.axis_size("cols")
    return lax.ppermute(block, "cols", [(i, i ^ distance) for i in range(count)])


def body(
    field, depth_kernel, point_weight, point_bias, vert_weight, vert_bias, exhaust, owner, cells
):
    columns, bands = lax.axis_size("cols"), lax.axis_size("rows")
    forward = [(i, i + 1) for i in range(bands - 1)]
    backward = [(target, source) for source, target in forward]
    levels, height, lanes = field.shape
    segments = lanes // SL
    per = segments // columns
    me = lax.axis_index("cols")
    own, first, last = to_segments(field)
    low = lax.ppermute(last, "rows", forward)
    high = lax.ppermute(first, "rows", backward)
    across = across_weights(depth_kernel, point_weight)
    bias = point_bias.reshape(1, C)
    if per % 16 == 0 and columns % 2 == 0:
        tiles = columns // 2
        spot, near = me % tiles, me // tiles
        place = lambda half: jnp.stack([half * (segments // 2), spot]).astype(jnp.int32)
        close_rows, far_rows = bucket(
            near.reshape(1).astype(jnp.int32), exhaust, owner, cells, columns, 2
        )
        relayed = exchange(far_rows, tiles)
        far = half_horizontal(place(1 - near), own, low, high, across, bias, tiles)
        pieces = [exchange(block, tiles + slot) for slot, block in enumerate(far)]
        spot_near, _ = lax.optimization_barrier((place(near), far[0]))
        close = half_horizontal(
            spot_near, own, low, high, across, bias, tiles, (close_rows, relayed)
        )
        close = [exchange(block, slot) if slot else block for slot, block in enumerate(close)]
        pieces += close
        got = close
        at = me ^ tiles
    else:
        (sent,) = bucket(jnp.zeros((1,), jnp.int32), exhaust, owner, cells, columns, 1)
        got = lax.all_to_all(sent, "cols", split_axis=0, concat_axis=0, tiled=True)
        got = [jnp.transpose(got, (1, 0, 2)).reshape(PACK, -1)]
        mixed = horizontal(own, low, high, across, bias, columns)
        mixed = mixed.reshape(columns, levels, -1, SL)
        taken = lax.all_to_all(mixed, "cols", split_axis=0, concat_axis=0, tiled=True)
        pieces = [taken.reshape(-1, SL)]
        at = me * 0
    depth = columns * levels
    source = make_source(got, depth * height * per).reshape(depth, height * per, SL)
    up = up_weights(vert_weight)
    return vertical(at.reshape(1).astype(jnp.int32), pieces, source, up, vert_bias, height)


def solution(mesh):
    placed = (
        P("cols", "rows", None),
        P(),
        P(),
        P(),
        P(),
        P(),
        P(("rows", "cols"), None),
        P(("rows", "cols"), None),
        P(("rows", "cols")),
    )
    return jax.shard_map(
        body, mesh=mesh, in_specs=placed, out_specs=P(None, "rows", "cols"), check_vma=False
    )
```

time: 77 us -> 57.8 us (0.75)
  the two profiles are of different devices: /device:TPU:0 before, /device:TPU:9 now
where the time goes in v2:
time: 57.8 us; the launch traced here: 57.3 us
  Pallas kernels  18.1 us (31%)
  waiting for transfers between devices  17.3 us (30%)
  starting transfers between devices  17 us (29%)
  local copies, waits for them, and re-layouts  4.8 us (8%)
    ppermute x8, waiting for transfers between devices, exchange(): lax.ppermute(block, 'cols', [(i, i ^ distance) for i in range(count)])  12.9 us
    ppermute x8, starting transfers between devices, exchange(): lax.ppermute(block, 'cols', [(i, i ^ distance) for i in range(count)])  11.4 us
    pallas_call x1, Pallas kernels, vertical(): pl.pallas_call(functools.partial(vertical_kernel, height), in_specs=[pl.B...  7.23 us
    pallas_call x2, Pallas kernels, half_horizontal(): pl.pallas_call(functools.partial(half_kernel, tiles), in_specs=[pl.BlockS...  5.88 us
    unnamed x18, local copies, waits for them, and re-layouts  4.8 us
    ppermute x1, waiting for transfers between devices, body(): high = lax.ppermute(first, 'rows', backward)  4.29 us
    ppermute x1, starting transfers between devices, body(): low = lax.ppermute(last, 'rows', forward)  3.67 us
    ppermute x1, starting transfers between devices, body(): high = lax.ppermute(first, 'rows', backward)  1.92 us
  transfers between devices with their start and end apart: 10, of which 7 were waited for; matrix products, arithmetic and copies ran while one was open for 0% of the time, Pallas kernels for 12%

profile of v2, /device:TPU:9, one launch (start us, length us, event | category | flops | bytes accessed | tf_op | source)
XLA Modules:
  0.0 57.3 jit_solution(10820641862203734757)
XLA Ops:
  0.0 0.0 copy-start
  0.0 1.2 %copy-done = bf16[4,4,32768]{2,1,0:T(4,128)(2,1)S(1)} copy-done((bf16[4,4,32768]{2,1,0:T(4,128)(2,1)S(1)}, bf16[4,4,32768]{2,1,0:T(4,128)(2,1)}, u32[]{:S(2)}) %copy-start) | copy-done | bytes 1048600
  1.2 0.0 copy-start.5
  1.2 1.7 %shard_map.91 = (bf16[4,4,128,256]{3,2,1,0:T(8,128)(2,1)S(1)}, bf16[3,4,128,256]{3,2,1,0:T(8,128)(2,1)}, bf16[3,4,128,256]{3,2,1,0:T(8,128)(2,1)}) custom-call(bf16[4,4,32768]{2,1,0:T(4,128)(2,1)S(1)} %copy-done), custom_call_target="tpu_custom_call" | custom-call | flops 268435456 | bytes 4194304 | tf_op jit(solution)/shard_map/pallas_call | solution.py:83
  2.9 3.7 %collective-permute-start = (bf16[3,4,128,256]{3,2,1,0:T(8,128)(2,1)}, bf16[3,4,128,256]{3,2,1,0:T(8,128)(2,1)S(1)}, u32[]{:S(2)}, u32[]{:S(2)}) collective-permute-start(bf16[3,4,128,256]{3,2,1,0:T(8,128)(2,1)} %get-tuple-element.20), channel_id=1, source_target_pairs={{0,8},{8,16},{16,24},{1,9},{9,17},{17,25},{2,10},{10,18},{18,26},{... | collective-permute-start | bytes 2359304 | tf_op jit(solution)/shard_map/ppermute | solution.py:451
  6.6 1.9 %collective-permute-start.1 = (bf16[3,4,128,256]{3,2,1,0:T(8,128)(2,1)}, bf16[3,4,128,256]{3,2,1,0:T(8,128)(2,1)S(1)}, u32[]{:S(2)}, u32[]{:S(2)}) collective-permute-start(bf16[3,4,128,256]{3,2,1,0:T(8,128)(2,1)} %get-tuple-element.21), channel_id=1, source_target_pairs={{8,0},{16,8},{24,16},{9,1},{17,9},{25,17},{10,2},{18,10},{26,18},{... | collective-permute-start | bytes 2359304 | tf_op jit(solution)/shard_map/ppermute | solution.py:452
  8.5 0.0 copy-start.2
  8.5 0.7 %copy-done.2 = bf16[512,32]{0,1:T(8,128)(2,1)S(1)} copy-done((bf16[512,32]{0,1:T(8,128)(2,1)S(1)}, bf16[512,32]{0,1:T(8,128)(2,1)}, u32[]{:S(2)}) %copy-start.2) | copy-done | bytes 32792
  9.3 0.0 copy-start.6
  9.3 0.7 %copy-done.6 = s32[512,1]{0,1:T(1,128)S(1)} copy-done((s32[512,1]{0,1:T(1,128)S(1)}, s32[512,1]{0,1:T(1,128)}, u32[]{:S(2)}) %copy-start.6) | copy-done | bytes 2072
  10.0 0.0 copy-start.7
  10.0 0.7 %copy-done.7 = s32[512]{0:T(512)S(1)} copy-done((s32[512]{0:T(512)S(1)}, s32[512]{0:T(512)}, u32[]{:S(2)}) %copy-start.7) | copy-done | bytes 2072
  10.6 0.7 %shard_map.94 = (bf16[4,48,128]{2,1,0:T(8,128)(2,1)S(1)}, bf16[4,48,128]{2,1,0:T(8,128)(2,1)S(1)}) custom-call(s32[1]{0:T(128)} %bitcast.5.near_ref, bf16[32,512]{1,0:T(8,128)(2,1)S(1)} %bitcast.13, s32[1,512]{1,0:T(1,128)S(1)} %bitcast.16, s32[1,512]{1,0:T(1,128)S(1)} %bitcast.17), custom_call_target="tpu_custom_call" | custom-call | flops 1000 | bytes 1000 | tf_op jit(solution)/shard_map/pallas_call | solution.py:331
  11.3 2.4 %collective-permute-start.6 = (bf16[4,48,128]{2,1,0:T(8,128)(2,1)S(1)}, bf16[4,48,128]{2,1,0:T(8,128)(2,1)S(1)}, u32[]{:S(2)}, u32[]{:S(2)}) collective-permute-start(bf16[4,48,128]{2,1,0:T(8,128)(2,1)S(1)} %get-tuple-element.28), channel_id=1, source_target_pairs={{0,4},{1,5},{2,6},{3,7},{4,0},{5,1},{6,2},{7,3},{8,12},{9,13},{10,... | collective-permute-start | bytes 147464 | tf_op jit(solution)/shard_map/ppermute | solution.py:437
  13.7 0.1 pad_add_fusion
  13.8 0.0 copy-start.3
  13.8 0.7 %copy-done.3 = f32[7,7,32]{2,1,0:T(8,128)S(1)} copy-done((f32[7,7,32]{2,1,0:T(8,128)S(1)}, f32[7,7,32]{2,1,0:T(8,128)}, u32[]{:S(2)}) %copy-start.3) | copy-done | bytes 6296
  14.5 0.0 copy-start.4
  14.5 0.7 %copy-done.4 = bf16[32,32]{1,0:T(8,128)(2,1)S(1)} copy-done((bf16[32,32]{1,0:T(8,128)(2,1)S(1)}, bf16[32,32]{1,0:T(8,128)(2,1)}, u32[]{:S(2)}) %copy-start.4) | copy-done | bytes 2072
  15.2 0.5 shard_map.92.weight_ref
  15.7 0.1 collective-permute-done.low_ref
  15.8 4.3 %collective-permute-done.1.high_ref = bf16[3,4,128,256]{3,2,1,0:T(8,128)(2,1)S(1)} collective-permute-done((bf16[3,4,128,256]{3,2,1,0:T(8,128)(2,1)}, bf16[3,4,128,256]{3,2,1,0:T(8,128)(2,1)S(1)}, u32[]{:S(2)}, u32[]{:S(2)}) %collective-permute-start.1) | collective-permute-done | bytes 786464 | tf_op jit(solution)/shard_map/ppermute | solution.py:452
  20.1 0.0 copy-done.5
  20.1 3.3 %shard_map.93 = (bf16[256,256]{1,0:T(8,128)(2,1)}, bf16[256,256]{1,0:T(8,128)(2,1)S(1)}, bf16[256,256]{1,0:T(8,128)(2,1)S(1)}, bf16[256,256]{1,0:T(8,128)(2,1)S(1)}) custom-call(s32[2]{0:T(128)S(1)} %get-tuple-element.33.place_ref, bf16[4,4,128,256]{3,2,1,0:T(8,128)(2,1)S(1)} %get-tuple-element.19.own_ref, ...), custom_call_target="tpu_custom_call" | custom-call | flops 1000 | bytes 1000 | tf_op jit(solution)/shard_map/pallas_call | solution.py:285
  23.4 0.0 collective-permute-done.6.rest_1_
  23.4 0.0 copy-start.1
  23.4 2.6 %shard_map.95 = (bf16[304,256]{1,0:T(8,128)(2,1)S(1)}, bf16[304,256]{1,0:T(8,128)(2,1)S(1)}, bf16[304,256]{1,0:T(8,128)(2,1)S(1)}, bf16[304,256]{1,0:T(8,128)(2,1)S(1)}) custom-call(s32[2]{0:T(128)S(1)} %get-tuple-element.26.place_ref, bf16[4,4,128,256]{3,2,1,0:T(8,128)(2,1)S(1)} %get-tuple-element.19.own_ref, ...), custom_call_target="tpu_custom_call" | custom-call | flops 1000 | bytes 1000 | tf_op jit(solution)/shard_map/pallas_call | solution.py:285
  26.0 1.3 %collective-permute-start.7 = (bf16[304,256]{1,0:T(8,128)(2,1)S(1)}, bf16[304,256]{1,0:T(8,128)(2,1)S(1)}, u32[]{:S(2)}, u32[]{:S(2)}) collective-permute-start(bf16[304,256]{1,0:T(8,128)(2,1)S(1)} %get-tuple-element.30), channel_id=1, source_target_pairs={{0,1},{1,0},{2,3},{3,2},{4,5},{5,4},{6,7},{7,6},{8,9},{9,8},{10,11... | collective-permute-start | bytes 466952 | tf_op jit(solution)/shard_map/ppermute | solution.py:437
  27.3 0.2 collective-permute-start.8
  27.5 1.2 %collective-permute-start.9 = (bf16[304,256]{1,0:T(8,128)(2,1)S(1)}, bf16[304,256]{1,0:T(8,128)(2,1)S(1)}, u32[]{:S(2)}, u32[]{:S(2)}) collective-permute-start(bf16[304,256]{1,0:T(8,128)(2,1)S(1)} %get-tuple-element.32), channel_id=1, source_target_pairs={{0,3},{1,2},{2,1},{3,0},{4,7},{5,6},{6,5},{7,4},{8,11},{9,10},{10,... | collective-permute-start | bytes 466952 | tf_op jit(solution)/shard_map/ppermute | solution.py:437
  28.7 2.3 %collective-permute-start.2 = (bf16[256,256]{1,0:T(8,128)(2,1)}, bf16[256,256]{1,0:T(8,128)(2,1)S(1)}, u32[]{:S(2)}, u32[]{:S(2)}) collective-permute-start(bf16[256,256]{1,0:T(8,128)(2,1)} %get-tuple-element.22), channel_id=1, source_target_pairs={{0,4},{1,5},{2,6},{3,7},{4,0},{5,1},{6,2},{7,3},{8,12},{9,13},{10,... | collective-permute-start | bytes 393224 | tf_op jit(solution)/shard_map/ppermute | solution.py:437
  31.0 1.0 %collective-permute-start.3 = (bf16[256,256]{1,0:T(8,128)(2,1)S(1)}, bf16[256,256]{1,0:T(8,128)(2,1)S(1)}, u32[]{:S(2)}, u32[]{:S(2)}) collective-permute-start(bf16[256,256]{1,0:T(8,128)(2,1)S(1)} %get-tuple-element.23), channel_id=1, source_target_pairs={{0,5},{1,4},{2,7},{3,6},{4,1},{5,0},{6,3},{7,2},{8,13},{9,12},{10,... | collective-permute-start | bytes 393224 | tf_op jit(solution)/shard_map/ppermute | solution.py:437
  32.0 0.0 collective-permute-done.7.refs_1_.refs_5_
  32.0 1.3 %collective-permute-start.4 = (bf16[256,256]{1,0:T(8,128)(2,1)S(1)}, bf16[256,256]{1,0:T(8,128)(2,1)S(1)}, u32[]{:S(2)}, u32[]{:S(2)}) collective-permute-start(bf16[256,256]{1,0:T(8,128)(2,1)S(1)} %get-tuple-element.24), channel_id=1, source_target_pairs={{0,6},{1,7},{2,4},{3,5},{4,2},{5,3},{6,0},{7,1},{8,14},{9,15},{10,... | collective-permute-start | bytes 393224 | tf_op jit(solution)/shard_map/ppermute | solution.py:437
  33.3 0.0 collective-permute-done.8.refs_2_.refs_6_
  33.3 1.7 %collective-permute-start.5 = (bf16[256,256]{1,0:T(8,128)(2,1)S(1)}, bf16[256,256]{1,0:T(8,128)(2,1)S(1)}, u32[]{:S(2)}, u32[]{:S(2)}) collective-permute-start(bf16[256,256]{1,0:T(8,128)(2,1)S(1)} %get-tuple-element.25), channel_id=1, source_target_pairs={{0,7},{1,6},{2,5},{3,4},{4,3},{5,2},{6,1},{7,0},{8,15},{9,14},{10,... | collective-permute-start | bytes 393224 | tf_op jit(solution)/shard_map/ppermute | solution.py:437
  35.0 0.0 copy-done.1
  35.0 0.9 %shard_map.97.refs_9_ = bf16[2,1280,256]{2,1,0:T(8,128)(2,1)S(1)} custom-call(bf16[2,32,288]{2,1,0:T(8,128)(2,1)S(1)} %bitcast.12), custom_call_target="tpu_custom_call" | custom-call | flops 1000 | bytes 1000 | tf_op jit(solution)/shard_map/pallas_call | solution.py:148
  35.9 0.0 copy-start.8
  35.9 1.3 %collective-permute-done.9.refs_3_.refs_7_ = bf16[304,256]{1,0:T(8,128)(2,1)S(1)} collective-permute-done((bf16[304,256]{1,0:T(8,128)(2,1)S(1)}, bf16[304,256]{1,0:T(8,128)(2,1)S(1)}, u32[]{:S(2)}, u32[]{:S(2)}) %collective-permute-start.9) | collective-permute-done | bytes 155680 | tf_op jit(solution)/shard_map/ppermute | solution.py:437
  37.2 1.3 %shard_map.96 = f32[2048,256]{1,0:T(8,128)S(1)} custom-call(bf16[304,256]{1,0:T(8,128)(2,1)S(1)} %get-tuple-element.29.refs_0_.refs_4_, bf16[304,256]{1,0:T(8,128)(2,1)S(1)} %collective-permute-done.7.refs_1_.refs_5_, bf16[304,256]{1,0:T(8,128)(2,1)S(1)} %collective-permute-done.8.refs_2_.refs_6_, bf16[304,256]{1,0:T(8,128)(2,1)S(1)} %collective-permute-done.9.refs_3_.refs_7_), custom_call_target="tpu_custom_call" | custom-call | flops 1000 | bytes 1000 | tf_op jit(solution)/shard_map/pallas_call | solution.py:358
  38.6 4.2 %collective-permute-done.2.refs_0_ = bf16[256,256]{1,0:T(8,128)(2,1)S(1)} collective-permute-done((bf16[256,256]{1,0:T(8,128)(2,1)}, bf16[256,256]{1,0:T(8,128)(2,1)S(1)}, u32[]{:S(2)}, u32[]{:S(2)}) %collective-permute-start.2) | collective-permute-done | bytes 131104 | tf_op jit(solution)/shard_map/ppermute | solution.py:437
  42.7 2.7 %collective-permute-done.3.refs_1_ = bf16[256,256]{1,0:T(8,128)(2,1)S(1)} collective-permute-done((bf16[256,256]{1,0:T(8,128)(2,1)S(1)}, bf16[256,256]{1,0:T(8,128)(2,1)S(1)}, u32[]{:S(2)}, u32[]{:S(2)}) %collective-permute-start.3) | collective-permute-done | bytes 131104 | tf_op jit(solution)/shard_map/ppermute | solution.py:437
  45.4 2.6 %collective-permute-done.4.refs_2_ = bf16[256,256]{1,0:T(8,128)(2,1)S(1)} collective-permute-done((bf16[256,256]{1,0:T(8,128)(2,1)S(1)}, bf16[256,256]{1,0:T(8,128)(2,1)S(1)}, u32[]{:S(2)}, u32[]{:S(2)}) %collective-permute-start.4) | collective-permute-done | bytes 131104 | tf_op jit(solution)/shard_map/ppermute | solution.py:437
  48.0 2.1 %collective-permute-done.5.refs_3_ = bf16[256,256]{1,0:T(8,128)(2,1)S(1)} collective-permute-done((bf16[256,256]{1,0:T(8,128)(2,1)S(1)}, bf16[256,256]{1,0:T(8,128)(2,1)S(1)}, u32[]{:S(2)}, u32[]{:S(2)}) %collective-permute-start.5) | collective-permute-done | bytes 131104 | tf_op jit(solution)/shard_map/ppermute | solution.py:437
  50.1 0.0 copy-done.8
  50.1 7.2 %shard_map.98 = bf16[32,4,4096]{2,1,0:T(4,128)(2,1)} custom-call(s32[1]{0:T(128)} %bitcast.me_ref, bf16[256,256]{1,0:T(8,128)(2,1)S(1)} %collective-permute-done.2.refs_0_, bf16[256,256]{1,0:T(8,128)(2,1)S(1)} %collective-permute-done.3.refs_1_, bf16[256,256]{1,0:T(8,128)(2,1)S(1)} %collective-permute-done.4.refs_2_, ...), custom_call_target="tpu_custom_call" | custom-call | flops 2684354560 | bytes 6000000 | tf_op jit(solution)/shard_map/pallas_call | solution.py:424
Async XLA Ops:
  0.0 1.2 %copy-start = (bf16[4,4,32768]{2,1,0:T(4,128)(2,1)S(1)}, bf16[4,4,32768]{2,1,0:T(4,128)(2,1)}, u32[]{:S(2)}) copy-start(bf16[4,4,32768]{2,1,0:T(4,128)(2,1)} %field_ref.1) | copy-start | bytes 3145732
  1.2 18.9 %copy-start.5 = (f32[32]{0:T(128)S(1)}, f32[32]{0:T(128)}, u32[]{:S(2)}) copy-start(f32[32]{0:T(128)} %param.12) | copy-start | bytes 388
  2.9 12.9 %collective-permute-start = (bf16[3,4,128,256]{3,2,1,0:T(8,128)(2,1)}, bf16[3,4,128,256]{3,2,1,0:T(8,128)(2,1)S(1)}, u32[]{:S(2)}, u32[]{:S(2)}) collective-permute-start(bf16[3,4,128,256]{3,2,1,0:T(8,128)(2,1)} %get-tuple-element.20), channel_id=1, source_target_pairs={{0,8},{8,16},{16,24},{1,9},{9,17},{17,25},{2,10},{10,18},{18,26},{... | collective-permute-start | bytes 2359304 | tf_op jit(solution)/shard_map/ppermute | solution.py:451
  6.6 13.5 %collective-permute-start.1 = (bf16[3,4,128,256]{3,2,1,0:T(8,128)(2,1)}, bf16[3,4,128,256]{3,2,1,0:T(8,128)(2,1)S(1)}, u32[]{:S(2)}, u32[]{:S(2)}) collective-permute-start(bf16[3,4,128,256]{3,2,1,0:T(8,128)(2,1)} %get-tuple-element.21), channel_id=1, source_target_pairs={{8,0},{16,8},{24,16},{9,1},{17,9},{25,17},{10,2},{18,10},{26,18},{... | collective-permute-start | bytes 2359304 | tf_op jit(solution)/shard_map/ppermute | solution.py:452
  8.5 0.8 %copy-start.2 = (bf16[512,32]{0,1:T(8,128)(2,1)S(1)}, bf16[512,32]{0,1:T(8,128)(2,1)}, u32[]{:S(2)}) copy-start(bf16[512,32]{0,1:T(8,128)(2,1)} %param.15) | copy-start | bytes 98308
  9.3 0.7 %copy-start.6 = (s32[512,1]{0,1:T(1,128)S(1)}, s32[512,1]{0,1:T(1,128)}, u32[]{:S(2)}) copy-start(s32[512,1]{0,1:T(1,128)} %param.16) | copy-start | bytes 6148
  10.0 0.7 %copy-start.7 = (s32[512]{0:T(512)S(1)}, s32[512]{0:T(512)}, u32[]{:S(2)}) copy-start(s32[512]{0:T(512)} %param.17) | copy-start | bytes 6148
  11.3 12.0 %collective-permute-start.6 = (bf16[4,48,128]{2,1,0:T(8,128)(2,1)S(1)}, bf16[4,48,128]{2,1,0:T(8,128)(2,1)S(1)}, u32[]{:S(2)}, u32[]{:S(2)}) collective-permute-start(bf16[4,48,128]{2,1,0:T(8,128)(2,1)S(1)} %get-tuple-element.28), channel_id=1, source_target_pairs={{0,4},{1,5},{2,6},{3,7},{4,0},{5,1},{6,2},{7,3},{8,12},{9,13},{10,... | collective-permute-start | bytes 147464 | tf_op jit(solution)/shard_map/ppermute | solution.py:437
  13.8 0.7 %copy-start.3 = (f32[7,7,32]{2,1,0:T(8,128)S(1)}, f32[7,7,32]{2,1,0:T(8,128)}, u32[]{:S(2)}) copy-start(f32[7,7,32]{2,1,0:T(8,128)} %depth_ref.1) | copy-start | bytes 18820
  14.5 0.7 %copy-start.4 = (bf16[32,32]{1,0:T(8,128)(2,1)S(1)}, bf16[32,32]{1,0:T(8,128)(2,1)}, u32[]{:S(2)}) copy-start(bf16[32,32]{1,0:T(8,128)(2,1)} %point_ref.1) | copy-start | bytes 6148
  23.4 11.6 %copy-start.1 = (bf16[2,288,32]{1,2,0:T(8,128)(2,1)S(1)}, bf16[2,288,32]{1,2,0:T(8,128)(2,1)}, u32[]{:S(2)}) copy-start(bf16[2,288,32]{1,2,0:T(8,128)(2,1)} %param.13) | copy-start | bytes 110596
  26.0 6.0 %collective-permute-start.7 = (bf16[304,256]{1,0:T(8,128)(2,1)S(1)}, bf16[304,256]{1,0:T(8,128)(2,1)S(1)}, u32[]{:S(2)}, u32[]{:S(2)}) collective-permute-start(bf16[304,256]{1,0:T(8,128)(2,1)S(1)} %get-tuple-element.30), channel_id=1, source_target_pairs={{0,1},{1,0},{2,3},{3,2},{4,5},{5,4},{6,7},{7,6},{8,9},{9,8},{10,11... | collective-permute-start | bytes 466952 | tf_op jit(solution)/shard_map/ppermute | solution.py:437
  27.3 6.0 %collective-permute-start.8 = (bf16[304,256]{1,0:T(8,128)(2,1)S(1)}, bf16[304,256]{1,0:T(8,128)(2,1)S(1)}, u32[]{:S(2)}, u32[]{:S(2)}) collective-permute-start(bf16[304,256]{1,0:T(8,128)(2,1)S(1)} %get-tuple-element.31), channel_id=1, source_target_pairs={{0,2},{1,3},{2,0},{3,1},{4,6},{5,7},{6,4},{7,5},{8,10},{9,11},{10,... | collective-permute-start | bytes 466952 | tf_op jit(solution)/shard_map/ppermute | solution.py:437
  27.5 9.8 %collective-permute-start.9 = (bf16[304,256]{1,0:T(8,128)(2,1)S(1)}, bf16[304,256]{1,0:T(8,128)(2,1)S(1)}, u32[]{:S(2)}, u32[]{:S(2)}) collective-permute-start(bf16[304,256]{1,0:T(8,128)(2,1)S(1)} %get-tuple-element.32), channel_id=1, source_target_pairs={{0,3},{1,2},{2,1},{3,0},{4,7},{5,6},{6,5},{7,4},{8,11},{9,10},{10,... | collective-permute-start | bytes 466952 | tf_op jit(solution)/shard_map/ppermute | solution.py:437
  28.7 14.0 %collective-permute-start.2 = (bf16[256,256]{1,0:T(8,128)(2,1)}, bf16[256,256]{1,0:T(8,128)(2,1)S(1)}, u32[]{:S(2)}, u32[]{:S(2)}) collective-permute-start(bf16[256,256]{1,0:T(8,128)(2,1)} %get-tuple-element.22), channel_id=1, source_target_pairs={{0,4},{1,5},{2,6},{3,7},{4,0},{5,1},{6,2},{7,3},{8,12},{9,13},{10,... | collective-permute-start | bytes 393224 | tf_op jit(solution)/shard_map/ppermute | solution.py:437
  31.0 14.4 %collective-permute-start.3 = (bf16[256,256]{1,0:T(8,128)(2,1)S(1)}, bf16[256,256]{1,0:T(8,128)(2,1)S(1)}, u32[]{:S(2)}, u32[]{:S(2)}) collective-permute-start(bf16[256,256]{1,0:T(8,128)(2,1)S(1)} %get-tuple-element.23), channel_id=1, source_target_pairs={{0,5},{1,4},{2,7},{3,6},{4,1},{5,0},{6,3},{7,2},{8,13},{9,12},{10,... | collective-permute-start | bytes 393224 | tf_op jit(solution)/shard_map/ppermute | solution.py:437
  32.0 16.0 %collective-permute-start.4 = (bf16[256,256]{1,0:T(8,128)(2,1)S(1)}, bf16[256,256]{1,0:T(8,128)(2,1)S(1)}, u32[]{:S(2)}, u32[]{:S(2)}) collective-permute-start(bf16[256,256]{1,0:T(8,128)(2,1)S(1)} %get-tuple-element.24), channel_id=1, source_target_pairs={{0,6},{1,7},{2,4},{3,5},{4,2},{5,3},{6,0},{7,1},{8,14},{9,15},{10,... | collective-permute-start | bytes 393224 | tf_op jit(solution)/shard_map/ppermute | solution.py:437
  33.3 16.8 %collective-permute-start.5 = (bf16[256,256]{1,0:T(8,128)(2,1)S(1)}, bf16[256,256]{1,0:T(8,128)(2,1)S(1)}, u32[]{:S(2)}, u32[]{:S(2)}) collective-permute-start(bf16[256,256]{1,0:T(8,128)(2,1)S(1)} %get-tuple-element.25), channel_id=1, source_target_pairs={{0,7},{1,6},{2,5},{3,4},{4,3},{5,2},{6,1},{7,0},{8,15},{9,14},{10,... | collective-permute-start | bytes 393224 | tf_op jit(solution)/shard_map/ppermute | solution.py:437
  35.9 14.2 %copy-start.8 = (f32[2,32]{1,0:T(2,128)S(1)}, f32[2,32]{1,0:T(2,128)}, u32[]{:S(2)}) copy-start(f32[2,32]{1,0:T(2,128)} %refs_10_.1) | copy-start | bytes 772

commit v3 on v2

v3 whole, which is shorter than its diff:
```python
import functools

import jax
import jax.numpy as jnp
from jax import lax
from jax.experimental import pallas as pl
from jax.experimental.pallas import tpu as pltpu
from jax.sharding import PartitionSpec as P

C = 32
KH = 7
KV = 9
SEG = 8
SL = SEG * C
PAD = 2
TAPS = (KV + 1) // 2
HALF = SL // 2
PACK = 48
VMEM = 20 * 1024 * 1024
NT = (((1,), (1,)), ((), ()))
F32 = jnp.float32
BF16 = jnp.bfloat16


def params():
    return pltpu.CompilerParams(vmem_limit_bytes=VMEM)


def cost(flops, moved):
    return pl.CostEstimate(flops=flops, bytes_accessed=moved, transcendentals=0)


def whole(shape):
    return pl.BlockSpec(shape, lambda *_: (0,) * len(shape))


def gelu(x):
    return 0.5 * x * (1.0 + jnp.tanh(0.7978845608028654 * (x + 0.044715 * (x * x * x))))


def swap_matrix(outer, inner):
    size = outer * inner
    row = lax.broadcasted_iota(jnp.int32, (size, size), 0)
    column = lax.broadcasted_iota(jnp.int32, (size, size), 1)
    return (column == (row % outer) * inner + row // outer).astype(BF16)


def segment_kernel(ids_ref, field_ref, own_ref, cross_ref, pair_ref):
    levels, height, lanes = field_ref.shape
    rows = levels * height
    group = 256 // rows
    swap = swap_matrix(group, rows)
    for g in range(lanes // (group * SL)):
        at = [(g * group + s) * SL for s in range(group)]
        pieces = [field_ref[:, :, n : n + SL].reshape(rows, SL) for n in at]
        got = jnp.dot(
            swap, jnp.concatenate(pieces, axis=0), preferred_element_type=F32
        ).astype(BF16)
        for z in range(levels):
            for y in range(height):
                start = (z * height + y) * group
                own_ref[y, z, g * group : (g + 1) * group] = got[start : start + group]
    odd = ids_ref[1] % 2
    for y in range(3):
        cross_ref[y] = own_ref[odd * (height - 3) + y]
        pair_ref[y] = own_ref[(1 - odd) * (height - 3) + y]


def to_segments(ids, field):
    levels, height, lanes = field.shape
    full = pl.BlockSpec(memory_space=pltpu.VMEM)
    out = lambda n: jax.ShapeDtypeStruct((n, levels, lanes // SL, SL), BF16)
    return pl.pallas_call(
        segment_kernel,
        in_specs=[pl.BlockSpec(memory_space=pltpu.SMEM), full],
        out_specs=[full] * 3,
        out_shape=[out(height), out(3), out(3)],
        compiler_params=params(),
        cost_estimate=cost(1000, 1000),
    )(ids, field)


def across_kernel(depth_ref, point_ref, out_ref):
    point = jnp.concatenate([point_ref[...].astype(F32)] * (HALF // C), axis=1)
    lane = lax.broadcasted_iota(jnp.int32, (C, HALF), 1) // C
    wide = 3 * HALF
    out_ref[...] = jnp.zeros_like(out_ref)
    for i in range(KH):
        columns = jnp.transpose(depth_ref[i])
        scaled = [point * columns[:, j : j + 1] for j in range(KH)]
        for xt in range(wide // C):
            block = jnp.zeros((C, HALF), F32)
            for xo in range(HALF // C):
                j = xt - 1 - xo
                if 0 <= j < KH:
                    block = jnp.where(lane == xo, scaled[j], block)
            block = block.astype(BF16)
            for yo in range(2):
                row = (i + yo + PAD) * wide + xt * C
                out_ref[row : row + C, yo * HALF : (yo + 1) * HALF] = block


def across_weights(depth_kernel, point_weight):
    return pl.pallas_call(
        across_kernel,
        out_shape=jax.ShapeDtypeStruct(((KH + 1 + 2 * PAD) * 3 * HALF, SL), BF16),
        compiler_params=params(),
        cost_estimate=cost(1000, 1000),
    )(depth_kernel, point_weight)


def up_kernel(tiles, ids_ref, vert_ref, out_ref):
    row = lax.broadcasted_iota(jnp.int32, (KV * HALF, KV * C), 0)
    column = lax.broadcasted_iota(jnp.int32, (KV * HALF, KV * C), 1)
    spread = ((row // HALF == column // C) & (row % C == column % C)).astype(BF16)
    row = lax.broadcasted_iota(jnp.int32, (C, HALF), 0)
    column = lax.broadcasted_iota(jnp.int32, (C, HALF), 1)
    repeat = (row == column % C).astype(BF16)
    row = lax.broadcasted_iota(jnp.int32, (KV * HALF, HALF), 0)
    column = lax.broadcasted_iota(jnp.int32, (KV * HALF, HALF), 1)
    same = (row % HALF) // C == column // C
    zero = jnp.zeros((HALF, HALF), BF16)
    for layer in range(vert_ref.shape[0]):
        tall = lax.dot_general(spread, vert_ref[layer], NT, preferred_element_type=F32).astype(BF16)
        wide = jnp.dot(tall, repeat, preferred_element_type=F32)
        wide = jnp.where(same, wide, 0.0).astype(BF16)
        for block in range(TAPS):
            at = pl.multiple_of(turned_index(ids_ref, tiles, block, TAPS) * SL, SL)
            for zi in range(2):
                parts = []
                for zo in range(2):
                    k = 2 * block + zi - zo
                    parts.append(wide[k * HALF : (k + 1) * HALF] if 0 <= k < KV else zero)
                out_ref[layer, pl.ds(at + zi * HALF, HALF)] = jnp.concatenate(parts, axis=1)


def turned_index(ids_ref, tiles, index, count):
    if not tiles:
        return index
    return jnp.where(ids_ref[0] // tiles == 0, index, count - 1 - index)


def up_weights(ids, vert_weight, tiles):
    vert = jnp.transpose(vert_weight, (0, 2, 1))
    full = pl.BlockSpec(memory_space=pltpu.VMEM)
    return pl.pallas_call(
        functools.partial(up_kernel, tiles),
        in_specs=[pl.BlockSpec(memory_space=pltpu.SMEM), full],
        out_specs=full,
        out_shape=jax.ShapeDtypeStruct((vert.shape[0], TAPS * SL, SL), BF16),
        compiler_params=params(),
        cost_estimate=cost(1000, 1000),
    )(ids, vert)


def bias_row(row):
    return jnp.concatenate([row] * (HALF // C), axis=1)


def horizontal_kernel(own_ref, low_ref, high_ref, weight_ref, bias_ref, out_ref):
    height = own_ref.shape[0]
    segments = own_ref.shape[2]
    row = lax.broadcasted_iota(jnp.int32, (segments, HALF), 0)
    lines = [low_ref[y, 0] for y in range(3)]
    lines += [own_ref[y, 0] for y in range(height)]
    lines += [high_ref[y, 0] for y in range(3)]
    left, right = [], []
    for line in lines:
        a0, a1 = line[:, :HALF], line[:, HALF:]
        before = jnp.where(row == 0, 0.0, pltpu.roll(a1.astype(F32), 1, 0)).astype(BF16)
        after = jnp.where(
            row == segments - 1, 0.0, pltpu.roll(a0.astype(F32), segments - 1, 0)
        ).astype(BF16)
        left.append([before, a0, a1])
        right.append([a0, a1, after])
    stacked = []
    for yp in range(height // 2):
        for side in (left, right):
            stacked.append(
                jnp.concatenate(
                    [tile for y in range(2 * yp, 2 * yp + KH + 1) for tile in side[y]], axis=1
                )
            )
    wide = 3 * HALF
    total = jnp.dot(
        jnp.concatenate(stacked, axis=0),
        weight_ref[PAD * wide : (PAD + KH + 1) * wide],
        preferred_element_type=F32,
    )
    bias = bias_row(bias_ref[...])
    tiles, _, _, per, _ = out_ref.shape
    for yp in range(height // 2):
        for h in range(2):
            start = (yp * 2 + h) * segments
            for yo in range(2):
                y = 2 * yp + yo
                part = total[start : start + segments, yo * HALF : (yo + 1) * HALF]
                center = lines[y + 3][:, h * HALF : (h + 1) * HALF].astype(F32)
                value = (center + gelu(part + bias)).astype(BF16)
                out_ref[:, 0, y, :, h * HALF : (h + 1) * HALF] = value.reshape(tiles, per, HALF)


def horizontal(own, low, high, weight, bias, tiles):
    height, levels, segments, _ = own.shape
    direct = (segments // tiles) % 16 == 0
    parts = tiles if direct else 1
    per = segments // parts
    line = lambda n: pl.BlockSpec((n, 1, segments, SL), lambda z: (0, z, 0, 0))
    out = pl.pallas_call(
        horizontal_kernel,
        grid=(levels,),
        in_specs=[line(height), line(3), line(3), whole(weight.shape), whole(bias.shape)],
        out_specs=pl.BlockSpec((parts, 1, height, per, SL), lambda z: (0, z, 0, 0, 0)),
        out_shape=jax.ShapeDtypeStruct((parts, levels, height, per, SL), BF16),
        compiler_params=params(),
        cost_estimate=cost(
            2 * levels * height * segments * weight.shape[0] * SL // 2, 4 * 10**6
        ),
    )(own, low, high, weight, bias)
    if not direct:
        out = out.reshape(levels, height, tiles, segments // tiles, SL)
        out = jnp.transpose(out, (2, 0, 1, 3, 4))
    return out


def line_sides(line, ahead, behind):
    count = line.shape[0]
    a0, a1 = line[:, :HALF], line[:, HALF:]
    before = jnp.concatenate([ahead, a1.astype(F32)], axis=0)
    before = pltpu.roll(before, 1, 0)[16:].astype(BF16)
    after = jnp.concatenate([a0.astype(F32), behind], axis=0)
    after = pltpu.roll(after, count + 15, 0)[:count].astype(BF16)
    return [before, a0, a1], [a0, a1, after]


def halo_weight(weight_ref, first, yp):
    wide = 3 * HALF
    at = pl.multiple_of((first - 2 * yp + PAD) * wide, wide)
    return weight_ref[pl.ds(at, 3 * wide)]


def early_kernel(ids_ref, own_ref, pair_ref, weight_ref, out_ref):
    height, levels, segments, _ = own_ref.shape
    wide = 3 * HALF
    zero = jnp.zeros((16, HALF), F32)
    own, pair = [], []
    for z in range(levels):
        for rows, ref in ((own, own_ref), (pair, pair_ref)):
            sides = [line_sides(ref[y, z], zero, zero) for y in range(ref.shape[0])]
            for h in range(2):
                rows.append(jnp.concatenate([tile for side in sides for tile in side[h]], axis=1))
    own = jnp.concatenate(own, axis=0)
    pair = jnp.concatenate(pair, axis=0)
    first = (1 - ids_ref[1] % 2) * (height + 3)
    for yp in range(height // 2):
        at = (3 - 2 * yp + PAD) * wide
        total = jnp.dot(own, weight_ref[at : at + height * wide], preferred_element_type=F32)
        total += jnp.dot(pair, halo_weight(weight_ref, first, yp), preferred_element_type=F32)
        out_ref[yp] = total.reshape(levels, 2, segments, SL)


def early_horizontal(ids, own, pair, weight):
    height, levels, segments, _ = own.shape
    full = pl.BlockSpec(memory_space=pltpu.VMEM)
    return pl.pallas_call(
        early_kernel,
        in_specs=[pl.BlockSpec(memory_space=pltpu.SMEM)] + [full] * 3,
        out_specs=full,
        out_shape=jax.ShapeDtypeStruct((height // 2, levels, 2, segments, SL), F32),
        compiler_params=params(),
        cost_estimate=cost(1000, 1000),
    )(ids, own, pair, weight)


def half_kernel(tiles, is_near, ids_ref, own_ref, cross_ref, early_ref, *rest):
    weight_ref, bias_ref = rest[:2]
    rest, done = rest[2:-1], rest[-1]
    extra_refs, out_refs = rest[:-tiles], rest[-tiles:]
    height, levels, segments, _ = own_ref.shape
    size = segments // 2
    near = ids_ref[0] // tiles
    start = pl.multiple_of((near if is_near else 1 - near) * size, size)
    per = size // tiles
    ahead = pl.multiple_of(jnp.maximum(start - 16, 0), 16)
    behind = pl.multiple_of(jnp.minimum(start + size, segments - 16), 16)
    has_ahead = jnp.where(start > 0, 1.0, 0.0)
    has_behind = jnp.where(start + size < segments, 1.0, 0.0)
    bias = bias_row(bias_ref[...])
    cross = []
    for z in range(levels):
        sides = []
        for y in range(3):
            sides.append(
                line_sides(
                    cross_ref[y, z, pl.ds(start, size)],
                    cross_ref[y, z, pl.ds(ahead, 16), HALF:].astype(F32) * has_ahead,
                    cross_ref[y, z, pl.ds(behind, 16), :HALF].astype(F32) * has_behind,
                )
            )
        for h in range(2):
            cross.append(jnp.concatenate([tile for side in sides for tile in side[h]], axis=1))
    cross = jnp.concatenate(cross, axis=0)
    first = ids_ref[1] % 2 * (height + 3)
    for yp in range(height // 2):
        total = jnp.dot(cross, halo_weight(weight_ref, first, yp), preferred_element_type=F32)
        for z in range(levels):
            for h in range(2):
                row = (z * 2 + h) * size
                part = total[row : row + size] + early_ref[yp, z, h, pl.ds(start, size)]
                for yo in range(2):
                    y = 2 * yp + yo
                    center = own_ref[y, z, pl.ds(start, size), h * HALF : (h + 1) * HALF]
                    value = gelu(part[:, yo * HALF : (yo + 1) * HALF] + bias)
                    value = (center.astype(F32) + value).astype(BF16)
                    at = ((z // 2 * 2 + h) * height + y) * per
                    lane = z % 2 * HALF
                    done[:, at : at + per, lane : lane + HALF] = value.reshape(tiles, per, HALF)
    rows = levels * height * per
    for slot, out_ref in enumerate(out_refs):
        tile = ids_ref[0] % tiles ^ slot
        out_ref[:rows] = done[tile]
        for n, extra_ref in enumerate(extra_refs):
            out_ref[rows:, n * HALF : (n + 1) * HALF] = extra_ref[tile]


def half_horizontal(ids, own, cross, early, weight, bias, tiles, is_near, extra=()):
    height, levels, segments, _ = own.shape
    per = segments // (2 * tiles)
    rows = levels * height * per
    full = pl.BlockSpec(memory_space=pltpu.VMEM)
    shape = (rows + (PACK if extra else 0), SL)
    return pl.pallas_call(
        functools.partial(half_kernel, tiles, is_near),
        in_specs=[pl.BlockSpec(memory_space=pltpu.SMEM)] + [full] * (5 + len(extra)),
        out_specs=[full] * tiles,
        out_shape=[jax.ShapeDtypeStruct(shape, BF16)] * tiles,
        scratch_shapes=[pltpu.VMEM((tiles, rows, SL), BF16)],
        compiler_params=params(),
        cost_estimate=cost(1000, 1000),
    )(ids, own, cross, early, weight, bias, *extra)


def bucket_kernel(ids_ref, rows_ref, owner_ref, cells_ref, *rest):
    out_refs, held = rest[:-1], rest[-1]
    count = rows_ref.shape[1]
    tiles, _, cap = held.shape
    owner, cells = owner_ref[...], cells_ref[...]
    row = lax.broadcasted_iota(jnp.int32, (count, count), 0)
    column = lax.broadcasted_iota(jnp.int32, (count, count), 1)
    before = (row < column).astype(BF16)
    named = (lax.broadcasted_iota(jnp.int32, (tiles, count), 0) == owner).astype(F32)
    rank = jnp.dot(named.astype(BF16), before, preferred_element_type=F32)
    rank = jnp.sum(rank * named, axis=0, keepdims=True).astype(jnp.int32)
    slot = owner * cap + rank
    chosen = lax.broadcasted_iota(jnp.int32, (tiles * cap, count), 0) == slot
    coarse = (cells // HALF).astype(F32)
    fine = (cells % HALF).astype(F32)
    index = lax.broadcasted_iota(jnp.int32, (PACK - C, count), 0)
    places = jnp.where(index == 0, coarse, jnp.where(index == 1, fine, 0.0)).astype(BF16)
    payload = jnp.concatenate([rows_ref[...], places], axis=0)
    out = lax.dot_general(
        payload, chosen.astype(BF16), NT, preferred_element_type=F32
    ).astype(BF16)
    if cap % HALF == 0:
        for t in range(tiles):
            held[t] = out[:, t * cap : (t + 1) * cap]
    else:
        held[...] = jnp.swapaxes(out.reshape(PACK, tiles, cap), 0, 1)
    size = tiles // len(out_refs)
    for n, out_ref in enumerate(out_refs):
        out_ref[...] = held[pl.ds((ids_ref[0] // size ^ n) * size, size)]


def bucket(ids, exhaust, owner, cells, tiles):
    count = exhaust.shape[0]
    cap = 2 * count // tiles
    full = pl.BlockSpec(memory_space=pltpu.VMEM)
    return pl.pallas_call(
        bucket_kernel,
        in_specs=[pl.BlockSpec(memory_space=pltpu.SMEM)] + [full] * 3,
        out_specs=[full],
        out_shape=[jax.ShapeDtypeStruct((tiles, PACK, cap), BF16)],
        scratch_shapes=[pltpu.VMEM((tiles, PACK, cap), BF16)],
        compiler_params=params(),
        cost_estimate=cost(1000, 1000),
    )(ids, exhaust.T, owner.reshape(1, count), cells.reshape(1, count))


def source_kernel(tiles, rows, ids_ref, *refs):
    got_refs, out_ref = refs[:-1], refs[-1]
    places = out_ref.shape[0]
    pairs = places // (2 * rows)
    got = jnp.concatenate([ref[ref.shape[0] - PACK :] for ref in got_refs], axis=1)
    slots = got.shape[1]
    cells = (got[C : C + 1].astype(F32) * HALF + got[C + 1 : C + 2].astype(F32)).astype(jnp.int32)
    x, row, level = cells % SEG, cells // SEG % rows, cells // (SEG * rows)
    pair = turned_index(ids_ref, tiles, level // 2, pairs)
    place = (pair * 2 + x // (SEG // 2)) * rows + row
    within = level % 2 * (SEG // 2) + x % (SEG // 2)
    lane = lax.broadcasted_iota(jnp.int32, (SL, slots), 0) // C
    spread = jnp.where(lane == within, jnp.concatenate([got[:C]] * SEG, axis=0).astype(F32), 0.0)
    index = lax.broadcasted_iota(jnp.int32, (places, slots), 0)
    chosen = (index == place).astype(BF16)
    out_ref[...] = lax.dot_general(chosen, spread.astype(BF16), NT, preferred_element_type=F32)


def make_source(ids, got, places, rows, tiles):
    full = pl.BlockSpec(memory_space=pltpu.VMEM)
    return pl.pallas_call(
        functools.partial(source_kernel, tiles, rows),
        in_specs=[pl.BlockSpec(memory_space=pltpu.SMEM)] + [full] * len(got),
        out_specs=full,
        out_shape=jax.ShapeDtypeStruct((places, SL), F32),
        compiler_params=params(),
        cost_estimate=cost(1000, 1000),
    )(ids, *got)


def prepare_kernel(ids_ref, depth_ref, point_ref, rows_ref, owner_ref, cells_ref, *rest):
    across_ref, close_ref, far_ref, held = rest
    bucket_kernel(ids_ref, rows_ref, owner_ref, cells_ref, close_ref, far_ref, held)
    across_kernel(depth_ref, point_ref, across_ref)


def prepare(ids, depth_kernel, point_weight, exhaust, owner, cells, tiles):
    count = exhaust.shape[0]
    cap = 2 * count // tiles
    full = pl.BlockSpec(memory_space=pltpu.VMEM)
    block = jax.ShapeDtypeStruct((tiles // 2, PACK, cap), BF16)
    return pl.pallas_call(
        prepare_kernel,
        in_specs=[pl.BlockSpec(memory_space=pltpu.SMEM)] + [full] * 5,
        out_specs=[full] * 3,
        out_shape=[jax.ShapeDtypeStruct(((KH + 1 + 2 * PAD) * 3 * HALF, SL), BF16), block, block],
        scratch_shapes=[pltpu.VMEM((tiles, PACK, cap), BF16)],
        compiler_params=params(),
        cost_estimate=cost(1000, 1000),
    )(
        ids,
        depth_kernel,
        point_weight,
        exhaust.T,
        owner.reshape(1, count),
        cells.reshape(1, count),
    )


def chunks(first, last, size):
    return [(n, min(n + size, last)) for n in range(first, last, size)]


def layer_step(held, base, first, last, block, weight, bias):
    taps = [held[(first - base + k) * block : (last - base + k) * block] for k in range(TAPS)]
    total = jnp.dot(jnp.concatenate(taps, axis=1), weight, preferred_element_type=F32)
    center = held[(first - base + 2) * block : (last - base + 2) * block].astype(F32)
    return center + gelu(total + bias)


def put_group(out_ref, value, height, block, at_of):
    rows = block // 2
    count = 256 // block
    across = rows // height
    swap = swap_matrix(2 * count * height, across)
    for g in range(value.shape[0] // (count * block)):
        pieces = []
        for n in range(count):
            start = (g * count + n) * block
            for j in range(2):
                lane = slice(j * HALF, (j + 1) * HALF)
                pieces.append(
                    jnp.concatenate(
                        [value[start : start + rows, lane], value[start + rows : start + block, lane]],
                        axis=1,
                    )
                )
        turned = jnp.dot(
            swap, jnp.concatenate(pieces, axis=0), preferred_element_type=F32
        ).astype(BF16)
        size = 2 * height
        for n in range(count):
            at = at_of(g * count + n) * 2
            for s in range(across):
                start = (s * count + n) * size
                out_ref[pl.ds(at, 2), :, s * SL : (s + 1) * SL] = turned[
                    start : start + size
                ].reshape(2, height, SL)


def near_kernel(tiles, height, ids_ref, *refs):
    piece_refs = refs[:tiles]
    source_ref, weight_ref, bias_ref, out_ref, kept_ref, later_ref, held, step = refs[tiles:]
    pairs = out_ref.shape[0] // 2 + 4
    block = kept_ref.shape[0] // 4
    bias = [bias_row(bias_ref[n : n + 1]) for n in range(2)]
    bias = [jnp.concatenate([row, row], axis=1) for row in bias]
    held[: 2 * block] = jnp.zeros((2 * block, SL), BF16)
    step[: 2 * block] = jnp.zeros((2 * block, SL), BF16)
    per = pairs // tiles
    for d, piece_ref in enumerate(piece_refs):
        for n in range(per):
            number = (ids_ref[0] % tiles ^ d) * per + n
            at = turned_index(ids_ref, tiles, number, pairs) + 2
            held[pl.ds(pl.multiple_of(at * block, block), block)] = piece_ref[
                n * block : (n + 1) * block
            ]
    kept_ref[...] = held[(pairs - 2) * block : (pairs + 2) * block]
    for first, last in chunks(0, pairs - 2, 4):
        value = layer_step(held, 0, first, last, block, weight_ref[0], bias[0])
        step[(first + 2) * block : (last + 2) * block] = value.astype(BF16)
    later_ref[...] = step[(pairs - 4) * block : pairs * block]
    for first, last in chunks(0, pairs - 4, 4):
        value = layer_step(step, 0, first, last, block, weight_ref[1], bias[1])
        value = (value + source_ref[first * block : last * block]).astype(BF16)
        put_group(
            out_ref,
            value,
            height,
            block,
            lambda n: turned_index(ids_ref, tiles, first + n, pairs - 4),
        )


def far_kernel(tiles, height, ids_ref, *refs):
    piece_refs = refs[:tiles]
    early_ref, kept_ref, later_ref, source_ref, weight_ref, bias_ref, out_ref, held, step = refs[tiles:]
    pairs = out_ref.shape[0] // 2
    half = pairs // 2
    block = kept_ref.shape[0] // 4
    bias = [bias_row(bias_ref[n : n + 1]) for n in range(2)]
    bias = [jnp.concatenate([row, row], axis=1) for row in bias]
    held[: 4 * block] = kept_ref[...]
    held[(half + 4) * block :] = jnp.zeros((2 * block, SL), BF16)
    step[: 4 * block] = later_ref[...]
    step[(half + 6) * block :] = jnp.zeros((2 * block, SL), BF16)
    per = half // tiles
    for d, piece_ref in enumerate(piece_refs):
        for n in range(per):
            number = (ids_ref[0] % tiles ^ d) * per + n
            at = turned_index(ids_ref, tiles, number, half) + 4
            held[pl.ds(pl.multiple_of(at * block, block), block)] = piece_ref[
                n * block : (n + 1) * block
            ]
    for first, last in chunks(half - 2, pairs, 5):
        value = layer_step(held, half - 2, first, last, block, weight_ref[0], bias[0])
        step[(first - half + 6) * block : (last - half + 6) * block] = value.astype(BF16)
    early = early_ref.shape[0]
    out_ref[pl.ds(turned_index(ids_ref, tiles, 0, 2 * pairs // early) * early, early)] = early_ref[...]
    for first, last in chunks(half - 4, pairs, 4):
        value = layer_step(step, half - 4, first, last, block, weight_ref[1], bias[1])
        value = (value + source_ref[first * block : last * block]).astype(BF16)
        put_group(
            out_ref, value, height, block, lambda n: turned_index(ids_ref, tiles, first + n, pairs)
        )


def whole_kernel(height, ids_ref, piece_ref, source_ref, weight_ref, bias_ref, out_ref, held, step):
    levels = out_ref.shape[0]
    pairs = levels // 2
    rows = piece_ref.shape[0] // levels
    block = 2 * rows
    bias = [bias_row(bias_ref[n : n + 1]) for n in range(2)]
    bias = [jnp.concatenate([row, row], axis=1) for row in bias]
    for buffer in (held, step):
        buffer[: 2 * block] = jnp.zeros((2 * block, SL), BF16)
        buffer[(pairs + 2) * block :] = jnp.zeros((2 * block, SL), BF16)
    for z in range(levels):
        for h in range(2):
            start = (z // 2 + 2) * block + h * rows
            held[start : start + rows, z % 2 * HALF : (z % 2 + 1) * HALF] = piece_ref[
                z * rows : (z + 1) * rows, h * HALF : (h + 1) * HALF
            ]
    value = layer_step(held, 0, 0, pairs, block, weight_ref[0], bias[0])
    step[2 * block : (pairs + 2) * block] = value.astype(BF16)
    value = layer_step(step, 0, 0, pairs, block, weight_ref[1], bias[1])
    value = (value + source_ref[...]).astype(BF16)
    put_group(out_ref, value, height, block, lambda n: n)


def vertical(ids, close, far, source, weight, bias, levels, height, tiles):
    full = pl.BlockSpec(memory_space=pltpu.VMEM)
    smem = pl.BlockSpec(memory_space=pltpu.SMEM)
    rows = source.shape[0] // levels
    block = 2 * rows
    pairs = levels // 2
    lanes = rows // height * SL
    buffer = lambda count: pltpu.VMEM((count * block, SL), BF16)
    array = lambda count: jax.ShapeDtypeStruct((count * block, SL), BF16)
    result = lambda count: jax.ShapeDtypeStruct((count, height, lanes), BF16)
    if not far:
        return pl.pallas_call(
            functools.partial(whole_kernel, height),
            in_specs=[smem] + [full] * 4,
            out_specs=full,
            out_shape=result(levels),
            scratch_shapes=[buffer(pairs + 4)] * 2,
            compiler_params=params(),
            cost_estimate=cost(1000, 1000),
        )(ids, *close, source, weight, bias)
    half = pairs // 2
    early, kept, later = pl.pallas_call(
        functools.partial(near_kernel, tiles, height),
        in_specs=[smem] + [full] * (len(close) + 3),
        out_specs=[full] * 3,
        out_shape=[result(2 * (half - 4)), array(4), array(4)],
        scratch_shapes=[buffer(half + 2), buffer(half)],
        compiler_params=params(),
        cost_estimate=cost(1000, 1000),
    )(ids, *close, source, weight, bias)
    return pl.pallas_call(
        functools.partial(far_kernel, tiles, height),
        in_specs=[smem] + [full] * (len(far) + 6),
        out_specs=full,
        out_shape=result(levels),
        scratch_shapes=[buffer(half + 6), buffer(half + 8)],
        compiler_params=params(),
        cost_estimate=cost(1000, 1000),
    )(ids, *far, early, kept, later, source, weight, bias)


def exchange(block, distance):
    count = lax.axis_size("cols")
    return lax.ppermute(block, "cols", [(i, i ^ distance) for i in range(count)])


def body(
    field, depth_kernel, point_weight, point_bias, vert_weight, vert_bias, exhaust, owner, cells
):
    columns, bands = lax.axis_size("cols"), lax.axis_size("rows")
    forward = [(i, i + 1) for i in range(bands - 1)]
    backward = [(target, source) for source, target in forward]
    levels, height, lanes = field.shape
    segments = lanes // SL
    per = segments // columns
    ids = jnp.stack([lax.axis_index("cols"), lax.axis_index("rows")]).astype(jnp.int32)
    bias = point_bias.reshape(1, C)
    if per % 16 == 0 and columns % 2 == 0 and bands % 2 == 0 and 256 % (levels * height) == 0:
        tiles = columns // 2
        own, cross, pair = to_segments(ids, field)
        inside = [(i, i ^ 1) for i in range(bands)]
        beyond = [(i, i + 1 if i % 2 else i - 1) for i in range(1, bands - 1)]
        cross = lax.ppermute(cross, "rows", beyond)
        pair = lax.ppermute(pair, "rows", inside)
        across, close_rows, far_rows = prepare(
            ids, depth_kernel, point_weight, exhaust, owner, cells, columns
        )
        relayed = exchange(far_rows, tiles)
        early = early_horizontal(ids, own, pair, across)
        far = half_horizontal(ids, own, cross, early, across, bias, tiles, False)
        ids_near, _ = lax.optimization_barrier((ids, far[0]))
        far = [exchange(block, tiles + slot) for slot, block in enumerate(far)]
        close = half_horizontal(
            ids_near, own, cross, early, across, bias, tiles, True, (close_rows, relayed)
        )
        close = [exchange(block, slot) if slot else block for slot, block in enumerate(close)]
        got = close
    else:
        tiles, far = 0, []
        (sent,) = bucket(ids, exhaust, owner, cells, columns)
        got = lax.all_to_all(sent, "cols", split_axis=0, concat_axis=0, tiled=True)
        got = [jnp.transpose(got, (1, 0, 2)).reshape(PACK, -1)]
        own = jnp.transpose(field.reshape(levels, height, segments, SL), (1, 0, 2, 3))
        low = lax.ppermute(own[height - 3 :], "rows", forward)
        high = lax.ppermute(own[:3], "rows", backward)
        across = across_weights(depth_kernel, point_weight)
        mixed = horizontal(own, low, high, across, bias, columns)
        mixed = mixed.reshape(columns, levels, -1, SL)
        taken = lax.all_to_all(mixed, "cols", split_axis=0, concat_axis=0, tiled=True)
        close = [taken.reshape(-1, SL)]
    depth = columns * levels
    source = make_source(ids, got, depth * height * per, height * per, tiles)
    up = up_weights(ids, vert_weight, tiles)
    return vertical(ids, close, far, source, up, vert_bias, depth, height, tiles)


def solution(mesh):
    placed = (
        P("cols", "rows", None),
        P(),
        P(),
        P(),
        P(),
        P(),
        P(("rows", "cols"), None),
        P(("rows", "cols"), None),
        P(("rows", "cols")),
    )
    return jax.shard_map(
        body, mesh=mesh, in_specs=placed, out_specs=P(None, "rows", "cols"), check_vma=False
    )
```

time: 57.8 us -> 54.6 us (0.945)
  waiting for transfers between devices: 17.3 us -> 14.2 us
  starting transfers between devices: 17 us -> 14 us
  Pallas kernels: 18.1 us -> 21 us
    ppermute x2, waiting for transfers between devices: 4.38 us -> 0.01 us  [the longest x1 0.01 us: body(): pair = lax.ppermute(pair, 'rows', inside)]
    pallas_call x8 -> x9, Pallas kernels: 18.1 us -> 21 us  [the longest x1 5.38 us: vertical(): pl.pallas_call(functools.partial(far_kernel, tiles, height), in_specs=[sm...]
    ppermute x2, starting transfers between devices: 5.59 us -> 3.77 us  [the longest x1 3.02 us: body(): cross = lax.ppermute(cross, 'rows', beyond)]
    ppermute x8, waiting for transfers between devices: 12.9 us -> 14.2 us  [exchange(): lax.ppermute(block, 'cols', [(i, i ^ distance) for i in range(count)])]
    ppermute x8, starting transfers between devices: 11.4 us -> 10.2 us  [exchange(): lax.ppermute(block, 'cols', [(i, i ^ distance) for i in range(count)])]
  transfers between devices with their start and end apart: 10 -> 10, of which waited for: 7 -> 5; matrix products, arithmetic and copies ran while one was open for 0% -> 0% of each run, Pallas kernels for 12% -> 23%
where the time goes in v3:
time: 54.6 us; the launch traced here: 54.2 us
  Pallas kernels  21 us (38%)
  waiting for transfers between devices  14.2 us (26%)
  starting transfers between devices  14 us (26%)
  local copies, waits for them, and re-layouts  4.8 us (9%)
    ppermute x8, waiting for transfers between devices, exchange(): lax.ppermute(block, 'cols', [(i, i ^ distance) for i in range(count)])  14.2 us
    ppermute x8, starting transfers between devices, exchange(): lax.ppermute(block, 'cols', [(i, i ^ distance) for i in range(count)])  10.2 us
    pallas_call x1, Pallas kernels, vertical(): pl.pallas_call(functools.partial(far_kernel, tiles, height), in_specs=[sm...  5.38 us
    unnamed x18, local copies, waits for them, and re-layouts  4.8 us
    pallas_call x1, Pallas kernels, early_horizontal(): pl.pallas_call(early_kernel, in_specs=[pl.BlockSpec(memory_space=pltpu.SM...  3.7 us
    pallas_call x2, Pallas kernels, half_horizontal(): pl.pallas_call(functools.partial(half_kernel, tiles, is_near), in_specs=[...  3.6 us
    ppermute x1, starting transfers between devices, body(): cross = lax.ppermute(cross, 'rows', beyond)  3.02 us
    pallas_call x1, Pallas kernels, vertical(): pl.pallas_call(functools.partial(near_kernel, tiles, height), in_specs=[s...  2.41 us
  transfers between devices with their start and end apart: 10, of which 5 were waited for; matrix products, arithmetic and copies ran while one was open for 0% of the time, Pallas kernels for 23%

profile of v3, /device:TPU:9, one launch (start us, length us, event | category | flops | bytes accessed | tf_op | source)
XLA Modules:
  0.0 54.2 jit_solution(16869102680023445378)
XLA Ops:
  0.0 0.1 pad_add_fusion.ids_ref
  0.1 0.0 copy-start
  0.1 1.2 %copy-done = bf16[4,4,32768]{2,1,0:T(4,128)(2,1)S(1)} copy-done((bf16[4,4,32768]{2,1,0:T(4,128)(2,1)S(1)}, bf16[4,4,32768]{2,1,0:T(4,128)(2,1)}, u32[]{:S(2)}) %copy-start) | copy-done | bytes 1048600
  1.3 1.1 %shard_map.91 = (bf16[4,4,128,256]{3,2,1,0:T(8,128)(2,1)S(1)}, bf16[3,4,128,256]{3,2,1,0:T(8,128)(2,1)S(1)}, bf16[3,4,128,256]{3,2,1,0:T(8,128)(2,1)S(1)}) custom-call(s32[2]{0:T(128)S(1)} %pad_add_fusion.ids_ref, bf16[4,4,32768]{2,1,0:T(4,128)(2,1)S(1)} %copy-done), custom_call_target="tpu_custom_call" | custom-call | flops 1000 | bytes 1000 | tf_op jit(solution)/shard_map/pallas_call | solution.py:73
  2.4 0.8 %collective-permute-start.1 = (bf16[3,4,128,256]{3,2,1,0:T(8,128)(2,1)S(1)}, bf16[3,4,128,256]{3,2,1,0:T(8,128)(2,1)S(1)}, u32[]{:S(2)}, u32[]{:S(2)}) collective-permute-start(bf16[3,4,128,256]{3,2,1,0:T(8,128)(2,1)S(1)} %get-tuple-element.25), channel_id=1, source_target_pairs={{0,8},{8,0},{16,24},{24,16},{1,9},{9,1},{17,25},{25,17},{2,10},{10... | collective-permute-start | bytes 2359304 | tf_op jit(solution)/shard_map/ppermute | solution.py:642
  3.2 3.0 %collective-permute-start = (bf16[3,4,128,256]{3,2,1,0:T(8,128)(2,1)S(1)}, bf16[3,4,128,256]{3,2,1,0:T(8,128)(2,1)S(1)}, u32[]{:S(2)}, u32[]{:S(2)}) collective-permute-start(bf16[3,4,128,256]{3,2,1,0:T(8,128)(2,1)S(1)} %get-tuple-element.24), channel_id=1, source_target_pairs={{8,16},{16,8},{9,17},{17,9},{10,18},{18,10},{11,19},{19,11},{12,20... | collective-permute-start | bytes 2359304 | tf_op jit(solution)/shard_map/ppermute | solution.py:641
  6.2 0.0 copy-start.2
  6.2 0.7 %copy-done.2 = bf16[512,32]{0,1:T(8,128)(2,1)S(1)} copy-done((bf16[512,32]{0,1:T(8,128)(2,1)S(1)}, bf16[512,32]{0,1:T(8,128)(2,1)}, u32[]{:S(2)}) %copy-start.2) | copy-done | bytes 32792
  7.0 0.0 copy-start.3
  7.0 0.7 %copy-done.3 = f32[7,7,32]{2,1,0:T(8,128)S(1)} copy-done((f32[7,7,32]{2,1,0:T(8,128)S(1)}, f32[7,7,32]{2,1,0:T(8,128)}, u32[]{:S(2)}) %copy-start.3) | copy-done | bytes 6296
  7.7 0.0 copy-start.4
  7.7 0.7 %copy-done.4 = bf16[32,32]{1,0:T(8,128)(2,1)S(1)} copy-done((bf16[32,32]{1,0:T(8,128)(2,1)S(1)}, bf16[32,32]{1,0:T(8,128)(2,1)}, u32[]{:S(2)}) %copy-start.4) | copy-done | bytes 2072
  8.4 0.0 copy-start.6
  8.4 0.7 %copy-done.6 = s32[512,1]{0,1:T(1,128)S(1)} copy-done((s32[512,1]{0,1:T(1,128)S(1)}, s32[512,1]{0,1:T(1,128)}, u32[]{:S(2)}) %copy-start.6) | copy-done | bytes 2072
  9.1 0.0 copy-start.7
  9.1 0.7 %copy-done.7 = s32[512]{0:T(512)S(1)} copy-done((s32[512]{0:T(512)S(1)}, s32[512]{0:T(512)}, u32[]{:S(2)}) %copy-start.7) | copy-done | bytes 2072
  9.8 1.5 %shard_map.92 = (bf16[4608,256]{1,0:T(8,128)(2,1)S(1)}, bf16[4,48,128]{2,1,0:T(8,128)(2,1)S(1)}, bf16[4,48,128]{2,1,0:T(8,128)(2,1)S(1)}) custom-call(s32[2]{0:T(128)S(1)} %pad_add_fusion.ids_ref, f32[7,7,32]{2,1,0:T(8,128)S(1)} %copy-done.3, bf16[32,32]{1,0:T(8,128)(2,1)S(1)} %copy-done.4, bf16[32,512]{1,0:T(8,128)(2,1)S(1)} %bitcast.8, ...), custom_call_target="tpu_custom_call" | custom-call | flops 1000 | bytes 1000 | tf_op jit(solution)/shard_map/pallas_call | solution.py:430
  11.3 2.4 %collective-permute-start.6 = (bf16[4,48,128]{2,1,0:T(8,128)(2,1)S(1)}, bf16[4,48,128]{2,1,0:T(8,128)(2,1)S(1)}, u32[]{:S(2)}, u32[]{:S(2)}) collective-permute-start(bf16[4,48,128]{2,1,0:T(8,128)(2,1)S(1)} %get-tuple-element.33), channel_id=1, source_target_pairs={{0,4},{1,5},{2,6},{3,7},{4,0},{5,1},{6,2},{7,3},{8,12},{9,13},{10,... | collective-permute-start | bytes 147464 | tf_op jit(solution)/shard_map/ppermute | solution.py:622
  13.7 0.0 collective-permute-done.1.pair_ref
  13.7 0.0 copy-start.8
  13.7 3.7 %shard_map.93.early_ref = f32[2,4,2,128,256]{4,3,2,1,0:T(8,128)S(1)} custom-call(s32[2]{0:T(128)S(1)} %pad_add_fusion.ids_ref, bf16[4,4,128,256]{3,2,1,0:T(8,128)(2,1)S(1)} %get-tuple-element.23.own_ref, bf16[3,4,128,256]{3,2,1,0:T(8,128)(2,1)S(1)} %collective-permute-done.1.pair_ref, bf16[4608,256]{1,0:T(8,128)(2,1)S(1)} %get-tuple-element.26.weight_ref.rest_0_), custom_call_target="tpu_custom_call" | custom-call | flops 1000 | bytes 1000 | tf_op jit(solution)/shard_map/pallas_call | solution.py:265
  17.4 0.0 collective-permute-done.cross_ref
  17.4 0.0 copy-done.8
  17.4 1.8 %shard_map.94 = (bf16[256,256]{1,0:T(8,128)(2,1)S(1)}, bf16[256,256]{1,0:T(8,128)(2,1)S(1)}, bf16[256,256]{1,0:T(8,128)(2,1)S(1)}, bf16[256,256]{1,0:T(8,128)(2,1)S(1)}) custom-call(s32[2]{0:T(128)S(1)} %pad_add_fusion.ids_ref, bf16[4,4,128,256]{3,2,1,0:T(8,128)(2,1)S(1)} %get-tuple-element.23.own_ref, ...), custom_call_target="tpu_custom_call" | custom-call | flops 1000 | bytes 1000 | tf_op jit(solution)/shard_map/pallas_call | solution.py:332
  19.2 0.0 collective-permute-done.6.rest_3_
  19.2 0.0 copy-start.1
  19.2 1.8 %shard_map.95 = (bf16[304,256]{1,0:T(8,128)(2,1)S(1)}, bf16[304,256]{1,0:T(8,128)(2,1)S(1)}, bf16[304,256]{1,0:T(8,128)(2,1)S(1)}, bf16[304,256]{1,0:T(8,128)(2,1)S(1)}) custom-call(s32[2]{0:T(128)S(1)} %pad_add_fusion.ids_ref, bf16[4,4,128,256]{3,2,1,0:T(8,128)(2,1)S(1)} %get-tuple-element.23.own_ref, ...), custom_call_target="tpu_custom_call" | custom-call | flops 1000 | bytes 1000 | tf_op jit(solution)/shard_map/pallas_call | solution.py:332
  21.0 0.0 copy-start.5
  21.0 1.3 %collective-permute-start.7 = (bf16[304,256]{1,0:T(8,128)(2,1)S(1)}, bf16[304,256]{1,0:T(8,128)(2,1)S(1)}, u32[]{:S(2)}, u32[]{:S(2)}) collective-permute-start(bf16[304,256]{1,0:T(8,128)(2,1)S(1)} %get-tuple-element.35), channel_id=1, source_target_pairs={{0,1},{1,0},{2,3},{3,2},{4,5},{5,4},{6,7},{7,6},{8,9},{9,8},{10,11... | collective-permute-start | bytes 466952 | tf_op jit(solution)/shard_map/ppermute | solution.py:622
  22.3 0.2 collective-permute-start.8
  22.5 1.3 %collective-permute-start.9 = (bf16[304,256]{1,0:T(8,128)(2,1)S(1)}, bf16[304,256]{1,0:T(8,128)(2,1)S(1)}, u32[]{:S(2)}, u32[]{:S(2)}) collective-permute-start(bf16[304,256]{1,0:T(8,128)(2,1)S(1)} %get-tuple-element.37), channel_id=1, source_target_pairs={{0,3},{1,2},{2,1},{3,0},{4,7},{5,6},{6,5},{7,4},{8,11},{9,10},{10,... | collective-permute-start | bytes 466952 | tf_op jit(solution)/shard_map/ppermute | solution.py:622
  23.8 1.4 %collective-permute-start.2 = (bf16[256,256]{1,0:T(8,128)(2,1)S(1)}, bf16[256,256]{1,0:T(8,128)(2,1)S(1)}, u32[]{:S(2)}, u32[]{:S(2)}) collective-permute-start(bf16[256,256]{1,0:T(8,128)(2,1)S(1)} %get-tuple-element.27), channel_id=1, source_target_pairs={{0,4},{1,5},{2,6},{3,7},{4,0},{5,1},{6,2},{7,3},{8,12},{9,13},{10,... | collective-permute-start | bytes 393224 | tf_op jit(solution)/shard_map/ppermute | solution.py:622
  25.1 1.9 %collective-permute-start.3 = (bf16[256,256]{1,0:T(8,128)(2,1)S(1)}, bf16[256,256]{1,0:T(8,128)(2,1)S(1)}, u32[]{:S(2)}, u32[]{:S(2)}) collective-permute-start(bf16[256,256]{1,0:T(8,128)(2,1)S(1)} %get-tuple-element.28), channel_id=1, source_target_pairs={{0,5},{1,4},{2,7},{3,6},{4,1},{5,0},{6,3},{7,2},{8,13},{9,12},{10,... | collective-permute-start | bytes 393224 | tf_op jit(solution)/shard_map/ppermute | solution.py:622
  27.1 0.0 collective-permute-done.7.refs_1_
  27.1 0.4 collective-permute-start.4
  27.5 1.2 %collective-permute-done.8.refs_2_ = bf16[304,256]{1,0:T(8,128)(2,1)S(1)} collective-permute-done((bf16[304,256]{1,0:T(8,128)(2,1)S(1)}, bf16[304,256]{1,0:T(8,128)(2,1)S(1)}, u32[]{:S(2)}, u32[]{:S(2)}) %collective-permute-start.8) | collective-permute-done | bytes 155680 | tf_op jit(solution)/shard_map/ppermute | solution.py:622
  28.6 1.4 %collective-permute-start.5 = (bf16[256,256]{1,0:T(8,128)(2,1)S(1)}, bf16[256,256]{1,0:T(8,128)(2,1)S(1)}, u32[]{:S(2)}, u32[]{:S(2)}) collective-permute-start(bf16[256,256]{1,0:T(8,128)(2,1)S(1)} %get-tuple-element.30), channel_id=1, source_target_pairs={{0,7},{1,6},{2,5},{3,4},{4,3},{5,2},{6,1},{7,0},{8,15},{9,14},{10,... | collective-permute-start | bytes 393224 | tf_op jit(solution)/shard_map/ppermute | solution.py:622
  30.1 0.0 copy-done.1
  30.1 1.4 %shard_map.97.refs_5_.refs_8_ = bf16[2,1280,256]{2,1,0:T(8,128)(2,1)S(1)} custom-call(s32[2]{0:T(128)S(1)} %pad_add_fusion.ids_ref, bf16[2,32,288]{2,1,0:T(8,128)(2,1)S(1)} %bitcast.7), custom_call_target="tpu_custom_call" | custom-call | flops 1000 | bytes 1000 | tf_op jit(solution)/shard_map/pallas_call | solution.py:146
  31.5 1.1 %collective-permute-done.9.refs_3_ = bf16[304,256]{1,0:T(8,128)(2,1)S(1)} collective-permute-done((bf16[304,256]{1,0:T(8,128)(2,1)S(1)}, bf16[304,256]{1,0:T(8,128)(2,1)S(1)}, u32[]{:S(2)}, u32[]{:S(2)}) %collective-permute-start.9) | collective-permute-done | bytes 155680 | tf_op jit(solution)/shard_map/ppermute | solution.py:622
  32.6 1.9 %shard_map.96.refs_4_.refs_7_ = f32[2048,256]{1,0:T(8,128)S(1)} custom-call(s32[2]{0:T(128)S(1)} %pad_add_fusion.ids_ref, bf16[304,256]{1,0:T(8,128)(2,1)S(1)} %get-tuple-element.34.refs_0_, bf16[304,256]{1,0:T(8,128)(2,1)S(1)} %collective-permute-done.7.refs_1_, bf16[304,256]{1,0:T(8,128)(2,1)S(1)} %collective-permute-done.8.refs_2_, ...), custom_call_target="tpu_custom_call" | custom-call | flops 1000 | bytes 1000 | tf_op jit(solution)/shard_map/pallas_call | solution.py:409
  34.5 0.0 copy-done.5
  34.5 2.4 %shard_map.98 = (bf16[8,4,4096]{2,1,0:T(4,128)(2,1)S(1)}, bf16[512,256]{1,0:T(8,128)(2,1)S(1)}, bf16[512,256]{1,0:T(8,128)(2,1)S(1)}) custom-call(s32[2]{0:T(128)S(1)} %pad_add_fusion.ids_ref, bf16[304,256]{1,0:T(8,128)(2,1)S(1)} %get-tuple-element.34.refs_0_, bf16[304,256]{1,0:T(8,128)(2,1)S(1)} %collective-permute-done.7.refs_1_, ...), custom_call_target="tpu_custom_call" | custom-call | flops 1000 | bytes 1000 | tf_op jit(solution)/shard_map/pallas_call | solution.py:600
  36.9 0.0 collective-permute-done.2.refs_0_
  36.9 4.5 %collective-permute-done.3.refs_1_ = bf16[256,256]{1,0:T(8,128)(2,1)S(1)} collective-permute-done((bf16[256,256]{1,0:T(8,128)(2,1)S(1)}, bf16[256,256]{1,0:T(8,128)(2,1)S(1)}, u32[]{:S(2)}, u32[]{:S(2)}) %collective-permute-start.3) | collective-permute-done | bytes 131104 | tf_op jit(solution)/shard_map/ppermute | solution.py:622
  41.4 4.6 %collective-permute-done.4.refs_2_ = bf16[256,256]{1,0:T(8,128)(2,1)S(1)} collective-permute-done((bf16[256,256]{1,0:T(8,128)(2,1)S(1)}, bf16[256,256]{1,0:T(8,128)(2,1)S(1)}, u32[]{:S(2)}, u32[]{:S(2)}) %collective-permute-start.4) | collective-permute-done | bytes 131104 | tf_op jit(solution)/shard_map/ppermute | solution.py:622
  46.0 2.8 %collective-permute-done.5.refs_3_ = bf16[256,256]{1,0:T(8,128)(2,1)S(1)} collective-permute-done((bf16[256,256]{1,0:T(8,128)(2,1)S(1)}, bf16[256,256]{1,0:T(8,128)(2,1)S(1)}, u32[]{:S(2)}, u32[]{:S(2)}) %collective-permute-start.5) | collective-permute-done | bytes 131104 | tf_op jit(solution)/shard_map/ppermute | solution.py:622
  48.8 5.4 %shard_map.99 = bf16[32,4,4096]{2,1,0:T(4,128)(2,1)} custom-call(s32[2]{0:T(128)S(1)} %pad_add_fusion.ids_ref, bf16[256,256]{1,0:T(8,128)(2,1)S(1)} %collective-permute-done.2.refs_0_, bf16[256,256]{1,0:T(8,128)(2,1)S(1)} %collective-permute-done.3.refs_1_, bf16[256,256]{1,0:T(8,128)(2,1)S(1)} %collective-permute-done.4.refs_2_, ...), custom_call_target="tpu_custom_call" | custom-call | flops 1000 | bytes 1000 | tf_op jit(solution)/shard_map/pallas_call | solution.py:609
Async XLA Ops:
  0.1 1.2 %copy-start = (bf16[4,4,32768]{2,1,0:T(4,128)(2,1)S(1)}, bf16[4,4,32768]{2,1,0:T(4,128)(2,1)}, u32[]{:S(2)}) copy-start(bf16[4,4,32768]{2,1,0:T(4,128)(2,1)} %field_ref.1) | copy-start | bytes 3145732
  2.4 11.2 %collective-permute-start.1 = (bf16[3,4,128,256]{3,2,1,0:T(8,128)(2,1)S(1)}, bf16[3,4,128,256]{3,2,1,0:T(8,128)(2,1)S(1)}, u32[]{:S(2)}, u32[]{:S(2)}) collective-permute-start(bf16[3,4,128,256]{3,2,1,0:T(8,128)(2,1)S(1)} %get-tuple-element.25), channel_id=1, source_target_pairs={{0,8},{8,0},{16,24},{24,16},{1,9},{9,1},{17,25},{25,17},{2,10},{10... | collective-permute-start | bytes 2359304 | tf_op jit(solution)/shard_map/ppermute | solution.py:642
  3.2 14.2 %collective-permute-start = (bf16[3,4,128,256]{3,2,1,0:T(8,128)(2,1)S(1)}, bf16[3,4,128,256]{3,2,1,0:T(8,128)(2,1)S(1)}, u32[]{:S(2)}, u32[]{:S(2)}) collective-permute-start(bf16[3,4,128,256]{3,2,1,0:T(8,128)(2,1)S(1)} %get-tuple-element.24), channel_id=1, source_target_pairs={{8,16},{16,8},{9,17},{17,9},{10,18},{18,10},{11,19},{19,11},{12,20... | collective-permute-start | bytes 2359304 | tf_op jit(solution)/shard_map/ppermute | solution.py:641
  6.2 0.8 %copy-start.2 = (bf16[512,32]{0,1:T(8,128)(2,1)S(1)}, bf16[512,32]{0,1:T(8,128)(2,1)}, u32[]{:S(2)}) copy-start(bf16[512,32]{0,1:T(8,128)(2,1)} %param.15) | copy-start | bytes 98308
  7.0 0.7 %copy-start.3 = (f32[7,7,32]{2,1,0:T(8,128)S(1)}, f32[7,7,32]{2,1,0:T(8,128)}, u32[]{:S(2)}) copy-start(f32[7,7,32]{2,1,0:T(8,128)} %depth_ref.1) | copy-start | bytes 18820
  7.7 0.7 %copy-start.4 = (bf16[32,32]{1,0:T(8,128)(2,1)S(1)}, bf16[32,32]{1,0:T(8,128)(2,1)}, u32[]{:S(2)}) copy-start(bf16[32,32]{1,0:T(8,128)(2,1)} %point_ref.1) | copy-start | bytes 6148
  8.4 0.7 %copy-start.6 = (s32[512,1]{0,1:T(1,128)S(1)}, s32[512,1]{0,1:T(1,128)}, u32[]{:S(2)}) copy-start(s32[512,1]{0,1:T(1,128)} %param.16) | copy-start | bytes 6148
  9.1 0.7 %copy-start.7 = (s32[512]{0:T(512)S(1)}, s32[512]{0:T(512)}, u32[]{:S(2)}) copy-start(s32[512]{0:T(512)} %param.17) | copy-start | bytes 6148
  11.3 7.9 %collective-permute-start.6 = (bf16[4,48,128]{2,1,0:T(8,128)(2,1)S(1)}, bf16[4,48,128]{2,1,0:T(8,128)(2,1)S(1)}, u32[]{:S(2)}, u32[]{:S(2)}) collective-permute-start(bf16[4,48,128]{2,1,0:T(8,128)(2,1)S(1)} %get-tuple-element.33), channel_id=1, source_target_pairs={{0,4},{1,5},{2,6},{3,7},{4,0},{5,1},{6,2},{7,3},{8,12},{9,13},{10,... | collective-permute-start | bytes 147464 | tf_op jit(solution)/shard_map/ppermute | solution.py:622
  13.7 3.7 %copy-start.8 = (f32[32]{0:T(128)S(1)}, f32[32]{0:T(128)}, u32[]{:S(2)}) copy-start(f32[32]{0:T(128)} %param.12) | copy-start | bytes 388
  19.2 10.9 %copy-start.1 = (bf16[2,288,32]{1,2,0:T(8,128)(2,1)S(1)}, bf16[2,288,32]{1,2,0:T(8,128)(2,1)}, u32[]{:S(2)}) copy-start(bf16[2,288,32]{1,2,0:T(8,128)(2,1)} %param.13) | copy-start | bytes 110596
  21.0 13.4 %copy-start.5 = (f32[2,32]{1,0:T(2,128)S(1)}, f32[2,32]{1,0:T(2,128)}, u32[]{:S(2)}) copy-start(f32[2,32]{1,0:T(2,128)} %refs_9_.1) | copy-start | bytes 772
  21.0 6.0 %collective-permute-start.7 = (bf16[304,256]{1,0:T(8,128)(2,1)S(1)}, bf16[304,256]{1,0:T(8,128)(2,1)S(1)}, u32[]{:S(2)}, u32[]{:S(2)}) collective-permute-start(bf16[304,256]{1,0:T(8,128)(2,1)S(1)} %get-tuple-element.35), channel_id=1, source_target_pairs={{0,1},{1,0},{2,3},{3,2},{4,5},{5,4},{6,7},{7,6},{8,9},{9,8},{10,11... | collective-permute-start | bytes 466952 | tf_op jit(solution)/shard_map/ppermute | solution.py:622
  22.3 6.3 %collective-permute-start.8 = (bf16[304,256]{1,0:T(8,128)(2,1)S(1)}, bf16[304,256]{1,0:T(8,128)(2,1)S(1)}, u32[]{:S(2)}, u32[]{:S(2)}) collective-permute-start(bf16[304,256]{1,0:T(8,128)(2,1)S(1)} %get-tuple-element.36), channel_id=1, source_target_pairs={{0,2},{1,3},{2,0},{3,1},{4,6},{5,7},{6,4},{7,5},{8,10},{9,11},{10,... | collective-permute-start | bytes 466952 | tf_op jit(solution)/shard_map/ppermute | solution.py:622
  22.5 10.1 %collective-permute-start.9 = (bf16[304,256]{1,0:T(8,128)(2,1)S(1)}, bf16[304,256]{1,0:T(8,128)(2,1)S(1)}, u32[]{:S(2)}, u32[]{:S(2)}) collective-permute-start(bf16[304,256]{1,0:T(8,128)(2,1)S(1)} %get-tuple-element.37), channel_id=1, source_target_pairs={{0,3},{1,2},{2,1},{3,0},{4,7},{5,6},{6,5},{7,4},{8,11},{9,10},{10,... | collective-permute-start | bytes 466952 | tf_op jit(solution)/shard_map/ppermute | solution.py:622
  23.8 13.1 %collective-permute-start.2 = (bf16[256,256]{1,0:T(8,128)(2,1)S(1)}, bf16[256,256]{1,0:T(8,128)(2,1)S(1)}, u32[]{:S(2)}, u32[]{:S(2)}) collective-permute-start(bf16[256,256]{1,0:T(8,128)(2,1)S(1)} %get-tuple-element.27), channel_id=1, source_target_pairs={{0,4},{1,5},{2,6},{3,7},{4,0},{5,1},{6,2},{7,3},{8,12},{9,13},{10,... | collective-permute-start | bytes 393224 | tf_op jit(solution)/shard_map/ppermute | solution.py:622
  25.1 16.2 %collective-permute-start.3 = (bf16[256,256]{1,0:T(8,128)(2,1)S(1)}, bf16[256,256]{1,0:T(8,128)(2,1)S(1)}, u32[]{:S(2)}, u32[]{:S(2)}) collective-permute-start(bf16[256,256]{1,0:T(8,128)(2,1)S(1)} %get-tuple-element.28), channel_id=1, source_target_pairs={{0,5},{1,4},{2,7},{3,6},{4,1},{5,0},{6,3},{7,2},{8,13},{9,12},{10,... | collective-permute-start | bytes 393224 | tf_op jit(solution)/shard_map/ppermute | solution.py:622
  27.1 18.9 %collective-permute-start.4 = (bf16[256,256]{1,0:T(8,128)(2,1)S(1)}, bf16[256,256]{1,0:T(8,128)(2,1)S(1)}, u32[]{:S(2)}, u32[]{:S(2)}) collective-permute-start(bf16[256,256]{1,0:T(8,128)(2,1)S(1)} %get-tuple-element.29), channel_id=1, source_target_pairs={{0,6},{1,7},{2,4},{3,5},{4,2},{5,3},{6,0},{7,1},{8,14},{9,15},{10,... | collective-permute-start | bytes 393224 | tf_op jit(solution)/shard_map/ppermute | solution.py:622
  28.6 20.2 %collective-permute-start.5 = (bf16[256,256]{1,0:T(8,128)(2,1)S(1)}, bf16[256,256]{1,0:T(8,128)(2,1)S(1)}, u32[]{:S(2)}, u32[]{:S(2)}) collective-permute-start(bf16[256,256]{1,0:T(8,128)(2,1)S(1)} %get-tuple-element.30), channel_id=1, source_target_pairs={{0,7},{1,6},{2,5},{3,4},{4,3},{5,2},{6,1},{7,0},{8,15},{9,14},{10,... | collective-permute-start | bytes 393224 | tf_op jit(solution)/shard_map/ppermute | solution.py:622

commit v4 on v3

--- a/solution.py
+++ b/solution.py
@@ -13,7 +13,8 @@
 SEG = 8
 SL = SEG * C
 PAD = 2
-TAPS = (KV + 1) // 2
+QUAD = 4
+TAPS = 3
 HALF = SL // 2
 PACK = 48
 VMEM = 20 * 1024 * 1024
@@ -76,7 +77,7 @@
         out_specs=[full] * 3,
         out_shape=[out(height), out(3), out(3)],
         compiler_params=params(),
-        cost_estimate=cost(1000, 1000),
+        cost_estimate=cost(2 * levels * height * lanes * 256, 8 * levels * height * lanes),
     )(ids, field)
 
 
@@ -110,28 +111,30 @@
 
 
 def up_kernel(tiles, ids_ref, vert_ref, out_ref):
-    row = lax.broadcasted_iota(jnp.int32, (KV * HALF, KV * C), 0)
-    column = lax.broadcasted_iota(jnp.int32, (KV * HALF, KV * C), 1)
-    spread = ((row // HALF == column // C) & (row % C == column % C)).astype(BF16)
+    two = 2 * C
+    row = lax.broadcasted_iota(jnp.int32, (KV * two, KV * C), 0)
+    column = lax.broadcasted_iota(jnp.int32, (KV * two, KV * C), 1)
+    spread = ((row // two == column // C) & (row % C == column % C)).astype(BF16)
     row = lax.broadcasted_iota(jnp.int32, (C, HALF), 0)
     column = lax.broadcasted_iota(jnp.int32, (C, HALF), 1)
     repeat = (row == column % C).astype(BF16)
-    row = lax.broadcasted_iota(jnp.int32, (KV * HALF, HALF), 0)
-    column = lax.broadcasted_iota(jnp.int32, (KV * HALF, HALF), 1)
-    same = (row % HALF) // C == column // C
-    zero = jnp.zeros((HALF, HALF), BF16)
+    row = lax.broadcasted_iota(jnp.int32, (KV * two, HALF), 0)
+    column = lax.broadcasted_iota(jnp.int32, (KV * two, HALF), 1)
+    same = (row % two) // C == (column % two) // C
+    low = lax.broadcasted_iota(jnp.int32, (two, HALF), 1) < two
     for layer in range(vert_ref.shape[0]):
         tall = lax.dot_general(spread, vert_ref[layer], NT, preferred_element_type=F32).astype(BF16)
         wide = jnp.dot(tall, repeat, preferred_element_type=F32)
-        wide = jnp.where(same, wide, 0.0).astype(BF16)
+        wide = jnp.where(same, wide, 0.0)
+        tap = lambda k: wide[k * two : (k + 1) * two] if 0 <= k < KV else jnp.zeros((two, HALF), F32)
         for block in range(TAPS):
             at = pl.multiple_of(turned_index(ids_ref, tiles, block, TAPS) * SL, SL)
-            for zi in range(2):
-                parts = []
-                for zo in range(2):
-                    k = 2 * block + zi - zo
-                    parts.append(wide[k * HALF : (k + 1) * HALF] if 0 <= k < KV else zero)
-                out_ref[layer, pl.ds(at + zi * HALF, HALF)] = jnp.concatenate(parts, axis=1)
+            rows = []
+            for n in range(QUAD):
+                zi = QUAD * block + n
+                parts = [jnp.where(low, tap(zi - zo), tap(zi - zo - 1)) for zo in (0, 2)]
+                rows.append(jnp.concatenate(parts, axis=1))
+            out_ref[layer, pl.ds(at, SL)] = jnp.concatenate(rows, axis=0).astype(BF16)
 
 
 def turned_index(ids_ref, tiles, index, count):
@@ -223,39 +226,52 @@
     return out
 
 
-def line_sides(line, ahead, behind):
+def line_sides(line):
     count = line.shape[0]
+    row = lax.broadcasted_iota(jnp.int32, (count, HALF), 0)
     a0, a1 = line[:, :HALF], line[:, HALF:]
-    before = jnp.concatenate([ahead, a1.astype(F32)], axis=0)
-    before = pltpu.roll(before, 1, 0)[16:].astype(BF16)
-    after = jnp.concatenate([a0.astype(F32), behind], axis=0)
-    after = pltpu.roll(after, count + 15, 0)[:count].astype(BF16)
-    return [before, a0, a1], [a0, a1, after]
-
-
-def halo_weight(weight_ref, first, yp):
+    before = pltpu.roll(a1.astype(F32), 1, 0)
+    before = jnp.where(row == 0, 0.0, before).astype(BF16)
+    after = pltpu.roll(a0.astype(F32), count - 1, 0)
+    after = jnp.where(row == count - 1, 0.0, after).astype(BF16)
+    first, second = [before, a0, a1], [a0, a1, after]
+    return jnp.concatenate(first, axis=1), jnp.concatenate(second, axis=1)
+
+
+def halo_sums(lines, weight_ref, beyond, height):
     wide = 3 * HALF
-    at = pl.multiple_of((first - 2 * yp + PAD) * wide, wide)
-    return weight_ref[pl.ds(at, 3 * wide)]
+    first = beyond * (height + 3)
+    full = beyond * (height // 2 - 1)
+    at = pl.multiple_of((first - 2 * full + PAD) * wide, wide)
+    stacked = jnp.concatenate([jnp.concatenate(line, axis=1) for line in lines], axis=0)
+    total = jnp.dot(stacked, weight_ref[pl.ds(at, 3 * wide)], preferred_element_type=F32)
+    nearest = [jnp.where(beyond == 1, line[0], line[2]) for line in lines]
+    thin = height // 2 - 1 - full
+    at = pl.multiple_of((first + 2 * (1 - beyond) - 2 * thin + PAD) * wide, wide)
+    less = jnp.dot(
+        jnp.concatenate(nearest, axis=0), weight_ref[pl.ds(at, wide)], preferred_element_type=F32
+    )
+    return total, less
 
 
 def early_kernel(ids_ref, own_ref, pair_ref, weight_ref, out_ref):
     height, levels, segments, _ = own_ref.shape
     wide = 3 * HALF
-    zero = jnp.zeros((16, HALF), F32)
     own, pair = [], []
     for z in range(levels):
-        for rows, ref in ((own, own_ref), (pair, pair_ref)):
-            sides = [line_sides(ref[y, z], zero, zero) for y in range(ref.shape[0])]
-            for h in range(2):
-                rows.append(jnp.concatenate([tile for side in sides for tile in side[h]], axis=1))
+        sides = [line_sides(own_ref[y, z]) for y in range(height)]
+        for h in range(2):
+            own.append(jnp.concatenate([side[h] for side in sides], axis=1))
+        sides = [line_sides(pair_ref[y, z]) for y in range(3)]
+        pair += [[side[h] for side in sides] for h in range(2)]
     own = jnp.concatenate(own, axis=0)
-    pair = jnp.concatenate(pair, axis=0)
-    first = (1 - ids_ref[1] % 2) * (height + 3)
-    for yp in range(height // 2):
-        at = (3 - 2 * yp + PAD) * wide
-        total = jnp.dot(own, weight_ref[at : at + height * wide], preferred_element_type=F32)
-        total += jnp.dot(pair, halo_weight(weight_ref, first, yp), preferred_element_type=F32)
+    beyond = 1 - ids_ref[1] % 2
+    sums = halo_sums(pair, weight_ref, beyond, height)
+    for n, total in enumerate(sums):
+        yp = beyond if n == 0 else 1 - beyond
+        at = pl.multiple_of((3 - 2 * yp + PAD) * wide, wide)
+        weight = weight_ref[pl.ds(at, height * wide)]
+        total = total + jnp.dot(own, weight, preferred_element_type=F32)
         out_ref[yp] = total.reshape(levels, 2, segments, SL)
 
 
@@ -272,68 +288,64 @@
     )(ids, own, pair, weight)
 
 
-def half_kernel(tiles, is_near, ids_ref, own_ref, cross_ref, early_ref, *rest):
-    weight_ref, bias_ref = rest[:2]
-    rest, done = rest[2:-1], rest[-1]
-    extra_refs, out_refs = rest[:-tiles], rest[-tiles:]
+def swap_halves(first, second):
+    low = lax.broadcasted_iota(jnp.int32, first.shape, 1) < HALF // 2
+    lower = jnp.where(low, first, pltpu.roll(second, HALF // 2, 1))
+    upper = jnp.where(low, pltpu.roll(first, HALF // 2, 1), second)
+    return lower, upper
+
+
+def level_lanes(values):
+    sides = [swap_halves(values[n], values[n + 1]) for n in (0, 2)]
+    return [jnp.concatenate([side[n] for side in sides], axis=1) for n in range(2)]
+
+
+def finish_kernel(ids_ref, own_ref, cross_ref, early_ref, weight_ref, bias_ref, *rest):
+    extra_refs, out_refs, done = rest[:2], rest[2:-1], rest[-1]
     height, levels, segments, _ = own_ref.shape
-    size = segments // 2
-    near = ids_ref[0] // tiles
-    start = pl.multiple_of((near if is_near else 1 - near) * size, size)
-    per = size // tiles
-    ahead = pl.multiple_of(jnp.maximum(start - 16, 0), 16)
-    behind = pl.multiple_of(jnp.minimum(start + size, segments - 16), 16)
-    has_ahead = jnp.where(start > 0, 1.0, 0.0)
-    has_behind = jnp.where(start + size < segments, 1.0, 0.0)
+    tiles = len(out_refs)
+    per = segments // tiles
     bias = bias_row(bias_ref[...])
     cross = []
     for z in range(levels):
-        sides = []
-        for y in range(3):
-            sides.append(
-                line_sides(
-                    cross_ref[y, z, pl.ds(start, size)],
-                    cross_ref[y, z, pl.ds(ahead, 16), HALF:].astype(F32) * has_ahead,
-                    cross_ref[y, z, pl.ds(behind, 16), :HALF].astype(F32) * has_behind,
-                )
-            )
+        sides = [line_sides(cross_ref[y, z]) for y in range(3)]
+        cross += [[side[h] for side in sides] for h in range(2)]
+    beyond = ids_ref[1] % 2
+    sums = halo_sums(cross, weight_ref, beyond, height)
+    for yn, total in enumerate(sums):
+        yp = beyond if yn == 0 else 1 - beyond
         for h in range(2):
-            cross.append(jnp.concatenate([tile for side in sides for tile in side[h]], axis=1))
-    cross = jnp.concatenate(cross, axis=0)
-    first = ids_ref[1] % 2 * (height + 3)
-    for yp in range(height // 2):
-        total = jnp.dot(cross, halo_weight(weight_ref, first, yp), preferred_element_type=F32)
-        for z in range(levels):
-            for h in range(2):
-                row = (z * 2 + h) * size
-                part = total[row : row + size] + early_ref[yp, z, h, pl.ds(start, size)]
-                for yo in range(2):
-                    y = 2 * yp + yo
-                    center = own_ref[y, z, pl.ds(start, size), h * HALF : (h + 1) * HALF]
-                    value = gelu(part[:, yo * HALF : (yo + 1) * HALF] + bias)
-                    value = (center.astype(F32) + value).astype(BF16)
-                    at = ((z // 2 * 2 + h) * height + y) * per
-                    lane = z % 2 * HALF
-                    done[:, at : at + per, lane : lane + HALF] = value.reshape(tiles, per, HALF)
+            for yo in range(2):
+                y = 2 * yp + yo
+                lane = slice(yo * HALF, (yo + 1) * HALF)
+                values = []
+                for z in range(levels):
+                    row = (z * 2 + h) * segments
+                    part = total[row : row + segments, lane] + early_ref[yp, z, h, :, lane]
+                    center = own_ref[y, z, :, h * HALF : (h + 1) * HALF]
+                    values.append(center.astype(F32) + gelu(part + bias))
+                for n, lanes in enumerate(level_lanes(values)):
+                    at = pl.multiple_of(((2 * h + n) * height + y) * per, per)
+                    done[:, pl.ds(at, per)] = lanes.astype(BF16).reshape(tiles, per, SL)
     rows = levels * height * per
     for slot, out_ref in enumerate(out_refs):
-        tile = ids_ref[0] % tiles ^ slot
+        tile = ids_ref[0] ^ slot
         out_ref[:rows] = done[tile]
-        for n, extra_ref in enumerate(extra_refs):
-            out_ref[rows:, n * HALF : (n + 1) * HALF] = extra_ref[tile]
-
-
-def half_horizontal(ids, own, cross, early, weight, bias, tiles, is_near, extra=()):
+        if slot < tiles // 2:
+            for n, extra_ref in enumerate(extra_refs):
+                out_ref[rows:, n * HALF : (n + 1) * HALF] = extra_ref[tile % (tiles // 2)]
+
+
+def finish_horizontal(ids, own, cross, early, weight, bias, extra, tiles):
     height, levels, segments, _ = own.shape
-    per = segments // (2 * tiles)
-    rows = levels * height * per
+    rows = levels * height * segments // tiles
     full = pl.BlockSpec(memory_space=pltpu.VMEM)
-    shape = (rows + (PACK if extra else 0), SL)
-    return pl.pallas_call(
-        functools.partial(half_kernel, tiles, is_near),
-        in_specs=[pl.BlockSpec(memory_space=pltpu.SMEM)] + [full] * (5 + len(extra)),
+    shape = lambda more: jax.ShapeDtypeStruct((rows + more, SL), BF16)
+    return pl.pallas_call(
+        finish_kernel,
+        in_specs=[pl.BlockSpec(memory_space=pltpu.SMEM)] + [full] * 7,
         out_specs=[full] * tiles,
-        out_shape=[jax.ShapeDtypeStruct(shape, BF16)] * tiles,
+        out_shape=[shape(PACK)] * (tiles // 2) + [shape(0)] * (tiles // 2),
         scratch_shapes=[pltpu.VMEM((tiles, rows, SL), BF16)],
         compiler_params=params(),
         cost_estimate=cost(1000, 1000),
@@ -389,14 +401,14 @@
 def source_kernel(tiles, rows, ids_ref, *refs):
     got_refs, out_ref = refs[:-1], refs[-1]
     places = out_ref.shape[0]
-    pairs = places // (2 * rows)
+    groups = places // (QUAD * rows)
     got = jnp.concatenate([ref[ref.shape[0] - PACK :] for ref in got_refs], axis=1)
     slots = got.shape[1]
     cells = (got[C : C + 1].astype(F32) * HALF + got[C + 1 : C + 2].astype(F32)).astype(jnp.int32)
     x, row, level = cells % SEG, cells // SEG % rows, cells // (SEG * rows)
-    pair = turned_index(ids_ref, tiles, level // 2, pairs)
-    place = (pair * 2 + x // (SEG // 2)) * rows + row
-    within = level % 2 * (SEG // 2) + x % (SEG // 2)
+    group = turned_index(ids_ref, tiles, level // QUAD, groups)
+    place = (group * QUAD + x // 2) * rows + row
+    within = level % QUAD * 2 + x % 2
     lane = lax.broadcasted_iota(jnp.int32, (SL, slots), 0) // C
     spread = jnp.where(lane == within, jnp.concatenate([got[:C]] * SEG, axis=0).astype(F32), 0.0)
     index = lax.broadcasted_iota(jnp.int32, (places, slots), 0)
@@ -452,136 +464,140 @@
 def layer_step(held, base, first, last, block, weight, bias):
     taps = [held[(first - base + k) * block : (last - base + k) * block] for k in range(TAPS)]
     total = jnp.dot(jnp.concatenate(taps, axis=1), weight, preferred_element_type=F32)
-    center = held[(first - base + 2) * block : (last - base + 2) * block].astype(F32)
+    center = held[(first - base + 1) * block : (last - base + 1) * block].astype(F32)
     return center + gelu(total + bias)
 
 
-def put_group(out_ref, value, height, block, at_of):
-    rows = block // 2
-    count = 256 // block
+def put_groups(out_ref, value, height, block, place_of):
+    rows = block // QUAD
     across = rows // height
-    swap = swap_matrix(2 * count * height, across)
-    for g in range(value.shape[0] // (count * block)):
+    count = max(1, 256 // block)
+    size = QUAD * height
+    swap = swap_matrix(count * size, across)
+    for g in range(0, value.shape[0] // block, count):
         pieces = []
+        for n in range(g, g + count):
+            tile = lambda q, t: value[
+                n * block + q * rows : n * block + (q + 1) * rows, t * HALF : (t + 1) * HALF
+            ]
+            for t in range(2):
+                sides = [swap_halves(tile(2 * h, t), tile(2 * h + 1, t)) for h in range(2)]
+                for level in range(2):
+                    pieces.append(jnp.concatenate([side[level] for side in sides], axis=1))
+        turned = jnp.dot(
+            swap, jnp.concatenate(pieces, axis=0).astype(BF16), preferred_element_type=F32
+        ).astype(BF16)
         for n in range(count):
-            start = (g * count + n) * block
-            for j in range(2):
-                lane = slice(j * HALF, (j + 1) * HALF)
-                pieces.append(
-                    jnp.concatenate(
-                        [value[start : start + rows, lane], value[start + rows : start + block, lane]],
-                        axis=1,
-                    )
-                )
-        turned = jnp.dot(
-            swap, jnp.concatenate(pieces, axis=0), preferred_element_type=F32
-        ).astype(BF16)
-        size = 2 * height
-        for n in range(count):
-            at = at_of(g * count + n) * 2
+            at = place_of(g + n) * QUAD
             for s in range(across):
                 start = (s * count + n) * size
-                out_ref[pl.ds(at, 2), :, s * SL : (s + 1) * SL] = turned[
+                out_ref[pl.ds(at, QUAD), :, s * SL : (s + 1) * SL] = turned[
                     start : start + size
-                ].reshape(2, height, SL)
+                ].reshape(QUAD, height, SL)
+
+
+def lane_biases(bias_ref):
+    rows = [bias_row(bias_ref[n : n + 1]) for n in range(2)]
+    return [jnp.concatenate([row, row], axis=1) for row in rows]
+
+
+def place_pieces(tiles, ids_ref, piece_refs, held, first, block):
+    for d, piece_ref in enumerate(piece_refs):
+        at = turned_index(ids_ref, tiles, ids_ref[0] % tiles ^ d, tiles) + first
+        held[pl.ds(pl.multiple_of(at * block, block), block)] = piece_ref[:block]
 
 
 def near_kernel(tiles, height, ids_ref, *refs):
     piece_refs = refs[:tiles]
     source_ref, weight_ref, bias_ref, out_ref, kept_ref, later_ref, held, step = refs[tiles:]
-    pairs = out_ref.shape[0] // 2 + 4
-    block = kept_ref.shape[0] // 4
-    bias = [bias_row(bias_ref[n : n + 1]) for n in range(2)]
-    bias = [jnp.concatenate([row, row], axis=1) for row in bias]
-    held[: 2 * block] = jnp.zeros((2 * block, SL), BF16)
-    step[: 2 * block] = jnp.zeros((2 * block, SL), BF16)
-    per = pairs // tiles
-    for d, piece_ref in enumerate(piece_refs):
-        for n in range(per):
-            number = (ids_ref[0] % tiles ^ d) * per + n
-            at = turned_index(ids_ref, tiles, number, pairs) + 2
-            held[pl.ds(pl.multiple_of(at * block, block), block)] = piece_ref[
-                n * block : (n + 1) * block
-            ]
-    kept_ref[...] = held[(pairs - 2) * block : (pairs + 2) * block]
-    for first, last in chunks(0, pairs - 2, 4):
+    groups = out_ref.shape[0] // QUAD + 2
+    block = kept_ref.shape[0] // 2
+    bias = lane_biases(bias_ref)
+    held[:block] = jnp.zeros((block, SL), BF16)
+    step[:block] = jnp.zeros((block, SL), BF16)
+    place_pieces(tiles, ids_ref, piece_refs, held, 1, block)
+    kept_ref[...] = held[(groups - 1) * block : (groups + 1) * block]
+    for first, last in chunks(0, groups - 1, 2):
         value = layer_step(held, 0, first, last, block, weight_ref[0], bias[0])
-        step[(first + 2) * block : (last + 2) * block] = value.astype(BF16)
-    later_ref[...] = step[(pairs - 4) * block : pairs * block]
-    for first, last in chunks(0, pairs - 4, 4):
+        step[(first + 1) * block : (last + 1) * block] = value.astype(BF16)
+    later_ref[...] = step[(groups - 2) * block : groups * block]
+    for first, last in chunks(0, groups - 2, 2):
         value = layer_step(step, 0, first, last, block, weight_ref[1], bias[1])
-        value = (value + source_ref[first * block : last * block]).astype(BF16)
-        put_group(
+        value = value + source_ref[first * block : last * block]
+        put_groups(
             out_ref,
             value,
             height,
             block,
-            lambda n: turned_index(ids_ref, tiles, first + n, pairs - 4),
+            lambda n: turned_index(ids_ref, tiles, first + n, groups - 2),
         )
 
 
 def far_kernel(tiles, height, ids_ref, *refs):
     piece_refs = refs[:tiles]
-    early_ref, kept_ref, later_ref, source_ref, weight_ref, bias_ref, out_ref, held, step = refs[tiles:]
-    pairs = out_ref.shape[0] // 2
-    half = pairs // 2
-    block = kept_ref.shape[0] // 4
-    bias = [bias_row(bias_ref[n : n + 1]) for n in range(2)]
-    bias = [jnp.concatenate([row, row], axis=1) for row in bias]
-    held[: 4 * block] = kept_ref[...]
-    held[(half + 4) * block :] = jnp.zeros((2 * block, SL), BF16)
-    step[: 4 * block] = later_ref[...]
-    step[(half + 6) * block :] = jnp.zeros((2 * block, SL), BF16)
-    per = half // tiles
-    for d, piece_ref in enumerate(piece_refs):
-        for n in range(per):
-            number = (ids_ref[0] % tiles ^ d) * per + n
-            at = turned_index(ids_ref, tiles, number, half) + 4
-            held[pl.ds(pl.multiple_of(at * block, block), block)] = piece_ref[
-                n * block : (n + 1) * block
-            ]
-    for first, last in chunks(half - 2, pairs, 5):
-        value = layer_step(held, half - 2, first, last, block, weight_ref[0], bias[0])
-        step[(first - half + 6) * block : (last - half + 6) * block] = value.astype(BF16)
+    early_ref, kept_ref, later_ref, source_ref, weight_ref, bias_ref = refs[tiles : tiles + 6]
+    out_ref, held, step, result, sems = refs[tiles + 6 :]
+    groups = out_ref.shape[0] // QUAD
+    half = groups // 2
+    block = kept_ref.shape[0] // 2
     early = early_ref.shape[0]
-    out_ref[pl.ds(turned_index(ids_ref, tiles, 0, 2 * pairs // early) * early, early)] = early_ref[...]
-    for first, last in chunks(half - 4, pairs, 4):
-        value = layer_step(step, half - 4, first, last, block, weight_ref[1], bias[1])
-        value = (value + source_ref[first * block : last * block]).astype(BF16)
-        put_group(
-            out_ref, value, height, block, lambda n: turned_index(ids_ref, tiles, first + n, pairs)
-        )
+    at = turned_index(ids_ref, tiles, 0, groups * QUAD // early) * early
+    copies = [pltpu.make_async_copy(early_ref, out_ref.at[pl.ds(at, early)], sems.at[groups])]
+    copies[0].start()
+    bias = lane_biases(bias_ref)
+    held[: 2 * block] = kept_ref[...]
+    held[(half + 2) * block :] = jnp.zeros((block, SL), BF16)
+    step[: 2 * block] = later_ref[...]
+    step[(half + 3) * block :] = jnp.zeros((block, SL), BF16)
+    place_pieces(tiles, ids_ref, piece_refs, held, 2, block)
+    for first, last in chunks(half - 1, groups, 3):
+        value = layer_step(held, half - 1, first, last, block, weight_ref[0], bias[0])
+        step[(first - half + 3) * block : (last - half + 3) * block] = value.astype(BF16)
+    for first, last in chunks(half - 2, groups, 2):
+        value = layer_step(step, half - 2, first, last, block, weight_ref[1], bias[1])
+        value = value + source_ref[first * block : last * block]
+        place_of = lambda n: turned_index(ids_ref, tiles, first + n, groups)
+        put_groups(result, value, height, block, place_of)
+        for n in range(last - first):
+            span = pl.ds(place_of(n) * QUAD, QUAD)
+            copies.append(
+                pltpu.make_async_copy(result.at[span], out_ref.at[span], sems.at[first + n])
+            )
+            copies[-1].start()
+    for copy in copies:
+        copy.wait()
 
 
 def whole_kernel(height, ids_ref, piece_ref, source_ref, weight_ref, bias_ref, out_ref, held, step):
     levels = out_ref.shape[0]
-    pairs = levels // 2
+    groups = levels // QUAD
     rows = piece_ref.shape[0] // levels
-    block = 2 * rows
-    bias = [bias_row(bias_ref[n : n + 1]) for n in range(2)]
-    bias = [jnp.concatenate([row, row], axis=1) for row in bias]
+    block = QUAD * rows
+    bias = lane_biases(bias_ref)
     for buffer in (held, step):
-        buffer[: 2 * block] = jnp.zeros((2 * block, SL), BF16)
-        buffer[(pairs + 2) * block :] = jnp.zeros((2 * block, SL), BF16)
-    for z in range(levels):
+        buffer[:block] = jnp.zeros((block, SL), BF16)
+        buffer[(groups + 1) * block :] = jnp.zeros((block, SL), BF16)
+    for group in range(groups):
         for h in range(2):
-            start = (z // 2 + 2) * block + h * rows
-            held[start : start + rows, z % 2 * HALF : (z % 2 + 1) * HALF] = piece_ref[
-                z * rows : (z + 1) * rows, h * HALF : (h + 1) * HALF
-            ]
-    value = layer_step(held, 0, 0, pairs, block, weight_ref[0], bias[0])
-    step[2 * block : (pairs + 2) * block] = value.astype(BF16)
-    value = layer_step(step, 0, 0, pairs, block, weight_ref[1], bias[1])
-    value = (value + source_ref[...]).astype(BF16)
-    put_group(out_ref, value, height, block, lambda n: n)
+            values = []
+            for z in range(group * QUAD, (group + 1) * QUAD):
+                tile = piece_ref[z * rows : (z + 1) * rows, h * HALF : (h + 1) * HALF]
+                values.append(tile.astype(F32))
+            for n, lanes in enumerate(level_lanes(values)):
+                at = (group + 1) * block + (2 * h + n) * rows
+                held[at : at + rows] = lanes.astype(BF16)
+    value = layer_step(held, 0, 0, groups, block, weight_ref[0], bias[0])
+    step[block : (groups + 1) * block] = value.astype(BF16)
+    value = layer_step(step, 0, 0, groups, block, weight_ref[1], bias[1])
+    put_groups(out_ref, value + source_ref[...], height, block, lambda n: n)
 
 
 def vertical(ids, close, far, source, weight, bias, levels, height, tiles):
     full = pl.BlockSpec(memory_space=pltpu.VMEM)
     smem = pl.BlockSpec(memory_space=pltpu.SMEM)
     rows = source.shape[0] // levels
-    block = 2 * rows
-    pairs = levels // 2
+    block = QUAD * rows
+    groups = levels // QUAD
     lanes = rows // height * SL
     buffer = lambda count: pltpu.VMEM((count * block, SL), BF16)
     array = lambda count: jax.ShapeDtypeStruct((count * block, SL), BF16)
@@ -592,26 +608,31 @@
             in_specs=[smem] + [full] * 4,
             out_specs=full,
             out_shape=result(levels),
-            scratch_shapes=[buffer(pairs + 4)] * 2,
+            scratch_shapes=[buffer(groups + 2)] * 2,
             compiler_params=params(),
             cost_estimate=cost(1000, 1000),
         )(ids, *close, source, weight, bias)
-    half = pairs // 2
+    half = groups // 2
     early, kept, later = pl.pallas_call(
         functools.partial(near_kernel, tiles, height),
         in_specs=[smem] + [full] * (len(close) + 3),
         out_specs=[full] * 3,
-        out_shape=[result(2 * (half - 4)), array(4), array(4)],
-        scratch_shapes=[buffer(half + 2), buffer(half)],
+        out_shape=[result(QUAD * (half - 2)), array(2), array(2)],
+        scratch_shapes=[buffer(half + 1), buffer(half)],
         compiler_params=params(),
         cost_estimate=cost(1000, 1000),
     )(ids, *close, source, weight, bias)
     return pl.pallas_call(
         functools.partial(far_kernel, tiles, height),
         in_specs=[smem] + [full] * (len(far) + 6),
-        out_specs=full,
+        out_specs=pl.BlockSpec(memory_space=pl.ANY),
         out_shape=result(levels),
-        scratch_shapes=[buffer(half + 6), buffer(half + 8)],
+        scratch_shapes=[
+            buffer(half + 3),
+            buffer(half + 4),
+            pltpu.VMEM((levels, height, lanes), BF16),
+            pltpu.SemaphoreType.DMA((groups + 1,)),
+        ],
         compiler_params=params(),
         cost_estimate=cost(1000, 1000),
     )(ids, *far, early, kept, later, source, weight, bias)
@@ -633,7 +654,7 @@
     per = segments // columns
     ids = jnp.stack([lax.axis_index("cols"), lax.axis_index("rows")]).astype(jnp.int32)
     bias = point_bias.reshape(1, C)
-    if per % 16 == 0 and columns % 2 == 0 and bands % 2 == 0 and 256 % (levels * height) == 0:
+    if per % 16 == 0 and columns % 2 == 0 and bands % 2 == 0 and levels == QUAD and 256 % (levels * height) == 0:
         tiles = columns // 2
         own, cross, pair = to_segments(ids, field)
         inside = [(i, i ^ 1) for i in range(bands)]
@@ -645,13 +666,11 @@
         )
         relayed = exchange(far_rows, tiles)
         early = early_horizontal(ids, own, pair, across)
-        far = half_horizontal(ids, own, cross, early, across, bias, tiles, False)
-        ids_near, _ = lax.optimization_barrier((ids, far[0]))
-        far = [exchange(block, tiles + slot) for slot, block in enumerate(far)]
-        close = half_horizontal(
-            ids_near, own, cross, early, across, bias, tiles, True, (close_rows, relayed)
+        pieces = finish_horizontal(
+            ids, own, cross, early, across, bias, (close_rows, relayed), columns
         )
-        close = [exchange(block, slot) if slot else block for slot, block in enumerate(close)]
+        pieces = [exchange(block, slot) if slot else block for slot, block in enumerate(pieces)]
+        close, far = pieces[:tiles], pieces[tiles:]
         got = close
     else:
         tiles, far = 0, []

time: 54.6 us -> 52.9 us (0.969)
  Pallas kernels: 21 us -> 18.1 us
  waiting for transfers between devices: 14.2 us -> 16 us
  starting transfers between devices: 14 us -> 12.9 us
    ppermute x8, waiting for transfers between devices: 14.2 us -> 16 us  [exchange(): lax.ppermute(block, 'cols', [(i, i ^ distance) for i in range(count)])]
    ppermute x8, starting transfers between devices: 10.2 us -> 9.14 us  [exchange(): lax.ppermute(block, 'cols', [(i, i ^ distance) for i in range(count)])]
    pallas_call x1, Pallas kernels: 5.38 us -> 4.39 us  [vertical(): pl.pallas_call(functools.partial(far_kernel, tiles, height), in_specs=[sm...]
    pallas_call x2 -> x1, Pallas kernels: 3.6 us -> 2.77 us  [finish_horizontal(): pl.pallas_call(finish_kernel, in_specs=[pl.BlockSpec(memory_space=pltpu.S...]
  transfers between devices with their start and end apart: 10 -> 10, of which waited for: 5 -> 5; matrix products, arithmetic and copies ran while one was open for 0% -> 0% of each run, Pallas kernels for 23% -> 19%
where the time goes in v4:
time: 52.9 us; the launch traced here: 52 us
  Pallas kernels  18.1 us (34%)
  waiting for transfers between devices  16 us (30%)
  starting transfers between devices  12.9 us (24%)
  local copies, waits for them, and re-layouts  4.8 us (9%)
    ppermute x8, waiting for transfers between devices, exchange(): lax.ppermute(block, 'cols', [(i, i ^ distance) for i in range(count)])  16 us
    ppermute x8, starting transfers between devices, exchange(): lax.ppermute(block, 'cols', [(i, i ^ distance) for i in range(count)])  9.14 us
    unnamed x18, local copies, waits for them, and re-layouts  4.8 us
    pallas_call x1, Pallas kernels, vertical(): pl.pallas_call(functools.partial(far_kernel, tiles, height), in_specs=[sm...  4.39 us
    pallas_call x1, Pallas kernels, early_horizontal(): pl.pallas_call(early_kernel, in_specs=[pl.BlockSpec(memory_space=pltpu.SM...  3.31 us
    ppermute x1, starting transfers between devices, body(): cross = lax.ppermute(cross, 'rows', beyond)  3.02 us
    pallas_call x1, Pallas kernels, finish_horizontal(): pl.pallas_call(finish_kernel, in_specs=[pl.BlockSpec(memory_space=pltpu.S...  2.77 us
    pallas_call x1, Pallas kernels, vertical(): pl.pallas_call(functools.partial(near_kernel, tiles, height), in_specs=[s...  1.95 us
  transfers between devices with their start and end apart: 10, of which 5 were waited for; matrix products, arithmetic and copies ran while one was open for 0% of the time, Pallas kernels for 19%

profile of v4, /device:TPU:9, one launch (start us, length us, event | category | flops | bytes accessed | tf_op | source)
XLA Modules:
  0.0 52.0 jit_solution(2382567015063566759)
XLA Ops:
  0.0 0.1 pad_add_fusion.ids_ref
  0.1 0.0 copy-start
  0.1 1.2 %copy-done = bf16[4,4,32768]{2,1,0:T(4,128)(2,1)S(1)} copy-done((bf16[4,4,32768]{2,1,0:T(4,128)(2,1)S(1)}, bf16[4,4,32768]{2,1,0:T(4,128)(2,1)}, u32[]{:S(2)}) %copy-start) | copy-done | bytes 1048600
  1.3 1.1 %shard_map.91 = (bf16[4,4,128,256]{3,2,1,0:T(8,128)(2,1)S(1)}, bf16[3,4,128,256]{3,2,1,0:T(8,128)(2,1)S(1)}, bf16[3,4,128,256]{3,2,1,0:T(8,128)(2,1)S(1)}) custom-call(s32[2]{0:T(128)S(1)} %pad_add_fusion.ids_ref, bf16[4,4,32768]{2,1,0:T(4,128)(2,1)S(1)} %copy-done), custom_call_target="tpu_custom_call" | custom-call | flops 268435456 | bytes 4194304 | tf_op jit(solution)/shard_map/pallas_call | solution.py:74
  2.4 0.8 %collective-permute-start.1 = (bf16[3,4,128,256]{3,2,1,0:T(8,128)(2,1)S(1)}, bf16[3,4,128,256]{3,2,1,0:T(8,128)(2,1)S(1)}, u32[]{:S(2)}, u32[]{:S(2)}) collective-permute-start(bf16[3,4,128,256]{3,2,1,0:T(8,128)(2,1)S(1)} %get-tuple-element.24), channel_id=1, source_target_pairs={{0,8},{8,0},{16,24},{24,16},{1,9},{9,1},{17,25},{25,17},{2,10},{10... | collective-permute-start | bytes 2359304 | tf_op jit(solution)/shard_map/ppermute | solution.py:663
  3.2 3.0 %collective-permute-start = (bf16[3,4,128,256]{3,2,1,0:T(8,128)(2,1)S(1)}, bf16[3,4,128,256]{3,2,1,0:T(8,128)(2,1)S(1)}, u32[]{:S(2)}, u32[]{:S(2)}) collective-permute-start(bf16[3,4,128,256]{3,2,1,0:T(8,128)(2,1)S(1)} %get-tuple-element.23), channel_id=1, source_target_pairs={{8,16},{16,8},{9,17},{17,9},{10,18},{18,10},{11,19},{19,11},{12,20... | collective-permute-start | bytes 2359304 | tf_op jit(solution)/shard_map/ppermute | solution.py:662
  6.2 0.0 copy-start.2
  6.2 0.7 %copy-done.2 = bf16[512,32]{0,1:T(8,128)(2,1)S(1)} copy-done((bf16[512,32]{0,1:T(8,128)(2,1)S(1)}, bf16[512,32]{0,1:T(8,128)(2,1)}, u32[]{:S(2)}) %copy-start.2) | copy-done | bytes 32792
  7.0 0.0 copy-start.3
  7.0 0.7 %copy-done.3 = f32[7,7,32]{2,1,0:T(8,128)S(1)} copy-done((f32[7,7,32]{2,1,0:T(8,128)S(1)}, f32[7,7,32]{2,1,0:T(8,128)}, u32[]{:S(2)}) %copy-start.3) | copy-done | bytes 6296
  7.7 0.0 copy-start.4
  7.7 0.7 %copy-done.4 = bf16[32,32]{1,0:T(8,128)(2,1)S(1)} copy-done((bf16[32,32]{1,0:T(8,128)(2,1)S(1)}, bf16[32,32]{1,0:T(8,128)(2,1)}, u32[]{:S(2)}) %copy-start.4) | copy-done | bytes 2072
  8.4 0.0 copy-start.6
  8.4 0.7 %copy-done.6 = s32[512,1]{0,1:T(1,128)S(1)} copy-done((s32[512,1]{0,1:T(1,128)S(1)}, s32[512,1]{0,1:T(1,128)}, u32[]{:S(2)}) %copy-start.6) | copy-done | bytes 2072
  9.1 0.0 copy-start.7
  9.1 0.7 %copy-done.7 = s32[512]{0:T(512)S(1)} copy-done((s32[512]{0:T(512)S(1)}, s32[512]{0:T(512)}, u32[]{:S(2)}) %copy-start.7) | copy-done | bytes 2072
  9.8 1.5 %shard_map.92 = (bf16[4608,256]{1,0:T(8,128)(2,1)S(1)}, bf16[4,48,128]{2,1,0:T(8,128)(2,1)S(1)}, bf16[4,48,128]{2,1,0:T(8,128)(2,1)S(1)}) custom-call(s32[2]{0:T(128)S(1)} %pad_add_fusion.ids_ref, f32[7,7,32]{2,1,0:T(8,128)S(1)} %copy-done.3, bf16[32,32]{1,0:T(8,128)(2,1)S(1)} %copy-done.4, bf16[32,512]{1,0:T(8,128)(2,1)S(1)} %bitcast.8, ...), custom_call_target="tpu_custom_call" | custom-call | flops 1000 | bytes 1000 | tf_op jit(solution)/shard_map/pallas_call | solution.py:442
  11.3 2.4 %collective-permute-start.2 = (bf16[4,48,128]{2,1,0:T(8,128)(2,1)S(1)}, bf16[4,48,128]{2,1,0:T(8,128)(2,1)S(1)}, u32[]{:S(2)}, u32[]{:S(2)}) collective-permute-start(bf16[4,48,128]{2,1,0:T(8,128)(2,1)S(1)} %get-tuple-element.27), channel_id=1, source_target_pairs={{0,4},{1,5},{2,6},{3,7},{4,0},{5,1},{6,2},{7,3},{8,12},{9,13},{10,... | collective-permute-start | bytes 147464 | tf_op jit(solution)/shard_map/ppermute | solution.py:643
  13.7 0.0 collective-permute-done.1.pair_ref
  13.7 0.0 copy-start.8
  13.7 3.3 %shard_map.93.early_ref = f32[2,4,2,128,256]{4,3,2,1,0:T(8,128)S(1)} custom-call(s32[2]{0:T(128)S(1)} %pad_add_fusion.ids_ref, bf16[4,4,128,256]{3,2,1,0:T(8,128)(2,1)S(1)} %get-tuple-element.22.own_ref, bf16[3,4,128,256]{3,2,1,0:T(8,128)(2,1)S(1)} %collective-permute-done.1.pair_ref, bf16[4608,256]{1,0:T(8,128)(2,1)S(1)} %get-tuple-element.25.weight_ref), custom_call_target="tpu_custom_call" | custom-call | flops 1000 | bytes 1000 | tf_op jit(solution)/shard_map/pallas_call | solution.py:281
  17.0 0.0 collective-permute-done.2.rest_1_
  17.0 0.0 collective-permute-done.cross_ref
  17.0 0.0 copy-done.8
  17.0 0.0 copy-start.1
  17.0 2.8 %shard_map.94 = (bf16[304,256]{1,0:T(8,128)(2,1)S(1)}, bf16[304,256]{1,0:T(8,128)(2,1)S(1)}, bf16[304,256]{1,0:T(8,128)(2,1)S(1)}, bf16[304,256]{1,0:T(8,128)(2,...) custom-call(s32[2]{0:T(128)S(1)} %pad_add_fusion.ids_ref, ...), custom_call_target="tpu_custom_call" | custom-call | flops 1000 | bytes 1000 | tf_op jit(solution)/shard_map/pallas_call | solution.py:344
  19.8 0.0 copy-start.5
  19.8 1.3 %collective-permute-start.7 = (bf16[304,256]{1,0:T(8,128)(2,1)S(1)}, bf16[304,256]{1,0:T(8,128)(2,1)S(1)}, u32[]{:S(2)}, u32[]{:S(2)}) collective-permute-start(bf16[304,256]{1,0:T(8,128)(2,1)S(1)} %get-tuple-element.33), channel_id=1, source_target_pairs={{0,1},{1,0},{2,3},{3,2},{4,5},{5,4},{6,7},{7,6},{8,9},{9,8},{10,11... | collective-permute-start | bytes 466952 | tf_op jit(solution)/shard_map/ppermute | solution.py:643
  21.1 0.2 collective-permute-start.8
  21.3 1.2 %collective-permute-start.9 = (bf16[304,256]{1,0:T(8,128)(2,1)S(1)}, bf16[304,256]{1,0:T(8,128)(2,1)S(1)}, u32[]{:S(2)}, u32[]{:S(2)}) collective-permute-start(bf16[304,256]{1,0:T(8,128)(2,1)S(1)} %get-tuple-element.35), channel_id=1, source_target_pairs={{0,3},{1,2},{2,1},{3,0},{4,7},{5,6},{6,5},{7,4},{8,11},{9,10},{10,... | collective-permute-start | bytes 466952 | tf_op jit(solution)/shard_map/ppermute | solution.py:643
  22.5 1.8 %collective-permute-start.3 = (bf16[256,256]{1,0:T(8,128)(2,1)S(1)}, bf16[256,256]{1,0:T(8,128)(2,1)S(1)}, u32[]{:S(2)}, u32[]{:S(2)}) collective-permute-start(bf16[256,256]{1,0:T(8,128)(2,1)S(1)} %get-tuple-element.28), channel_id=1, source_target_pairs={{0,4},{1,5},{2,6},{3,7},{4,0},{5,1},{6,2},{7,3},{8,12},{9,13},{10,... | collective-permute-start | bytes 393224 | tf_op jit(solution)/shard_map/ppermute | solution.py:643
  24.3 1.6 %collective-permute-start.4 = (bf16[256,256]{1,0:T(8,128)(2,1)S(1)}, bf16[256,256]{1,0:T(8,128)(2,1)S(1)}, u32[]{:S(2)}, u32[]{:S(2)}) collective-permute-start(bf16[256,256]{1,0:T(8,128)(2,1)S(1)} %get-tuple-element.29), channel_id=1, source_target_pairs={{0,5},{1,4},{2,7},{3,6},{4,1},{5,0},{6,3},{7,2},{8,13},{9,12},{10,... | collective-permute-start | bytes 393224 | tf_op jit(solution)/shard_map/ppermute | solution.py:643
  25.9 0.0 collective-permute-done.7.refs_1_
  25.9 0.7 %collective-permute-start.5 = (bf16[256,256]{1,0:T(8,128)(2,1)S(1)}, bf16[256,256]{1,0:T(8,128)(2,1)S(1)}, u32[]{:S(2)}, u32[]{:S(2)}) collective-permute-start(bf16[256,256]{1,0:T(8,128)(2,1)S(1)} %get-tuple-element.30), channel_id=1, source_target_pairs={{0,6},{1,7},{2,4},{3,5},{4,2},{5,3},{6,0},{7,1},{8,14},{9,15},{10,... | collective-permute-start | bytes 393224 | tf_op jit(solution)/shard_map/ppermute | solution.py:643
  26.6 3.2 %collective-permute-done.8.refs_2_ = bf16[304,256]{1,0:T(8,128)(2,1)S(1)} collective-permute-done((bf16[304,256]{1,0:T(8,128)(2,1)S(1)}, bf16[304,256]{1,0:T(8,128)(2,1)S(1)}, u32[]{:S(2)}, u32[]{:S(2)}) %collective-permute-start.8) | collective-permute-done | bytes 155680 | tf_op jit(solution)/shard_map/ppermute | solution.py:643
  29.8 0.0 collective-permute-start.6
  29.8 0.0 copy-done.1
  29.8 1.1 %shard_map.96.refs_5_.refs_8_ = bf16[2,768,256]{2,1,0:T(8,128)(2,1)S(1)} custom-call(s32[2]{0:T(128)S(1)} %pad_add_fusion.ids_ref, bf16[2,32,288]{2,1,0:T(8,128)(2,1)S(1)} %bitcast.7), custom_call_target="tpu_custom_call" | custom-call | flops 1000 | bytes 1000 | tf_op jit(solution)/shard_map/pallas_call | solution.py:149
  31.0 1.2 %collective-permute-done.9.refs_3_ = bf16[304,256]{1,0:T(8,128)(2,1)S(1)} collective-permute-done((bf16[304,256]{1,0:T(8,128)(2,1)S(1)}, bf16[304,256]{1,0:T(8,128)(2,1)S(1)}, u32[]{:S(2)}, u32[]{:S(2)}) %collective-permute-start.9) | collective-permute-done | bytes 155680 | tf_op jit(solution)/shard_map/ppermute | solution.py:643
  32.1 1.9 %shard_map.95.refs_4_.refs_7_ = f32[2048,256]{1,0:T(8,128)S(1)} custom-call(s32[2]{0:T(128)S(1)} %pad_add_fusion.ids_ref, bf16[304,256]{1,0:T(8,128)(2,1)S(1)} %get-tuple-element.32.refs_0_, bf16[304,256]{1,0:T(8,128)(2,1)S(1)} %collective-permute-done.7.refs_1_, bf16[304,256]{1,0:T(8,128)(2,1)S(1)} %collective-permute-done.8.refs_2_, ...), custom_call_target="tpu_custom_call" | custom-call | flops 1000 | bytes 1000 | tf_op jit(solution)/shard_map/pallas_call | solution.py:421
  34.0 0.0 copy-done.5
  34.1 2.0 %shard_map.97 = (bf16[8,4,4096]{2,1,0:T(4,128)(2,1)S(1)}, bf16[512,256]{1,0:T(8,128)(2,1)S(1)}, bf16[512,256]{1,0:T(8,128)(2,1)S(1)}) custom-call(s32[2]{0:T(128)S(1)} %pad_add_fusion.ids_ref, bf16[304,256]{1,0:T(8,128)(2,1)S(1)} %get-tuple-element.32.refs_0_, bf16[304,256]{1,0:T(8,128)(2,1)S(1)} %collective-permute-done.7.refs_1_, ...), custom_call_target="tpu_custom_call" | custom-call | flops 1000 | bytes 1000 | tf_op jit(solution)/shard_map/pallas_call | solution.py:616
  36.0 0.0 collective-permute-done.3.refs_0_
  36.0 5.6 %collective-permute-done.4.refs_1_ = bf16[256,256]{1,0:T(8,128)(2,1)S(1)} collective-permute-done((bf16[256,256]{1,0:T(8,128)(2,1)S(1)}, bf16[256,256]{1,0:T(8,128)(2,1)S(1)}, u32[]{:S(2)}, u32[]{:S(2)}) %collective-permute-start.4) | collective-permute-done | bytes 131104 | tf_op jit(solution)/shard_map/ppermute | solution.py:643
  41.7 3.0 %collective-permute-done.5.refs_2_ = bf16[256,256]{1,0:T(8,128)(2,1)S(1)} collective-permute-done((bf16[256,256]{1,0:T(8,128)(2,1)S(1)}, bf16[256,256]{1,0:T(8,128)(2,1)S(1)}, u32[]{:S(2)}, u32[]{:S(2)}) %collective-permute-start.5) | collective-permute-done | bytes 131104 | tf_op jit(solution)/shard_map/ppermute | solution.py:643
  44.6 2.9 %collective-permute-done.6.refs_3_ = bf16[256,256]{1,0:T(8,128)(2,1)S(1)} collective-permute-done((bf16[256,256]{1,0:T(8,128)(2,1)S(1)}, bf16[256,256]{1,0:T(8,128)(2,1)S(1)}, u32[]{:S(2)}, u32[]{:S(2)}) %collective-permute-start.6) | collective-permute-done | bytes 131104 | tf_op jit(solution)/shard_map/ppermute | solution.py:643
  47.6 4.4 %shard_map.98 = bf16[32,4,4096]{2,1,0:T(4,128)(2,1)} custom-call(s32[2]{0:T(128)S(1)} %pad_add_fusion.ids_ref, bf16[256,256]{1,0:T(8,128)(2,1)S(1)} %collective-permute-done.3.refs_0_, bf16[256,256]{1,0:T(8,128)(2,1)S(1)} %collective-permute-done.4.refs_1_, bf16[256,256]{1,0:T(8,128)(2,1)S(1)} %collective-permute-done.5.refs_2_, ...), custom_call_target="tpu_custom_call" | custom-call | flops 1000 | bytes 1000 | tf_op jit(solution)/shard_map/pallas_call | solution.py:625
Async XLA Ops:
  0.1 1.2 %copy-start = (bf16[4,4,32768]{2,1,0:T(4,128)(2,1)S(1)}, bf16[4,4,32768]{2,1,0:T(4,128)(2,1)}, u32[]{:S(2)}) copy-start(bf16[4,4,32768]{2,1,0:T(4,128)(2,1)} %field_ref.1) | copy-start | bytes 3145732
  2.4 11.2 %collective-permute-start.1 = (bf16[3,4,128,256]{3,2,1,0:T(8,128)(2,1)S(1)}, bf16[3,4,128,256]{3,2,1,0:T(8,128)(2,1)S(1)}, u32[]{:S(2)}, u32[]{:S(2)}) collective-permute-start(bf16[3,4,128,256]{3,2,1,0:T(8,128)(2,1)S(1)} %get-tuple-element.24), channel_id=1, source_target_pairs={{0,8},{8,0},{16,24},{24,16},{1,9},{9,1},{17,25},{25,17},{2,10},{10... | collective-permute-start | bytes 2359304 | tf_op jit(solution)/shard_map/ppermute | solution.py:663
  3.2 13.8 %collective-permute-start = (bf16[3,4,128,256]{3,2,1,0:T(8,128)(2,1)S(1)}, bf16[3,4,128,256]{3,2,1,0:T(8,128)(2,1)S(1)}, u32[]{:S(2)}, u32[]{:S(2)}) collective-permute-start(bf16[3,4,128,256]{3,2,1,0:T(8,128)(2,1)S(1)} %get-tuple-element.23), channel_id=1, source_target_pairs={{8,16},{16,8},{9,17},{17,9},{10,18},{18,10},{11,19},{19,11},{12,20... | collective-permute-start | bytes 2359304 | tf_op jit(solution)/shard_map/ppermute | solution.py:662
  6.2 0.8 %copy-start.2 = (bf16[512,32]{0,1:T(8,128)(2,1)S(1)}, bf16[512,32]{0,1:T(8,128)(2,1)}, u32[]{:S(2)}) copy-start(bf16[512,32]{0,1:T(8,128)(2,1)} %param.15) | copy-start | bytes 98308
  7.0 0.7 %copy-start.3 = (f32[7,7,32]{2,1,0:T(8,128)S(1)}, f32[7,7,32]{2,1,0:T(8,128)}, u32[]{:S(2)}) copy-start(f32[7,7,32]{2,1,0:T(8,128)} %depth_ref.1) | copy-start | bytes 18820
  7.7 0.7 %copy-start.4 = (bf16[32,32]{1,0:T(8,128)(2,1)S(1)}, bf16[32,32]{1,0:T(8,128)(2,1)}, u32[]{:S(2)}) copy-start(bf16[32,32]{1,0:T(8,128)(2,1)} %point_ref.1) | copy-start | bytes 6148
  8.4 0.7 %copy-start.6 = (s32[512,1]{0,1:T(1,128)S(1)}, s32[512,1]{0,1:T(1,128)}, u32[]{:S(2)}) copy-start(s32[512,1]{0,1:T(1,128)} %param.16) | copy-start | bytes 6148
  9.1 0.7 %copy-start.7 = (s32[512]{0:T(512)S(1)}, s32[512]{0:T(512)}, u32[]{:S(2)}) copy-start(s32[512]{0:T(512)} %param.17) | copy-start | bytes 6148
  11.3 5.7 %collective-permute-start.2 = (bf16[4,48,128]{2,1,0:T(8,128)(2,1)S(1)}, bf16[4,48,128]{2,1,0:T(8,128)(2,1)S(1)}, u32[]{:S(2)}, u32[]{:S(2)}) collective-permute-start(bf16[4,48,128]{2,1,0:T(8,128)(2,1)S(1)} %get-tuple-element.27), channel_id=1, source_target_pairs={{0,4},{1,5},{2,6},{3,7},{4,0},{5,1},{6,2},{7,3},{8,12},{9,13},{10,... | collective-permute-start | bytes 147464 | tf_op jit(solution)/shard_map/ppermute | solution.py:643
  13.7 3.3 %copy-start.8 = (f32[32]{0:T(128)S(1)}, f32[32]{0:T(128)}, u32[]{:S(2)}) copy-start(f32[32]{0:T(128)} %param.12) | copy-start | bytes 388
  17.0 12.8 %copy-start.1 = (bf16[2,288,32]{1,2,0:T(8,128)(2,1)S(1)}, bf16[2,288,32]{1,2,0:T(8,128)(2,1)}, u32[]{:S(2)}) copy-start(bf16[2,288,32]{1,2,0:T(8,128)(2,1)} %param.13) | copy-start | bytes 110596
  19.8 14.2 %copy-start.5 = (f32[2,32]{1,0:T(2,128)S(1)}, f32[2,32]{1,0:T(2,128)}, u32[]{:S(2)}) copy-start(f32[2,32]{1,0:T(2,128)} %refs_9_.1) | copy-start | bytes 772
  19.8 6.0 %collective-permute-start.7 = (bf16[304,256]{1,0:T(8,128)(2,1)S(1)}, bf16[304,256]{1,0:T(8,128)(2,1)S(1)}, u32[]{:S(2)}, u32[]{:S(2)}) collective-permute-start(bf16[304,256]{1,0:T(8,128)(2,1)S(1)} %get-tuple-element.33), channel_id=1, source_target_pairs={{0,1},{1,0},{2,3},{3,2},{4,5},{5,4},{6,7},{7,6},{8,9},{9,8},{10,11... | collective-permute-start | bytes 466952 | tf_op jit(solution)/shard_map/ppermute | solution.py:643
  21.1 8.7 %collective-permute-start.8 = (bf16[304,256]{1,0:T(8,128)(2,1)S(1)}, bf16[304,256]{1,0:T(8,128)(2,1)S(1)}, u32[]{:S(2)}, u32[]{:S(2)}) collective-permute-start(bf16[304,256]{1,0:T(8,128)(2,1)S(1)} %get-tuple-element.34), channel_id=1, source_target_pairs={{0,2},{1,3},{2,0},{3,1},{4,6},{5,7},{6,4},{7,5},{8,10},{9,11},{10,... | collective-permute-start | bytes 466952 | tf_op jit(solution)/shard_map/ppermute | solution.py:643
  21.3 10.9 %collective-permute-start.9 = (bf16[304,256]{1,0:T(8,128)(2,1)S(1)}, bf16[304,256]{1,0:T(8,128)(2,1)S(1)}, u32[]{:S(2)}, u32[]{:S(2)}) collective-permute-start(bf16[304,256]{1,0:T(8,128)(2,1)S(1)} %get-tuple-element.35), channel_id=1, source_target_pairs={{0,3},{1,2},{2,1},{3,0},{4,7},{5,6},{6,5},{7,4},{8,11},{9,10},{10,... | collective-permute-start | bytes 466952 | tf_op jit(solution)/shard_map/ppermute | solution.py:643
  22.5 13.5 %collective-permute-start.3 = (bf16[256,256]{1,0:T(8,128)(2,1)S(1)}, bf16[256,256]{1,0:T(8,128)(2,1)S(1)}, u32[]{:S(2)}, u32[]{:S(2)}) collective-permute-start(bf16[256,256]{1,0:T(8,128)(2,1)S(1)} %get-tuple-element.28), channel_id=1, source_target_pairs={{0,4},{1,5},{2,6},{3,7},{4,0},{5,1},{6,2},{7,3},{8,12},{9,13},{10,... | collective-permute-start | bytes 393224 | tf_op jit(solution)/shard_map/ppermute | solution.py:643
  24.3 17.4 %collective-permute-start.4 = (bf16[256,256]{1,0:T(8,128)(2,1)S(1)}, bf16[256,256]{1,0:T(8,128)(2,1)S(1)}, u32[]{:S(2)}, u32[]{:S(2)}) collective-permute-start(bf16[256,256]{1,0:T(8,128)(2,1)S(1)} %get-tuple-element.29), channel_id=1, source_target_pairs={{0,5},{1,4},{2,7},{3,6},{4,1},{5,0},{6,3},{7,2},{8,13},{9,12},{10,... | collective-permute-start | bytes 393224 | tf_op jit(solution)/shard_map/ppermute | solution.py:643
  25.9 18.8 %collective-permute-start.5 = (bf16[256,256]{1,0:T(8,128)(2,1)S(1)}, bf16[256,256]{1,0:T(8,128)(2,1)S(1)}, u32[]{:S(2)}, u32[]{:S(2)}) collective-permute-start(bf16[256,256]{1,0:T(8,128)(2,1)S(1)} %get-tuple-element.30), channel_id=1, source_target_pairs={{0,6},{1,7},{2,4},{3,5},{4,2},{5,3},{6,0},{7,1},{8,14},{9,15},{10,... | collective-permute-start | bytes 393224 | tf_op jit(solution)/shard_map/ppermute | solution.py:643
  29.8 17.8 %collective-permute-start.6 = (bf16[256,256]{1,0:T(8,128)(2,1)S(1)}, bf16[256,256]{1,0:T(8,128)(2,1)S(1)}, u32[]{:S(2)}, u32[]{:S(2)}) collective-permute-start(bf16[256,256]{1,0:T(8,128)(2,1)S(1)} %get-tuple-element.31), channel_id=1, source_target_pairs={{0,7},{1,6},{2,5},{3,4},{4,3},{5,2},{6,1},{7,0},{8,15},{9,14},{10,... | collective-permute-start | bytes 393224 | tf_op jit(solution)/shard_map/ppermute | solution.py:643

commit v5 on v4

--- a/solution.py
+++ b/solution.py
@@ -36,7 +36,8 @@
 
 
 def gelu(x):
-    return 0.5 * x * (1.0 + jnp.tanh(0.7978845608028654 * (x + 0.044715 * (x * x * x))))
+    half = 0.5 * x
+    return half + half * jnp.tanh(x * (0.7978845608028654 + 0.035677408136300125 * (x * x)))
 
 
 def swap_matrix(outer, inner):
@@ -464,36 +465,48 @@
 def layer_step(held, base, first, last, block, weight, bias):
     taps = [held[(first - base + k) * block : (last - base + k) * block] for k in range(TAPS)]
     total = jnp.dot(jnp.concatenate(taps, axis=1), weight, preferred_element_type=F32)
-    center = held[(first - base + 1) * block : (last - base + 1) * block].astype(F32)
-    return center + gelu(total + bias)
-
-
-def put_groups(out_ref, value, height, block, place_of):
     rows = block // QUAD
-    across = rows // height
-    count = max(1, 256 // block)
-    size = QUAD * height
-    swap = swap_matrix(count * size, across)
-    for g in range(0, value.shape[0] // block, count):
-        pieces = []
-        for n in range(g, g + count):
-            tile = lambda q, t: value[
-                n * block + q * rows : n * block + (q + 1) * rows, t * HALF : (t + 1) * HALF
-            ]
-            for t in range(2):
-                sides = [swap_halves(tile(2 * h, t), tile(2 * h + 1, t)) for h in range(2)]
-                for level in range(2):
-                    pieces.append(jnp.concatenate([side[level] for side in sides], axis=1))
-        turned = jnp.dot(
-            swap, jnp.concatenate(pieces, axis=0).astype(BF16), preferred_element_type=F32
-        ).astype(BF16)
-        for n in range(count):
-            at = place_of(g + n) * QUAD
-            for s in range(across):
-                start = (s * count + n) * size
-                out_ref[pl.ds(at, QUAD), :, s * SL : (s + 1) * SL] = turned[
-                    start : start + size
-                ].reshape(QUAD, height, SL)
+    start = (first - base + 1) * block
+    for n in range(0, (last - first) * block, rows):
+        center = held[start + n : start + n + rows].astype(F32)
+        yield n, center + gelu(total[n : n + rows] + bias)
+
+
+def layer_store(out, at, values):
+    for n, value in values:
+        out[at + n : at + n + value.shape[0]] = value.astype(BF16)
+
+
+def tile_matrix(height, across):
+    size = 2 * height * across
+    row = lax.broadcasted_iota(jnp.int32, (size, size), 0)
+    column = lax.broadcasted_iota(jnp.int32, (size, size), 1)
+    tile = row // height % 4
+    segment = row // (4 * height) * 2 + tile // 2
+    wanted = (tile % 2 * height + row % height) * across + segment
+    return (column == wanted).astype(BF16)
+
+
+def put_groups(out_ref, values, source_ref, first, height, block, place_of):
+    rows = block // QUAD
+    turn = tile_matrix(height, rows // height)
+    parts, halves = [], [[], []]
+    for n, value in values:
+        value = value + source_ref[first * block + n : first * block + n + rows]
+        parts.append([value[:, :HALF], value[:, HALF:]])
+        if len(parts) == QUAD:
+            for h in range(2):
+                for t in range(2):
+                    pair = swap_halves(parts[2 * h][t], parts[2 * h + 1][t])
+                    halves[h] += [one.astype(BF16) for one in pair]
+            parts = []
+    stacked = jnp.concatenate([jnp.concatenate(half, axis=1) for half in halves], axis=0)
+    turned = jnp.dot(turn, stacked, preferred_element_type=F32).astype(BF16)
+    for n in range(len(halves[0]) // QUAD):
+        at = place_of(n) * QUAD
+        for z in range(QUAD):
+            lane = (n * QUAD + z) * HALF
+            out_ref[at + z] = turned[:, lane : lane + HALF].reshape(out_ref.shape[1:])
 
 
 def lane_biases(bias_ref):
@@ -518,19 +531,13 @@
     place_pieces(tiles, ids_ref, piece_refs, held, 1, block)
     kept_ref[...] = held[(groups - 1) * block : (groups + 1) * block]
     for first, last in chunks(0, groups - 1, 2):
-        value = layer_step(held, 0, first, last, block, weight_ref[0], bias[0])
-        step[(first + 1) * block : (last + 1) * block] = value.astype(BF16)
+        values = layer_step(held, 0, first, last, block, weight_ref[0], bias[0])
+        layer_store(step, (first + 1) * block, values)
     later_ref[...] = step[(groups - 2) * block : groups * block]
     for first, last in chunks(0, groups - 2, 2):
-        value = layer_step(step, 0, first, last, block, weight_ref[1], bias[1])
-        value = value + source_ref[first * block : last * block]
-        put_groups(
-            out_ref,
-            value,
-            height,
-            block,
-            lambda n: turned_index(ids_ref, tiles, first + n, groups - 2),
-        )
+        values = layer_step(step, 0, first, last, block, weight_ref[1], bias[1])
+        place_of = lambda n: turned_index(ids_ref, tiles, first + n, groups - 2)
+        put_groups(out_ref, values, source_ref, first, height, block, place_of)
 
 
 def far_kernel(tiles, height, ids_ref, *refs):
@@ -551,13 +558,12 @@
     step[(half + 3) * block :] = jnp.zeros((block, SL), BF16)
     place_pieces(tiles, ids_ref, piece_refs, held, 2, block)
     for first, last in chunks(half - 1, groups, 3):
-        value = layer_step(held, half - 1, first, last, block, weight_ref[0], bias[0])
-        step[(first - half + 3) * block : (last - half + 3) * block] = value.astype(BF16)
+        values = layer_step(held, half - 1, first, last, block, weight_ref[0], bias[0])
+        layer_store(step, (first - half + 3) * block, values)
     for first, last in chunks(half - 2, groups, 2):
-        value = layer_step(step, half - 2, first, last, block, weight_ref[1], bias[1])
-        value = value + source_ref[first * block : last * block]
+        values = layer_step(step, half - 2, first, last, block, weight_ref[1], bias[1])
         place_of = lambda n: turned_index(ids_ref, tiles, first + n, groups)
-        put_groups(result, value, height, block, place_of)
+        put_groups(result, values, source_ref, first, height, block, place_of)
         for n in range(last - first):
             span = pl.ds(place_of(n) * QUAD, QUAD)
             copies.append(
@@ -586,10 +592,15 @@
             for n, lanes in enumerate(level_lanes(values)):
                 at = (group + 1) * block + (2 * h + n) * rows
                 held[at : at + rows] = lanes.astype(BF16)
-    value = layer_step(held, 0, 0, groups, block, weight_ref[0], bias[0])
-    step[block : (groups + 1) * block] = value.astype(BF16)
-    value = layer_step(step, 0, 0, groups, block, weight_ref[1], bias[1])
-    put_groups(out_ref, value + source_ref[...], height, block, lambda n: n)
+    layer_store(step, block, layer_step(held, 0, 0, groups, block, weight_ref[0], bias[0]))
+    values = layer_step(step, 0, 0, groups, block, weight_ref[1], bias[1])
+    put_groups(out_ref, values, source_ref, 0, height, block, lambda n: n)
+
+
+def in_order(out, height):
+    levels, blocks, rows, lanes = out.shape
+    out = out.reshape(levels, blocks, rows // height, height, lanes)
+    return jnp.transpose(out, (0, 3, 1, 2, 4)).reshape(levels, height, -1)
 
 
 def vertical(ids, close, far, source, weight, bias, levels, height, tiles):
@@ -601,9 +612,10 @@
     lanes = rows // height * SL
     buffer = lambda count: pltpu.VMEM((count * block, SL), BF16)
     array = lambda count: jax.ShapeDtypeStruct((count * block, SL), BF16)
-    result = lambda count: jax.ShapeDtypeStruct((count, height, lanes), BF16)
+    kind = (lanes // (4 * HALF), 4 * height, HALF)
+    result = lambda count: jax.ShapeDtypeStruct((count, *kind), BF16)
     if not far:
-        return pl.pallas_call(
+        out = pl.pallas_call(
             functools.partial(whole_kernel, height),
             in_specs=[smem] + [full] * 4,
             out_specs=full,
@@ -612,6 +624,7 @@
             compiler_params=params(),
             cost_estimate=cost(1000, 1000),
         )(ids, *close, source, weight, bias)
+        return in_order(out, height)
     half = groups // 2
     early, kept, later = pl.pallas_call(
         functools.partial(near_kernel, tiles, height),
@@ -622,7 +635,7 @@
         compiler_params=params(),
         cost_estimate=cost(1000, 1000),
     )(ids, *close, source, weight, bias)
-    return pl.pallas_call(
+    out = pl.pallas_call(
         functools.partial(far_kernel, tiles, height),
         in_specs=[smem] + [full] * (len(far) + 6),
         out_specs=pl.BlockSpec(memory_space=pl.ANY),
@@ -630,12 +643,13 @@
         scratch_shapes=[
             buffer(half + 3),
             buffer(half + 4),
-            pltpu.VMEM((levels, height, lanes), BF16),
+            pltpu.VMEM((levels, *kind), BF16),
             pltpu.SemaphoreType.DMA((groups + 1,)),
         ],
         compiler_params=params(),
         cost_estimate=cost(1000, 1000),
     )(ids, *far, early, kept, later, source, weight, bias)
+    return in_order(out, height)
 
 
 def exchange(block, distance):

time: 52.9 us -> 52.8 us (level)
  no operation moved by 1% of the time
where the time goes in v5:
time: 52.8 us; the launch traced here: 51.9 us
  Pallas kernels  18 us (34%)
  waiting for transfers between devices  16 us (30%)
  starting transfers between devices  12.9 us (24%)
  local copies, waits for them, and re-layouts  4.8 us (9%)
    ppermute x8, waiting for transfers between devices, exchange(): lax.ppermute(block, 'cols', [(i, i ^ distance) for i in range(count)])  16 us
    ppermute x8, starting transfers between devices, exchange(): lax.ppermute(block, 'cols', [(i, i ^ distance) for i in range(count)])  9.14 us
    unnamed x18, local copies, waits for them, and re-layouts  4.8 us
    pallas_call x1, Pallas kernels, vertical(): pl.pallas_call(functools.partial(far_kernel, tiles, height), in_specs=[sm...  4.31 us
    pallas_call x1, Pallas kernels, early_horizontal(): pl.pallas_call(early_kernel, in_specs=[pl.BlockSpec(memory_space=pltpu.SM...  3.31 us
    ppermute x1, starting transfers between devices, body(): cross = lax.ppermute(cross, 'rows', beyond)  3.02 us
    pallas_call x1, Pallas kernels, finish_horizontal(): pl.pallas_call(finish_kernel, in_specs=[pl.BlockSpec(memory_space=pltpu.S...  2.75 us
    pallas_call x1, Pallas kernels, vertical(): pl.pallas_call(functools.partial(near_kernel, tiles, height), in_specs=[s...  1.95 us
  transfers between devices with their start and end apart: 10, of which 5 were waited for; matrix products, arithmetic and copies ran while one was open for 0% of the time, Pallas kernels for 19%

profile of v5, /device:TPU:9, one launch (start us, length us, event | category | flops | bytes accessed | tf_op | source)
XLA Modules:
  0.0 51.9 jit_solution(12659201267470618316)
XLA Ops:
  0.0 0.1 pad_add_fusion.ids_ref
  0.1 0.0 copy-start
  0.1 1.2 %copy-done = bf16[4,4,32768]{2,1,0:T(4,128)(2,1)S(1)} copy-done((bf16[4,4,32768]{2,1,0:T(4,128)(2,1)S(1)}, bf16[4,4,32768]{2,1,0:T(4,128)(2,1)}, u32[]{:S(2)}) %copy-start) | copy-done | bytes 1048600
  1.3 1.1 %shard_map.91 = (bf16[4,4,128,256]{3,2,1,0:T(8,128)(2,1)S(1)}, bf16[3,4,128,256]{3,2,1,0:T(8,128)(2,1)S(1)}, bf16[3,4,128,256]{3,2,1,0:T(8,128)(2,1)S(1)}) custom-call(s32[2]{0:T(128)S(1)} %pad_add_fusion.ids_ref, bf16[4,4,32768]{2,1,0:T(4,128)(2,1)S(1)} %copy-done), custom_call_target="tpu_custom_call" | custom-call | flops 268435456 | bytes 4194304 | tf_op jit(solution)/shard_map/pallas_call | solution.py:75
  2.4 0.8 %collective-permute-start.1 = (bf16[3,4,128,256]{3,2,1,0:T(8,128)(2,1)S(1)}, bf16[3,4,128,256]{3,2,1,0:T(8,128)(2,1)S(1)}, u32[]{:S(2)}, u32[]{:S(2)}) collective-permute-start(bf16[3,4,128,256]{3,2,1,0:T(8,128)(2,1)S(1)} %get-tuple-element.24), channel_id=1, source_target_pairs={{0,8},{8,0},{16,24},{24,16},{1,9},{9,1},{17,25},{25,17},{2,10},{10... | collective-permute-start | bytes 2359304 | tf_op jit(solution)/shard_map/ppermute | solution.py:677
  3.2 3.0 %collective-permute-start = (bf16[3,4,128,256]{3,2,1,0:T(8,128)(2,1)S(1)}, bf16[3,4,128,256]{3,2,1,0:T(8,128)(2,1)S(1)}, u32[]{:S(2)}, u32[]{:S(2)}) collective-permute-start(bf16[3,4,128,256]{3,2,1,0:T(8,128)(2,1)S(1)} %get-tuple-element.23), channel_id=1, source_target_pairs={{8,16},{16,8},{9,17},{17,9},{10,18},{18,10},{11,19},{19,11},{12,20... | collective-permute-start | bytes 2359304 | tf_op jit(solution)/shard_map/ppermute | solution.py:676
  6.2 0.0 copy-start.2
  6.2 0.7 %copy-done.2 = bf16[512,32]{0,1:T(8,128)(2,1)S(1)} copy-done((bf16[512,32]{0,1:T(8,128)(2,1)S(1)}, bf16[512,32]{0,1:T(8,128)(2,1)}, u32[]{:S(2)}) %copy-start.2) | copy-done | bytes 32792
  7.0 0.0 copy-start.3
  7.0 0.7 %copy-done.3 = f32[7,7,32]{2,1,0:T(8,128)S(1)} copy-done((f32[7,7,32]{2,1,0:T(8,128)S(1)}, f32[7,7,32]{2,1,0:T(8,128)}, u32[]{:S(2)}) %copy-start.3) | copy-done | bytes 6296
  7.7 0.0 copy-start.4
  7.7 0.7 %copy-done.4 = bf16[32,32]{1,0:T(8,128)(2,1)S(1)} copy-done((bf16[32,32]{1,0:T(8,128)(2,1)S(1)}, bf16[32,32]{1,0:T(8,128)(2,1)}, u32[]{:S(2)}) %copy-start.4) | copy-done | bytes 2072
  8.4 0.0 copy-start.6
  8.4 0.7 %copy-done.6 = s32[512,1]{0,1:T(1,128)S(1)} copy-done((s32[512,1]{0,1:T(1,128)S(1)}, s32[512,1]{0,1:T(1,128)}, u32[]{:S(2)}) %copy-start.6) | copy-done | bytes 2072
  9.1 0.0 copy-start.7
  9.1 0.7 %copy-done.7 = s32[512]{0:T(512)S(1)} copy-done((s32[512]{0:T(512)S(1)}, s32[512]{0:T(512)}, u32[]{:S(2)}) %copy-start.7) | copy-done | bytes 2072
  9.8 1.5 %shard_map.92 = (bf16[4608,256]{1,0:T(8,128)(2,1)S(1)}, bf16[4,48,128]{2,1,0:T(8,128)(2,1)S(1)}, bf16[4,48,128]{2,1,0:T(8,128)(2,1)S(1)}) custom-call(s32[2]{0:T(128)S(1)} %pad_add_fusion.ids_ref, f32[7,7,32]{2,1,0:T(8,128)S(1)} %copy-done.3, bf16[32,32]{1,0:T(8,128)(2,1)S(1)} %copy-done.4, bf16[32,512]{1,0:T(8,128)(2,1)S(1)} %bitcast.13, ...), custom_call_target="tpu_custom_call" | custom-call | flops 1000 | bytes 1000 | tf_op jit(solution)/shard_map/pallas_call | solution.py:443
  11.3 2.4 %collective-permute-start.2 = (bf16[4,48,128]{2,1,0:T(8,128)(2,1)S(1)}, bf16[4,48,128]{2,1,0:T(8,128)(2,1)S(1)}, u32[]{:S(2)}, u32[]{:S(2)}) collective-permute-start(bf16[4,48,128]{2,1,0:T(8,128)(2,1)S(1)} %get-tuple-element.27), channel_id=1, source_target_pairs={{0,4},{1,5},{2,6},{3,7},{4,0},{5,1},{6,2},{7,3},{8,12},{9,13},{10,... | collective-permute-start | bytes 147464 | tf_op jit(solution)/shard_map/ppermute | solution.py:657
  13.7 0.0 collective-permute-done.1.pair_ref
  13.7 0.0 copy-start.8
  13.7 3.3 %shard_map.93.early_ref = f32[2,4,2,128,256]{4,3,2,1,0:T(8,128)S(1)} custom-call(s32[2]{0:T(128)S(1)} %pad_add_fusion.ids_ref, bf16[4,4,128,256]{3,2,1,0:T(8,128)(2,1)S(1)} %get-tuple-element.22.own_ref, bf16[3,4,128,256]{3,2,1,0:T(8,128)(2,1)S(1)} %collective-permute-done.1.pair_ref, bf16[4608,256]{1,0:T(8,128)(2,1)S(1)} %get-tuple-element.25.weight_ref), custom_call_target="tpu_custom_call" | custom-call | flops 1000 | bytes 1000 | tf_op jit(solution)/shard_map/pallas_call | solution.py:282
  17.0 0.0 collective-permute-done.2.rest_1_
  17.0 0.0 collective-permute-done.cross_ref
  17.0 0.0 copy-done.8
  17.0 0.0 copy-start.1
  17.0 2.7 %shard_map.94 = (bf16[304,256]{1,0:T(8,128)(2,1)S(1)}, bf16[304,256]{1,0:T(8,128)(2,1)S(1)}, bf16[304,256]{1,0:T(8,128)(2,1)S(1)}, bf16[304,256]{1,0:T(8,128)(2,...) custom-call(s32[2]{0:T(128)S(1)} %pad_add_fusion.ids_ref, ...), custom_call_target="tpu_custom_call" | custom-call | flops 1000 | bytes 1000 | tf_op jit(solution)/shard_map/pallas_call | solution.py:345
  19.8 0.0 copy-start.5
  19.8 1.3 %collective-permute-start.7 = (bf16[304,256]{1,0:T(8,128)(2,1)S(1)}, bf16[304,256]{1,0:T(8,128)(2,1)S(1)}, u32[]{:S(2)}, u32[]{:S(2)}) collective-permute-start(bf16[304,256]{1,0:T(8,128)(2,1)S(1)} %get-tuple-element.33), channel_id=1, source_target_pairs={{0,1},{1,0},{2,3},{3,2},{4,5},{5,4},{6,7},{7,6},{8,9},{9,8},{10,11... | collective-permute-start | bytes 466952 | tf_op jit(solution)/shard_map/ppermute | solution.py:657
  21.1 0.2 collective-permute-start.8
  21.3 1.2 %collective-permute-start.9 = (bf16[304,256]{1,0:T(8,128)(2,1)S(1)}, bf16[304,256]{1,0:T(8,128)(2,1)S(1)}, u32[]{:S(2)}, u32[]{:S(2)}) collective-permute-start(bf16[304,256]{1,0:T(8,128)(2,1)S(1)} %get-tuple-element.35), channel_id=1, source_target_pairs={{0,3},{1,2},{2,1},{3,0},{4,7},{5,6},{6,5},{7,4},{8,11},{9,10},{10,... | collective-permute-start | bytes 466952 | tf_op jit(solution)/shard_map/ppermute | solution.py:657
  22.5 1.8 %collective-permute-start.3 = (bf16[256,256]{1,0:T(8,128)(2,1)S(1)}, bf16[256,256]{1,0:T(8,128)(2,1)S(1)}, u32[]{:S(2)}, u32[]{:S(2)}) collective-permute-start(bf16[256,256]{1,0:T(8,128)(2,1)S(1)} %get-tuple-element.28), channel_id=1, source_target_pairs={{0,4},{1,5},{2,6},{3,7},{4,0},{5,1},{6,2},{7,3},{8,12},{9,13},{10,... | collective-permute-start | bytes 393224 | tf_op jit(solution)/shard_map/ppermute | solution.py:657
  24.3 1.6 %collective-permute-start.4 = (bf16[256,256]{1,0:T(8,128)(2,1)S(1)}, bf16[256,256]{1,0:T(8,128)(2,1)S(1)}, u32[]{:S(2)}, u32[]{:S(2)}) collective-permute-start(bf16[256,256]{1,0:T(8,128)(2,1)S(1)} %get-tuple-element.29), channel_id=1, source_target_pairs={{0,5},{1,4},{2,7},{3,6},{4,1},{5,0},{6,3},{7,2},{8,13},{9,12},{10,... | collective-permute-start | bytes 393224 | tf_op jit(solution)/shard_map/ppermute | solution.py:657
  25.8 0.0 collective-permute-done.7.refs_1_
  25.8 0.7 %collective-permute-start.5 = (bf16[256,256]{1,0:T(8,128)(2,1)S(1)}, bf16[256,256]{1,0:T(8,128)(2,1)S(1)}, u32[]{:S(2)}, u32[]{:S(2)}) collective-permute-start(bf16[256,256]{1,0:T(8,128)(2,1)S(1)} %get-tuple-element.30), channel_id=1, source_target_pairs={{0,6},{1,7},{2,4},{3,5},{4,2},{5,3},{6,0},{7,1},{8,14},{9,15},{10,... | collective-permute-start | bytes 393224 | tf_op jit(solution)/shard_map/ppermute | solution.py:657
  26.6 3.2 %collective-permute-done.8.refs_2_ = bf16[304,256]{1,0:T(8,128)(2,1)S(1)} collective-permute-done((bf16[304,256]{1,0:T(8,128)(2,1)S(1)}, bf16[304,256]{1,0:T(8,128)(2,1)S(1)}, u32[]{:S(2)}, u32[]{:S(2)}) %collective-permute-start.8) | collective-permute-done | bytes 155680 | tf_op jit(solution)/shard_map/ppermute | solution.py:657
  29.8 0.0 collective-permute-start.6
  29.8 0.0 copy-done.1
  29.8 1.1 %shard_map.96.refs_5_.refs_8_ = bf16[2,768,256]{2,1,0:T(8,128)(2,1)S(1)} custom-call(s32[2]{0:T(128)S(1)} %pad_add_fusion.ids_ref, bf16[2,32,288]{2,1,0:T(8,128)(2,1)S(1)} %bitcast.12), custom_call_target="tpu_custom_call" | custom-call | flops 1000 | bytes 1000 | tf_op jit(solution)/shard_map/pallas_call | solution.py:150
  31.0 1.2 %collective-permute-done.9.refs_3_ = bf16[304,256]{1,0:T(8,128)(2,1)S(1)} collective-permute-done((bf16[304,256]{1,0:T(8,128)(2,1)S(1)}, bf16[304,256]{1,0:T(8,128)(2,1)S(1)}, u32[]{:S(2)}, u32[]{:S(2)}) %collective-permute-start.9) | collective-permute-done | bytes 155680 | tf_op jit(solution)/shard_map/ppermute | solution.py:657
  32.1 1.9 %shard_map.95.refs_4_.refs_7_ = f32[2048,256]{1,0:T(8,128)S(1)} custom-call(s32[2]{0:T(128)S(1)} %pad_add_fusion.ids_ref, bf16[304,256]{1,0:T(8,128)(2,1)S(1)} %get-tuple-element.32.refs_0_, bf16[304,256]{1,0:T(8,128)(2,1)S(1)} %collective-permute-done.7.refs_1_, bf16[304,256]{1,0:T(8,128)(2,1)S(1)} %collective-permute-done.8.refs_2_, ...), custom_call_target="tpu_custom_call" | custom-call | flops 1000 | bytes 1000 | tf_op jit(solution)/shard_map/pallas_call | solution.py:422
  34.0 0.0 copy-done.5
  34.0 2.0 %shard_map.97 = (bf16[8,8,16,128]{3,2,1,0:T(8,128)(2,1)S(1)}, bf16[512,256]{1,0:T(8,128)(2,1)S(1)}, bf16[512,256]{1,0:T(8,128)(2,1)S(1)}) custom-call(s32[2]{0:T(128)S(1)} %pad_add_fusion.ids_ref, bf16[304,256]{1,0:T(8,128)(2,1)S(1)} %get-tuple-element.32.refs_0_, bf16[304,256]{1,0:T(8,128)(2,1)S(1)} %collective-permute-done.7.refs_1_, ...), custom_call_target="tpu_custom_call" | custom-call | flops 1000 | bytes 1000 | tf_op jit(solution)/shard_map/pallas_call | solution.py:629
  36.0 0.0 collective-permute-done.3.refs_0_
  36.0 5.6 %collective-permute-done.4.refs_1_ = bf16[256,256]{1,0:T(8,128)(2,1)S(1)} collective-permute-done((bf16[256,256]{1,0:T(8,128)(2,1)S(1)}, bf16[256,256]{1,0:T(8,128)(2,1)S(1)}, u32[]{:S(2)}, u32[]{:S(2)}) %collective-permute-start.4) | collective-permute-done | bytes 131104 | tf_op jit(solution)/shard_map/ppermute | solution.py:657
  41.6 3.0 %collective-permute-done.5.refs_2_ = bf16[256,256]{1,0:T(8,128)(2,1)S(1)} collective-permute-done((bf16[256,256]{1,0:T(8,128)(2,1)S(1)}, bf16[256,256]{1,0:T(8,128)(2,1)S(1)}, u32[]{:S(2)}, u32[]{:S(2)}) %collective-permute-start.5) | collective-permute-done | bytes 131104 | tf_op jit(solution)/shard_map/ppermute | solution.py:657
  44.6 2.9 %collective-permute-done.6.refs_3_ = bf16[256,256]{1,0:T(8,128)(2,1)S(1)} collective-permute-done((bf16[256,256]{1,0:T(8,128)(2,1)S(1)}, bf16[256,256]{1,0:T(8,128)(2,1)S(1)}, u32[]{:S(2)}, u32[]{:S(2)}) %collective-permute-start.6) | collective-permute-done | bytes 131104 | tf_op jit(solution)/shard_map/ppermute | solution.py:657
  47.6 4.3 %shard_map.98 = bf16[32,8,16,128]{3,2,1,0:T(8,128)(2,1)} custom-call(s32[2]{0:T(128)S(1)} %pad_add_fusion.ids_ref, bf16[256,256]{1,0:T(8,128)(2,1)S(1)} %collective-permute-done.3.refs_0_, bf16[256,256]{1,0:T(8,128)(2,1)S(1)} %collective-permute-done.4.refs_1_, bf16[256,256]{1,0:T(8,128)(2,1)S(1)} %collective-permute-done.5.refs_2_, ...), custom_call_target="tpu_custom_call" | custom-call | flops 1000 | bytes 1000 | tf_op jit(solution)/shard_map/pallas_call | solution.py:638
Async XLA Ops:
  0.1 1.2 %copy-start = (bf16[4,4,32768]{2,1,0:T(4,128)(2,1)S(1)}, bf16[4,4,32768]{2,1,0:T(4,128)(2,1)}, u32[]{:S(2)}) copy-start(bf16[4,4,32768]{2,1,0:T(4,128)(2,1)} %field_ref.1) | copy-start | bytes 3145732
  2.4 11.2 %collective-permute-start.1 = (bf16[3,4,128,256]{3,2,1,0:T(8,128)(2,1)S(1)}, bf16[3,4,128,256]{3,2,1,0:T(8,128)(2,1)S(1)}, u32[]{:S(2)}, u32[]{:S(2)}) collective-permute-start(bf16[3,4,128,256]{3,2,1,0:T(8,128)(2,1)S(1)} %get-tuple-element.24), channel_id=1, source_target_pairs={{0,8},{8,0},{16,24},{24,16},{1,9},{9,1},{17,25},{25,17},{2,10},{10... | collective-permute-start | bytes 2359304 | tf_op jit(solution)/shard_map/ppermute | solution.py:677
  3.2 13.8 %collective-permute-start = (bf16[3,4,128,256]{3,2,1,0:T(8,128)(2,1)S(1)}, bf16[3,4,128,256]{3,2,1,0:T(8,128)(2,1)S(1)}, u32[]{:S(2)}, u32[]{:S(2)}) collective-permute-start(bf16[3,4,128,256]{3,2,1,0:T(8,128)(2,1)S(1)} %get-tuple-element.23), channel_id=1, source_target_pairs={{8,16},{16,8},{9,17},{17,9},{10,18},{18,10},{11,19},{19,11},{12,20... | collective-permute-start | bytes 2359304 | tf_op jit(solution)/shard_map/ppermute | solution.py:676
  6.2 0.8 %copy-start.2 = (bf16[512,32]{0,1:T(8,128)(2,1)S(1)}, bf16[512,32]{0,1:T(8,128)(2,1)}, u32[]{:S(2)}) copy-start(bf16[512,32]{0,1:T(8,128)(2,1)} %param.15) | copy-start | bytes 98308
  7.0 0.7 %copy-start.3 = (f32[7,7,32]{2,1,0:T(8,128)S(1)}, f32[7,7,32]{2,1,0:T(8,128)}, u32[]{:S(2)}) copy-start(f32[7,7,32]{2,1,0:T(8,128)} %depth_ref.1) | copy-start | bytes 18820
  7.7 0.7 %copy-start.4 = (bf16[32,32]{1,0:T(8,128)(2,1)S(1)}, bf16[32,32]{1,0:T(8,128)(2,1)}, u32[]{:S(2)}) copy-start(bf16[32,32]{1,0:T(8,128)(2,1)} %point_ref.1) | copy-start | bytes 6148
  8.4 0.7 %copy-start.6 = (s32[512,1]{0,1:T(1,128)S(1)}, s32[512,1]{0,1:T(1,128)}, u32[]{:S(2)}) copy-start(s32[512,1]{0,1:T(1,128)} %param.16) | copy-start | bytes 6148
  9.1 0.7 %copy-start.7 = (s32[512]{0:T(512)S(1)}, s32[512]{0:T(512)}, u32[]{:S(2)}) copy-start(s32[512]{0:T(512)} %param.17) | copy-start | bytes 6148
  11.3 5.7 %collective-permute-start.2 = (bf16[4,48,128]{2,1,0:T(8,128)(2,1)S(1)}, bf16[4,48,128]{2,1,0:T(8,128)(2,1)S(1)}, u32[]{:S(2)}, u32[]{:S(2)}) collective-permute-start(bf16[4,48,128]{2,1,0:T(8,128)(2,1)S(1)} %get-tuple-element.27), channel_id=1, source_target_pairs={{0,4},{1,5},{2,6},{3,7},{4,0},{5,1},{6,2},{7,3},{8,12},{9,13},{10,... | collective-permute-start | bytes 147464 | tf_op jit(solution)/shard_map/ppermute | solution.py:657
  13.7 3.3 %copy-start.8 = (f32[32]{0:T(128)S(1)}, f32[32]{0:T(128)}, u32[]{:S(2)}) copy-start(f32[32]{0:T(128)} %param.12) | copy-start | bytes 388
  17.0 12.8 %copy-start.1 = (bf16[2,288,32]{1,2,0:T(8,128)(2,1)S(1)}, bf16[2,288,32]{1,2,0:T(8,128)(2,1)}, u32[]{:S(2)}) copy-start(bf16[2,288,32]{1,2,0:T(8,128)(2,1)} %param.13) | copy-start | bytes 110596
  19.8 14.2 %copy-start.5 = (f32[2,32]{1,0:T(2,128)S(1)}, f32[2,32]{1,0:T(2,128)}, u32[]{:S(2)}) copy-start(f32[2,32]{1,0:T(2,128)} %refs_9_.1) | copy-start | bytes 772
  19.8 6.0 %collective-permute-start.7 = (bf16[304,256]{1,0:T(8,128)(2,1)S(1)}, bf16[304,256]{1,0:T(8,128)(2,1)S(1)}, u32[]{:S(2)}, u32[]{:S(2)}) collective-permute-start(bf16[304,256]{1,0:T(8,128)(2,1)S(1)} %get-tuple-element.33), channel_id=1, source_target_pairs={{0,1},{1,0},{2,3},{3,2},{4,5},{5,4},{6,7},{7,6},{8,9},{9,8},{10,11... | collective-permute-start | bytes 466952 | tf_op jit(solution)/shard_map/ppermute | solution.py:657
  21.1 8.7 %collective-permute-start.8 = (bf16[304,256]{1,0:T(8,128)(2,1)S(1)}, bf16[304,256]{1,0:T(8,128)(2,1)S(1)}, u32[]{:S(2)}, u32[]{:S(2)}) collective-permute-start(bf16[304,256]{1,0:T(8,128)(2,1)S(1)} %get-tuple-element.34), channel_id=1, source_target_pairs={{0,2},{1,3},{2,0},{3,1},{4,6},{5,7},{6,4},{7,5},{8,10},{9,11},{10,... | collective-permute-start | bytes 466952 | tf_op jit(solution)/shard_map/ppermute | solution.py:657
  21.3 10.9 %collective-permute-start.9 = (bf16[304,256]{1,0:T(8,128)(2,1)S(1)}, bf16[304,256]{1,0:T(8,128)(2,1)S(1)}, u32[]{:S(2)}, u32[]{:S(2)}) collective-permute-start(bf16[304,256]{1,0:T(8,128)(2,1)S(1)} %get-tuple-element.35), channel_id=1, source_target_pairs={{0,3},{1,2},{2,1},{3,0},{4,7},{5,6},{6,5},{7,4},{8,11},{9,10},{10,... | collective-permute-start | bytes 466952 | tf_op jit(solution)/shard_map/ppermute | solution.py:657
  22.5 13.5 %collective-permute-start.3 = (bf16[256,256]{1,0:T(8,128)(2,1)S(1)}, bf16[256,256]{1,0:T(8,128)(2,1)S(1)}, u32[]{:S(2)}, u32[]{:S(2)}) collective-permute-start(bf16[256,256]{1,0:T(8,128)(2,1)S(1)} %get-tuple-element.28), channel_id=1, source_target_pairs={{0,4},{1,5},{2,6},{3,7},{4,0},{5,1},{6,2},{7,3},{8,12},{9,13},{10,... | collective-permute-start | bytes 393224 | tf_op jit(solution)/shard_map/ppermute | solution.py:657
  24.3 17.4 %collective-permute-start.4 = (bf16[256,256]{1,0:T(8,128)(2,1)S(1)}, bf16[256,256]{1,0:T(8,128)(2,1)S(1)}, u32[]{:S(2)}, u32[]{:S(2)}) collective-permute-start(bf16[256,256]{1,0:T(8,128)(2,1)S(1)} %get-tuple-element.29), channel_id=1, source_target_pairs={{0,5},{1,4},{2,7},{3,6},{4,1},{5,0},{6,3},{7,2},{8,13},{9,12},{10,... | collective-permute-start | bytes 393224 | tf_op jit(solution)/shard_map/ppermute | solution.py:657
  25.8 18.8 %collective-permute-start.5 = (bf16[256,256]{1,0:T(8,128)(2,1)S(1)}, bf16[256,256]{1,0:T(8,128)(2,1)S(1)}, u32[]{:S(2)}, u32[]{:S(2)}) collective-permute-start(bf16[256,256]{1,0:T(8,128)(2,1)S(1)} %get-tuple-element.30), channel_id=1, source_target_pairs={{0,6},{1,7},{2,4},{3,5},{4,2},{5,3},{6,0},{7,1},{8,14},{9,15},{10,... | collective-permute-start | bytes 393224 | tf_op jit(solution)/shard_map/ppermute | solution.py:657
  29.8 17.8 %collective-permute-start.6 = (bf16[256,256]{1,0:T(8,128)(2,1)S(1)}, bf16[256,256]{1,0:T(8,128)(2,1)S(1)}, u32[]{:S(2)}, u32[]{:S(2)}) collective-permute-start(bf16[256,256]{1,0:T(8,128)(2,1)S(1)} %get-tuple-element.31), channel_id=1, source_target_pairs={{0,7},{1,6},{2,5},{3,4},{4,3},{5,2},{6,1},{7,0},{8,15},{9,14},{10,... | collective-permute-start | bytes 393224 | tf_op jit(solution)/shard_map/ppermute | solution.py:657

commit v6 on v5

--- a/solution.py
+++ b/solution.py
@@ -47,7 +47,9 @@
     return (column == (row % outer) * inner + row // outer).astype(BF16)
 
 
-def segment_kernel(ids_ref, field_ref, own_ref, cross_ref, pair_ref):
+def segment_kernel(only_cross, ids_ref, field_ref, own_ref, halo_ref):
+    if only_cross:
+        own_ref, halo_ref = halo_ref, own_ref
     levels, height, lanes = field_ref.shape
     rows = levels * height
     group = 256 // rows
@@ -63,22 +65,24 @@
                 start = (z * height + y) * group
                 own_ref[y, z, g * group : (g + 1) * group] = got[start : start + group]
     odd = ids_ref[1] % 2
+    first = odd if only_cross else 1 - odd
     for y in range(3):
-        cross_ref[y] = own_ref[odd * (height - 3) + y]
-        pair_ref[y] = own_ref[(1 - odd) * (height - 3) + y]
-
-
-def to_segments(ids, field):
+        halo_ref[y] = own_ref[first * (height - 3) + y]
+
+
+def to_segments(ids, field, only_cross):
     levels, height, lanes = field.shape
     full = pl.BlockSpec(memory_space=pltpu.VMEM)
-    out = lambda n: jax.ShapeDtypeStruct((n, levels, lanes // SL, SL), BF16)
+    shape = lambda n: (n, levels, lanes // SL, SL)
+    out = lambda n: jax.ShapeDtypeStruct(shape(n), BF16)
     return pl.pallas_call(
-        segment_kernel,
+        functools.partial(segment_kernel, only_cross),
         in_specs=[pl.BlockSpec(memory_space=pltpu.SMEM), full],
-        out_specs=[full] * 3,
-        out_shape=[out(height), out(3), out(3)],
-        compiler_params=params(),
-        cost_estimate=cost(2 * levels * height * lanes * 256, 8 * levels * height * lanes),
+        out_specs=[full] if only_cross else [full] * 2,
+        out_shape=[out(3)] if only_cross else [out(height), out(3)],
+        scratch_shapes=[pltpu.VMEM(shape(height), BF16)] if only_cross else [],
+        compiler_params=params(),
+        cost_estimate=cost(1000, 1000),
     )(ids, field)
 
 
@@ -670,7 +674,9 @@
     bias = point_bias.reshape(1, C)
     if per % 16 == 0 and columns % 2 == 0 and bands % 2 == 0 and levels == QUAD and 256 % (levels * height) == 0:
         tiles = columns // 2
-        own, cross, pair = to_segments(ids, field)
+        (cross,) = to_segments(ids, field, True)
+        ids_after, _ = lax.optimization_barrier((ids, cross))
+        own, pair = to_segments(ids_after, field, False)
         inside = [(i, i ^ 1) for i in range(bands)]
         beyond = [(i, i + 1 if i % 2 else i - 1) for i in range(1, bands - 1)]
         cross = lax.ppermute(cross, "rows", beyond)

time: 52.8 us -> 49.8 us (0.943); the launches traced: 51.9 us -> 49.5 us
  local copies, waits for them, and re-layouts: 4.8 us -> 1.26 us
  starting transfers between devices: 12.9 us -> 15.1 us
  waiting for transfers between devices: 16 us -> 14 us
  Pallas kernels: 18 us -> 18.9 us
    ppermute x8, waiting for transfers between devices: 16 us -> 11 us  [exchange(): lax.ppermute(block, 'cols', [(i, i ^ distance) for i in range(count)])]
    unnamed x18, local copies, waits for them, and re-layouts: 4.8 us -> 1.26 us
    ppermute x1, waiting for transfers between devices: 0.01 us -> 2.99 us  [body(): cross = lax.ppermute(cross, 'rows', beyond)]
    ppermute x8, starting transfers between devices: 9.14 us -> 11.3 us  [exchange(): lax.ppermute(block, 'cols', [(i, i ^ distance) for i in range(count)])]
    pallas_call x1 -> x2, Pallas kernels: 1.11 us -> 2.01 us  [to_segments(): pl.pallas_call(functools.partial(segment_kernel, only_cross), in_specs=[p...]
  transfers between devices with their start and end apart: 10 -> 10, of which waited for: 5 -> 6; matrix products, arithmetic and copies ran while one was open for 0% -> 0% of each run, Pallas kernels for 19% -> 20%
where the time goes in v6:
time: 49.8 us; the launch traced here: 49.5 us
  Pallas kernels  18.9 us (38%)
  starting transfers between devices  15.1 us (30%)
  waiting for transfers between devices  14 us (28%)
  local copies, waits for them, and re-layouts  1.26 us (3%)
    ppermute x8, starting transfers between devices, exchange(): lax.ppermute(block, 'cols', [(i, i ^ distance) for i in range(count)])  11.3 us
    ppermute x8, waiting for transfers between devices, exchange(): lax.ppermute(block, 'cols', [(i, i ^ distance) for i in range(count)])  11 us
    pallas_call x1, Pallas kernels, vertical(): pl.pallas_call(functools.partial(far_kernel, tiles, height), in_specs=[sm...  4.31 us
    pallas_call x1, Pallas kernels, early_horizontal(): pl.pallas_call(early_kernel, in_specs=[pl.BlockSpec(memory_space=pltpu.SM...  3.31 us
    ppermute x1, starting transfers between devices, body(): cross = lax.ppermute(cross, 'rows', beyond)  3.02 us
    ppermute x1, waiting for transfers between devices, body(): cross = lax.ppermute(cross, 'rows', beyond)  2.99 us
    pallas_call x1, Pallas kernels, finish_horizontal(): pl.pallas_call(finish_kernel, in_specs=[pl.BlockSpec(memory_space=pltpu.S...  2.74 us
    pallas_call x2, Pallas kernels, to_segments(): pl.pallas_call(functools.partial(segment_kernel, only_cross), in_specs=[p...  2.01 us
  transfers between devices with their start and end apart: 10, of which 6 were waited for; matrix products, arithmetic and copies ran while one was open for 0% of the time, Pallas kernels for 20%

profile of v6, /device:TPU:9, one launch (start us, length us, event | category | flops | bytes accessed | tf_op | source)
XLA Modules:
  0.0 49.5 jit_solution(16614842166940216434)
XLA Ops:
  0.0 0.0 copy-start.6
  0.0 0.0 copy-start.7
  0.0 0.0 copy-start.4
  0.0 0.1 pad_add_fusion.ids_ref
  0.1 0.0 copy-start
  0.1 1.2 %copy-done = bf16[4,4,32768]{2,1,0:T(4,128)(2,1)S(1)} copy-done((bf16[4,4,32768]{2,1,0:T(4,128)(2,1)S(1)}, bf16[4,4,32768]{2,1,0:T(4,128)(2,1)}, u32[]{:S(2)}) %copy-start) | copy-done | bytes 1048600
  1.3 0.0 copy-start.2
  1.3 0.0 copy-start.3
  1.3 1.0 %shard_map.91 = bf16[3,4,128,256]{3,2,1,0:T(8,128)(2,1)S(1)} custom-call(s32[2]{0:T(128)S(1)} %pad_add_fusion.ids_ref, bf16[4,4,32768]{2,1,0:T(4,128)(2,1)S(1)} %copy-done), custom_call_target="tpu_custom_call" | custom-call | flops 1000 | bytes 1000 | tf_op jit(solution)/shard_map/pallas_call | solution.py:78
  2.3 1.0 %shard_map.92 = (bf16[4,4,128,256]{3,2,1,0:T(8,128)(2,1)S(1)}, bf16[3,4,128,256]{3,2,1,0:T(8,128)(2,1)S(1)}) custom-call(s32[2]{0:T(128)S(1)} %pad_add_fusion.ids_ref, bf16[4,4,32768]{2,1,0:T(4,128)(2,1)S(1)} %copy-done), custom_call_target="tpu_custom_call" | custom-call | flops 1000 | bytes 1000 | tf_op jit(solution)/shard_map/pallas_call | solution.py:78
  3.3 0.8 %collective-permute-start.1 = (bf16[3,4,128,256]{3,2,1,0:T(8,128)(2,1)S(1)}, bf16[3,4,128,256]{3,2,1,0:T(8,128)(2,1)S(1)}, u32[]{:S(2)}, u32[]{:S(2)}) collective-permute-start(bf16[3,4,128,256]{3,2,1,0:T(8,128)(2,1)S(1)} %get-tuple-element.24), channel_id=1, source_target_pairs={{0,8},{8,0},{16,24},{24,16},{1,9},{9,1},{17,25},{25,17},{2,10},{10... | collective-permute-start | bytes 2359304 | tf_op jit(solution)/shard_map/ppermute | solution.py:683
  4.1 3.0 %collective-permute-start = (bf16[3,4,128,256]{3,2,1,0:T(8,128)(2,1)S(1)}, bf16[3,4,128,256]{3,2,1,0:T(8,128)(2,1)S(1)}, u32[]{:S(2)}, u32[]{:S(2)}) collective-permute-start(bf16[3,4,128,256]{3,2,1,0:T(8,128)(2,1)S(1)} %shard_map.91), channel_id=1, source_target_pairs={{8,16},{16,8},{9,17},{17,9},{10,18},{18,10},{11,19},{19,11},{12,20... | collective-permute-start | bytes 2359304 | tf_op jit(solution)/shard_map/ppermute | solution.py:682
  7.1 0.0 copy-done.6
  7.1 0.0 copy-done.7
  7.1 0.0 copy-done.4
  7.2 0.0 copy-done.2
  7.2 0.0 copy-done.3
  7.2 1.5 %shard_map.93 = (bf16[4608,256]{1,0:T(8,128)(2,1)S(1)}, bf16[4,48,128]{2,1,0:T(8,128)(2,1)S(1)}, bf16[4,48,128]{2,1,0:T(8,128)(2,1)S(1)}) custom-call(s32[2]{0:T(128)S(1)} %pad_add_fusion.ids_ref, f32[7,7,32]{2,1,0:T(8,128)S(1)} %copy-done.3, bf16[32,32]{1,0:T(8,128)(2,1)S(1)} %copy-done.4, bf16[32,512]{1,0:T(8,128)(2,1)S(1)} %bitcast.13, ...), custom_call_target="tpu_custom_call" | custom-call | flops 1000 | bytes 1000 | tf_op jit(solution)/shard_map/pallas_call | solution.py:447
  8.7 2.4 %collective-permute-start.2 = (bf16[4,48,128]{2,1,0:T(8,128)(2,1)S(1)}, bf16[4,48,128]{2,1,0:T(8,128)(2,1)S(1)}, u32[]{:S(2)}, u32[]{:S(2)}) collective-permute-start(bf16[4,48,128]{2,1,0:T(8,128)(2,1)S(1)} %get-tuple-element.27), channel_id=1, source_target_pairs={{0,4},{1,5},{2,6},{3,7},{4,0},{5,1},{6,2},{7,3},{8,12},{9,13},{10,... | collective-permute-start | bytes 147464 | tf_op jit(solution)/shard_map/ppermute | solution.py:661
  11.1 0.0 collective-permute-done.1.pair_ref
  11.1 0.0 copy-start.8
  11.1 3.3 %shard_map.94.early_ref = f32[2,4,2,128,256]{4,3,2,1,0:T(8,128)S(1)} custom-call(s32[2]{0:T(128)S(1)} %pad_add_fusion.ids_ref, bf16[4,4,128,256]{3,2,1,0:T(8,128)(2,1)S(1)} %get-tuple-element.23.own_ref, bf16[3,4,128,256]{3,2,1,0:T(8,128)(2,1)S(1)} %collective-permute-done.1.pair_ref, bf16[4608,256]{1,0:T(8,128)(2,1)S(1)} %get-tuple-element.25.weight_ref), custom_call_target="tpu_custom_call" | custom-call | flops 1000 | bytes 1000 | tf_op jit(solution)/shard_map/pallas_call | solution.py:286
  14.4 0.0 collective-permute-done.2.rest_1_
  14.4 3.0 %collective-permute-done.cross_ref = bf16[3,4,128,256]{3,2,1,0:T(8,128)(2,1)S(1)} collective-permute-done((bf16[3,4,128,256]{3,2,1,0:T(8,128)(2,1)S(1)}, bf16[3,4,128,256]{3,2,1,0:T(8,128)(2,1)S(1)}, u32[]{:S(2)}, u32[]{:S(2)}) %collective-permute-start) | collective-permute-done | bytes 786464 | tf_op jit(solution)/shard_map/ppermute | solution.py:682
  17.4 0.0 copy-done.8
  17.4 0.0 copy-start.1
  17.4 2.7 %shard_map.95 = (bf16[304,256]{1,0:T(8,128)(2,1)S(1)}, bf16[304,256]{1,0:T(8,128)(2,1)S(1)}, bf16[304,256]{1,0:T(8,128)(2,1)S(1)}, bf16[304,256]{1,0:T(8,128)(2,...) custom-call(s32[2]{0:T(128)S(1)} %pad_add_fusion.ids_ref, ...), custom_call_target="tpu_custom_call" | custom-call | flops 1000 | bytes 1000 | tf_op jit(solution)/shard_map/pallas_call | solution.py:349
  20.1 0.0 copy-start.5
  20.2 1.3 %collective-permute-start.7 = (bf16[304,256]{1,0:T(8,128)(2,1)S(1)}, bf16[304,256]{1,0:T(8,128)(2,1)S(1)}, u32[]{:S(2)}, u32[]{:S(2)}) collective-permute-start(bf16[304,256]{1,0:T(8,128)(2,1)S(1)} %get-tuple-element.33), channel_id=1, source_target_pairs={{0,1},{1,0},{2,3},{3,2},{4,5},{5,4},{6,7},{7,6},{8,9},{9,8},{10,11... | collective-permute-start | bytes 466952 | tf_op jit(solution)/shard_map/ppermute | solution.py:661
  21.5 0.2 collective-permute-start.8
  21.6 1.2 %collective-permute-start.9 = (bf16[304,256]{1,0:T(8,128)(2,1)S(1)}, bf16[304,256]{1,0:T(8,128)(2,1)S(1)}, u32[]{:S(2)}, u32[]{:S(2)}) collective-permute-start(bf16[304,256]{1,0:T(8,128)(2,1)S(1)} %get-tuple-element.35), channel_id=1, source_target_pairs={{0,3},{1,2},{2,1},{3,0},{4,7},{5,6},{6,5},{7,4},{8,11},{9,10},{10,... | collective-permute-start | bytes 466952 | tf_op jit(solution)/shard_map/ppermute | solution.py:661
  22.9 2.3 %collective-permute-start.3 = (bf16[256,256]{1,0:T(8,128)(2,1)S(1)}, bf16[256,256]{1,0:T(8,128)(2,1)S(1)}, u32[]{:S(2)}, u32[]{:S(2)}) collective-permute-start(bf16[256,256]{1,0:T(8,128)(2,1)S(1)} %get-tuple-element.28), channel_id=1, source_target_pairs={{0,4},{1,5},{2,6},{3,7},{4,0},{5,1},{6,2},{7,3},{8,12},{9,13},{10,... | collective-permute-start | bytes 393224 | tf_op jit(solution)/shard_map/ppermute | solution.py:661
  25.2 1.0 %collective-permute-start.4 = (bf16[256,256]{1,0:T(8,128)(2,1)S(1)}, bf16[256,256]{1,0:T(8,128)(2,1)S(1)}, u32[]{:S(2)}, u32[]{:S(2)}) collective-permute-start(bf16[256,256]{1,0:T(8,128)(2,1)S(1)} %get-tuple-element.29), channel_id=1, source_target_pairs={{0,5},{1,4},{2,7},{3,6},{4,1},{5,0},{6,3},{7,2},{8,13},{9,12},{10,... | collective-permute-start | bytes 393224 | tf_op jit(solution)/shard_map/ppermute | solution.py:661
  26.2 0.0 collective-permute-done.7.refs_1_
  26.2 1.6 %collective-permute-start.5 = (bf16[256,256]{1,0:T(8,128)(2,1)S(1)}, bf16[256,256]{1,0:T(8,128)(2,1)S(1)}, u32[]{:S(2)}, u32[]{:S(2)}) collective-permute-start(bf16[256,256]{1,0:T(8,128)(2,1)S(1)} %get-tuple-element.30), channel_id=1, source_target_pairs={{0,6},{1,7},{2,4},{3,5},{4,2},{5,3},{6,0},{7,1},{8,14},{9,15},{10,... | collective-permute-start | bytes 393224 | tf_op jit(solution)/shard_map/ppermute | solution.py:661
  27.8 0.0 collective-permute-done.8.refs_2_
  27.8 1.3 %collective-permute-start.6 = (bf16[256,256]{1,0:T(8,128)(2,1)S(1)}, bf16[256,256]{1,0:T(8,128)(2,1)S(1)}, u32[]{:S(2)}, u32[]{:S(2)}) collective-permute-start(bf16[256,256]{1,0:T(8,128)(2,1)S(1)} %get-tuple-element.31), channel_id=1, source_target_pairs={{0,7},{1,6},{2,5},{3,4},{4,3},{5,2},{6,1},{7,0},{8,15},{9,14},{10,... | collective-permute-start | bytes 393224 | tf_op jit(solution)/shard_map/ppermute | solution.py:661
  29.1 0.0 copy-done.1
  29.1 1.1 %shard_map.97.refs_5_.refs_8_ = bf16[2,768,256]{2,1,0:T(8,128)(2,1)S(1)} custom-call(s32[2]{0:T(128)S(1)} %pad_add_fusion.ids_ref, bf16[2,32,288]{2,1,0:T(8,128)(2,1)S(1)} %bitcast.12), custom_call_target="tpu_custom_call" | custom-call | flops 1000 | bytes 1000 | tf_op jit(solution)/shard_map/pallas_call | solution.py:154
  30.3 0.3 collective-permute-done.9.refs_3_
  30.6 1.9 %shard_map.96.refs_4_.refs_7_ = f32[2048,256]{1,0:T(8,128)S(1)} custom-call(s32[2]{0:T(128)S(1)} %pad_add_fusion.ids_ref, bf16[304,256]{1,0:T(8,128)(2,1)S(1)} %get-tuple-element.32.refs_0_, bf16[304,256]{1,0:T(8,128)(2,1)S(1)} %collective-permute-done.7.refs_1_, bf16[304,256]{1,0:T(8,128)(2,1)S(1)} %collective-permute-done.8.refs_2_, ...), custom_call_target="tpu_custom_call" | custom-call | flops 1000 | bytes 1000 | tf_op jit(solution)/shard_map/pallas_call | solution.py:426
  32.4 0.0 copy-done.5
  32.5 2.0 %shard_map.98 = (bf16[8,8,16,128]{3,2,1,0:T(8,128)(2,1)S(1)}, bf16[512,256]{1,0:T(8,128)(2,1)S(1)}, bf16[512,256]{1,0:T(8,128)(2,1)S(1)}) custom-call(s32[2]{0:T(128)S(1)} %pad_add_fusion.ids_ref, bf16[304,256]{1,0:T(8,128)(2,1)S(1)} %get-tuple-element.32.refs_0_, bf16[304,256]{1,0:T(8,128)(2,1)S(1)} %collective-permute-done.7.refs_1_, ...), custom_call_target="tpu_custom_call" | custom-call | flops 1000 | bytes 1000 | tf_op jit(solution)/shard_map/pallas_call | solution.py:633
  34.4 3.2 %collective-permute-done.3.refs_0_ = bf16[256,256]{1,0:T(8,128)(2,1)S(1)} collective-permute-done((bf16[256,256]{1,0:T(8,128)(2,1)S(1)}, bf16[256,256]{1,0:T(8,128)(2,1)S(1)}, u32[]{:S(2)}, u32[]{:S(2)}) %collective-permute-start.3) | collective-permute-done | bytes 131104 | tf_op jit(solution)/shard_map/ppermute | solution.py:661
  37.7 2.8 %collective-permute-done.4.refs_1_ = bf16[256,256]{1,0:T(8,128)(2,1)S(1)} collective-permute-done((bf16[256,256]{1,0:T(8,128)(2,1)S(1)}, bf16[256,256]{1,0:T(8,128)(2,1)S(1)}, u32[]{:S(2)}, u32[]{:S(2)}) %collective-permute-start.4) | collective-permute-done | bytes 131104 | tf_op jit(solution)/shard_map/ppermute | solution.py:661
  40.5 2.7 %collective-permute-done.5.refs_2_ = bf16[256,256]{1,0:T(8,128)(2,1)S(1)} collective-permute-done((bf16[256,256]{1,0:T(8,128)(2,1)S(1)}, bf16[256,256]{1,0:T(8,128)(2,1)S(1)}, u32[]{:S(2)}, u32[]{:S(2)}) %collective-permute-start.5) | collective-permute-done | bytes 131104 | tf_op jit(solution)/shard_map/ppermute | solution.py:661
  43.2 2.0 %collective-permute-done.6.refs_3_ = bf16[256,256]{1,0:T(8,128)(2,1)S(1)} collective-permute-done((bf16[256,256]{1,0:T(8,128)(2,1)S(1)}, bf16[256,256]{1,0:T(8,128)(2,1)S(1)}, u32[]{:S(2)}, u32[]{:S(2)}) %collective-permute-start.6) | collective-permute-done | bytes 131104 | tf_op jit(solution)/shard_map/ppermute | solution.py:661
  45.1 4.3 %shard_map.99 = bf16[32,8,16,128]{3,2,1,0:T(8,128)(2,1)} custom-call(s32[2]{0:T(128)S(1)} %pad_add_fusion.ids_ref, bf16[256,256]{1,0:T(8,128)(2,1)S(1)} %collective-permute-done.3.refs_0_, bf16[256,256]{1,0:T(8,128)(2,1)S(1)} %collective-permute-done.4.refs_1_, bf16[256,256]{1,0:T(8,128)(2,1)S(1)} %collective-permute-done.5.refs_2_, ...), custom_call_target="tpu_custom_call" | custom-call | flops 1000 | bytes 1000 | tf_op jit(solution)/shard_map/pallas_call | solution.py:642
Async XLA Ops:
  0.0 7.1 %copy-start.6 = (s32[512,1]{0,1:T(1,128)S(1)}, s32[512,1]{0,1:T(1,128)}, u32[]{:S(2)}) copy-start(s32[512,1]{0,1:T(1,128)} %param.16) | copy-start | bytes 6148
  0.0 7.1 %copy-start.7 = (s32[512]{0:T(512)S(1)}, s32[512]{0:T(512)}, u32[]{:S(2)}) copy-start(s32[512]{0:T(512)} %param.17) | copy-start | bytes 6148
  0.0 7.1 %copy-start.4 = (bf16[32,32]{1,0:T(8,128)(2,1)S(1)}, bf16[32,32]{1,0:T(8,128)(2,1)}, u32[]{:S(2)}) copy-start(bf16[32,32]{1,0:T(8,128)(2,1)} %point_ref.1) | copy-start | bytes 6148
  0.1 1.2 %copy-start = (bf16[4,4,32768]{2,1,0:T(4,128)(2,1)S(1)}, bf16[4,4,32768]{2,1,0:T(4,128)(2,1)}, u32[]{:S(2)}) copy-start(bf16[4,4,32768]{2,1,0:T(4,128)(2,1)} %field_ref.3) | copy-start | bytes 3145732
  1.3 5.8 %copy-start.2 = (bf16[512,32]{0,1:T(8,128)(2,1)S(1)}, bf16[512,32]{0,1:T(8,128)(2,1)}, u32[]{:S(2)}) copy-start(bf16[512,32]{0,1:T(8,128)(2,1)} %param.15) | copy-start | bytes 98308
  1.3 5.8 %copy-start.3 = (f32[7,7,32]{2,1,0:T(8,128)S(1)}, f32[7,7,32]{2,1,0:T(8,128)}, u32[]{:S(2)}) copy-start(f32[7,7,32]{2,1,0:T(8,128)} %depth_ref.1) | copy-start | bytes 18820
  3.3 7.7 %collective-permute-start.1 = (bf16[3,4,128,256]{3,2,1,0:T(8,128)(2,1)S(1)}, bf16[3,4,128,256]{3,2,1,0:T(8,128)(2,1)S(1)}, u32[]{:S(2)}, u32[]{:S(2)}) collective-permute-start(bf16[3,4,128,256]{3,2,1,0:T(8,128)(2,1)S(1)} %get-tuple-element.24), channel_id=1, source_target_pairs={{0,8},{8,0},{16,24},{24,16},{1,9},{9,1},{17,25},{25,17},{2,10},{10... | collective-permute-start | bytes 2359304 | tf_op jit(solution)/shard_map/ppermute | solution.py:683
  4.1 13.3 %collective-permute-start = (bf16[3,4,128,256]{3,2,1,0:T(8,128)(2,1)S(1)}, bf16[3,4,128,256]{3,2,1,0:T(8,128)(2,1)S(1)}, u32[]{:S(2)}, u32[]{:S(2)}) collective-permute-start(bf16[3,4,128,256]{3,2,1,0:T(8,128)(2,1)S(1)} %shard_map.91), channel_id=1, source_target_pairs={{8,16},{16,8},{9,17},{17,9},{10,18},{18,10},{11,19},{19,11},{12,20... | collective-permute-start | bytes 2359304 | tf_op jit(solution)/shard_map/ppermute | solution.py:682
  8.7 5.7 %collective-permute-start.2 = (bf16[4,48,128]{2,1,0:T(8,128)(2,1)S(1)}, bf16[4,48,128]{2,1,0:T(8,128)(2,1)S(1)}, u32[]{:S(2)}, u32[]{:S(2)}) collective-permute-start(bf16[4,48,128]{2,1,0:T(8,128)(2,1)S(1)} %get-tuple-element.27), channel_id=1, source_target_pairs={{0,4},{1,5},{2,6},{3,7},{4,0},{5,1},{6,2},{7,3},{8,12},{9,13},{10,... | collective-permute-start | bytes 147464 | tf_op jit(solution)/shard_map/ppermute | solution.py:661
  11.1 6.3 %copy-start.8 = (f32[32]{0:T(128)S(1)}, f32[32]{0:T(128)}, u32[]{:S(2)}) copy-start(f32[32]{0:T(128)} %param.12) | copy-start | bytes 388
  17.4 11.7 %copy-start.1 = (bf16[2,288,32]{1,2,0:T(8,128)(2,1)S(1)}, bf16[2,288,32]{1,2,0:T(8,128)(2,1)}, u32[]{:S(2)}) copy-start(bf16[2,288,32]{1,2,0:T(8,128)(2,1)} %param.13) | copy-start | bytes 110596
  20.1 12.3 %copy-start.5 = (f32[2,32]{1,0:T(2,128)S(1)}, f32[2,32]{1,0:T(2,128)}, u32[]{:S(2)}) copy-start(f32[2,32]{1,0:T(2,128)} %refs_9_.1) | copy-start | bytes 772
  20.2 6.0 %collective-permute-start.7 = (bf16[304,256]{1,0:T(8,128)(2,1)S(1)}, bf16[304,256]{1,0:T(8,128)(2,1)S(1)}, u32[]{:S(2)}, u32[]{:S(2)}) collective-permute-start(bf16[304,256]{1,0:T(8,128)(2,1)S(1)} %get-tuple-element.33), channel_id=1, source_target_pairs={{0,1},{1,0},{2,3},{3,2},{4,5},{5,4},{6,7},{7,6},{8,9},{9,8},{10,11... | collective-permute-start | bytes 466952 | tf_op jit(solution)/shard_map/ppermute | solution.py:661
  21.5 6.3 %collective-permute-start.8 = (bf16[304,256]{1,0:T(8,128)(2,1)S(1)}, bf16[304,256]{1,0:T(8,128)(2,1)S(1)}, u32[]{:S(2)}, u32[]{:S(2)}) collective-permute-start(bf16[304,256]{1,0:T(8,128)(2,1)S(1)} %get-tuple-element.34), channel_id=1, source_target_pairs={{0,2},{1,3},{2,0},{3,1},{4,6},{5,7},{6,4},{7,5},{8,10},{9,11},{10,... | collective-permute-start | bytes 466952 | tf_op jit(solution)/shard_map/ppermute | solution.py:661
  21.6 8.9 %collective-permute-start.9 = (bf16[304,256]{1,0:T(8,128)(2,1)S(1)}, bf16[304,256]{1,0:T(8,128)(2,1)S(1)}, u32[]{:S(2)}, u32[]{:S(2)}) collective-permute-start(bf16[304,256]{1,0:T(8,128)(2,1)S(1)} %get-tuple-element.35), channel_id=1, source_target_pairs={{0,3},{1,2},{2,1},{3,0},{4,7},{5,6},{6,5},{7,4},{8,11},{9,10},{10,... | collective-permute-start | bytes 466952 | tf_op jit(solution)/shard_map/ppermute | solution.py:661
  22.9 14.8 %collective-permute-start.3 = (bf16[256,256]{1,0:T(8,128)(2,1)S(1)}, bf16[256,256]{1,0:T(8,128)(2,1)S(1)}, u32[]{:S(2)}, u32[]{:S(2)}) collective-permute-start(bf16[256,256]{1,0:T(8,128)(2,1)S(1)} %get-tuple-element.28), channel_id=1, source_target_pairs={{0,4},{1,5},{2,6},{3,7},{4,0},{5,1},{6,2},{7,3},{8,12},{9,13},{10,... | collective-permute-start | bytes 393224 | tf_op jit(solution)/shard_map/ppermute | solution.py:661
  25.2 15.3 %collective-permute-start.4 = (bf16[256,256]{1,0:T(8,128)(2,1)S(1)}, bf16[256,256]{1,0:T(8,128)(2,1)S(1)}, u32[]{:S(2)}, u32[]{:S(2)}) collective-permute-start(bf16[256,256]{1,0:T(8,128)(2,1)S(1)} %get-tuple-element.29), channel_id=1, source_target_pairs={{0,5},{1,4},{2,7},{3,6},{4,1},{5,0},{6,3},{7,2},{8,13},{9,12},{10,... | collective-permute-start | bytes 393224 | tf_op jit(solution)/shard_map/ppermute | solution.py:661
  26.2 17.0 %collective-permute-start.5 = (bf16[256,256]{1,0:T(8,128)(2,1)S(1)}, bf16[256,256]{1,0:T(8,128)(2,1)S(1)}, u32[]{:S(2)}, u32[]{:S(2)}) collective-permute-start(bf16[256,256]{1,0:T(8,128)(2,1)S(1)} %get-tuple-element.30), channel_id=1, source_target_pairs={{0,6},{1,7},{2,4},{3,5},{4,2},{5,3},{6,0},{7,1},{8,14},{9,15},{10,... | collective-permute-start | bytes 393224 | tf_op jit(solution)/shard_map/ppermute | solution.py:661
  27.8 17.3 %collective-permute-start.6 = (bf16[256,256]{1,0:T(8,128)(2,1)S(1)}, bf16[256,256]{1,0:T(8,128)(2,1)S(1)}, u32[]{:S(2)}, u32[]{:S(2)}) collective-permute-start(bf16[256,256]{1,0:T(8,128)(2,1)S(1)} %get-tuple-element.31), channel_id=1, source_target_pairs={{0,7},{1,6},{2,5},{3,4},{4,3},{5,2},{6,1},{7,0},{8,15},{9,14},{10,... | collective-permute-start | bytes 393224 | tf_op jit(solution)/shard_map/ppermute | solution.py:661

commit v7 on v6

--- a/solution.py
+++ b/solution.py
@@ -47,27 +47,28 @@
     return (column == (row % outer) * inner + row // outer).astype(BF16)
 
 
-def segment_kernel(only_cross, ids_ref, field_ref, own_ref, halo_ref):
-    if only_cross:
-        own_ref, halo_ref = halo_ref, own_ref
+def segment_kernel(only_cross, ids_ref, field_ref, *out_refs):
     levels, height, lanes = field_ref.shape
     rows = levels * height
     group = 256 // rows
-    swap = swap_matrix(group, rows)
+    odd = ids_ref[1] % 2
+    count = 3 if only_cross else height
+    first = odd * (height - 3) if only_cross else 0
+    row = lax.broadcasted_iota(jnp.int32, (count * levels * group, 256), 0)
+    column = lax.broadcasted_iota(jnp.int32, (count * levels * group, 256), 1)
+    line = row // group
+    wanted = row % group * rows + line % levels * height + line // levels + first
+    turn = (column == wanted).astype(BF16)
     for g in range(lanes // (group * SL)):
         at = [(g * group + s) * SL for s in range(group)]
         pieces = [field_ref[:, :, n : n + SL].reshape(rows, SL) for n in at]
         got = jnp.dot(
-            swap, jnp.concatenate(pieces, axis=0), preferred_element_type=F32
+            turn, jnp.concatenate(pieces, axis=0), preferred_element_type=F32
         ).astype(BF16)
-        for z in range(levels):
-            for y in range(height):
-                start = (z * height + y) * group
-                own_ref[y, z, g * group : (g + 1) * group] = got[start : start + group]
-    odd = ids_ref[1] % 2
-    first = odd if only_cross else 1 - odd
-    for y in range(3):
-        halo_ref[y] = own_ref[first * (height - 3) + y]
+        out_refs[0][:, :, g * group : (g + 1) * group] = got.reshape(count, levels, group, SL)
+    if not only_cross:
+        for y in range(3):
+            out_refs[1][y] = out_refs[0][(1 - odd) * (height - 3) + y]
 
 
 def to_segments(ids, field, only_cross):
@@ -80,7 +81,6 @@
         in_specs=[pl.BlockSpec(memory_space=pltpu.SMEM), full],
         out_specs=[full] if only_cross else [full] * 2,
         out_shape=[out(3)] if only_cross else [out(height), out(3)],
-        scratch_shapes=[pltpu.VMEM(shape(height), BF16)] if only_cross else [],
         compiler_params=params(),
         cost_estimate=cost(1000, 1000),
     )(ids, field)

time: 49.8 us -> 49.7 us (level)
  no operation moved by 1% of the time
where the time goes in v7:
time: 49.7 us; the launch traced here: 49.4 us
  Pallas kernels  18.8 us (38%)
  starting transfers between devices  15.1 us (30%)
  waiting for transfers between devices  14 us (28%)
  local copies, waits for them, and re-layouts  1.26 us (3%)
    ppermute x8, starting transfers between devices, exchange(): lax.ppermute(block, 'cols', [(i, i ^ distance) for i in range(count)])  11.3 us
    ppermute x8, waiting for transfers between devices, exchange(): lax.ppermute(block, 'cols', [(i, i ^ distance) for i in range(count)])  11 us
    pallas_call x1, Pallas kernels, vertical(): pl.pallas_call(functools.partial(far_kernel, tiles, height), in_specs=[sm...  4.31 us
    pallas_call x1, Pallas kernels, early_horizontal(): pl.pallas_call(early_kernel, in_specs=[pl.BlockSpec(memory_space=pltpu.SM...  3.31 us
    ppermute x1, starting transfers between devices, body(): cross = lax.ppermute(cross, 'rows', beyond)  3.02 us
    ppermute x1, waiting for transfers between devices, body(): cross = lax.ppermute(cross, 'rows', beyond)  2.99 us
    pallas_call x1, Pallas kernels, finish_horizontal(): pl.pallas_call(finish_kernel, in_specs=[pl.BlockSpec(memory_space=pltpu.S...  2.74 us
    pallas_call x2, Pallas kernels, to_segments(): pl.pallas_call(functools.partial(segment_kernel, only_cross), in_specs=[p...  1.97 us
  transfers between devices with their start and end apart: 10, of which 6 were waited for; matrix products, arithmetic and copies ran while one was open for 0% of the time, Pallas kernels for 20%

profile of v7, /device:TPU:9, one launch (start us, length us, event | category | flops | bytes accessed | tf_op | source)
XLA Modules:
  0.0 49.4 jit_solution(6823957399793209415)
XLA Ops:
  0.0 0.0 copy-start.6
  0.0 0.0 copy-start.7
  0.0 0.0 copy-start.4
  0.0 0.1 pad_add_fusion.ids_ref
  0.1 0.0 copy-start
  0.1 1.2 %copy-done = bf16[4,4,32768]{2,1,0:T(4,128)(2,1)S(1)} copy-done((bf16[4,4,32768]{2,1,0:T(4,128)(2,1)S(1)}, bf16[4,4,32768]{2,1,0:T(4,128)(2,1)}, u32[]{:S(2)}) %copy-start) | copy-done | bytes 1048600
  1.3 0.0 copy-start.2
  1.3 0.0 copy-start.3
  1.3 0.9 %shard_map.91 = bf16[3,4,128,256]{3,2,1,0:T(8,128)(2,1)S(1)} custom-call(s32[2]{0:T(128)S(1)} %pad_add_fusion.ids_ref, bf16[4,4,32768]{2,1,0:T(4,128)(2,1)S(1)} %copy-done), custom_call_target="tpu_custom_call" | custom-call | flops 1000 | bytes 1000 | tf_op jit(solution)/shard_map/pallas_call | solution.py:79
  2.3 1.0 %shard_map.92 = (bf16[4,4,128,256]{3,2,1,0:T(8,128)(2,1)S(1)}, bf16[3,4,128,256]{3,2,1,0:T(8,128)(2,1)S(1)}) custom-call(s32[2]{0:T(128)S(1)} %pad_add_fusion.ids_ref, bf16[4,4,32768]{2,1,0:T(4,128)(2,1)S(1)} %copy-done), custom_call_target="tpu_custom_call" | custom-call | flops 1000 | bytes 1000 | tf_op jit(solution)/shard_map/pallas_call | solution.py:79
  3.3 0.8 %collective-permute-start.1 = (bf16[3,4,128,256]{3,2,1,0:T(8,128)(2,1)S(1)}, bf16[3,4,128,256]{3,2,1,0:T(8,128)(2,1)S(1)}, u32[]{:S(2)}, u32[]{:S(2)}) collective-permute-start(bf16[3,4,128,256]{3,2,1,0:T(8,128)(2,1)S(1)} %get-tuple-element.24), channel_id=1, source_target_pairs={{0,8},{8,0},{16,24},{24,16},{1,9},{9,1},{17,25},{25,17},{2,10},{10... | collective-permute-start | bytes 2359304 | tf_op jit(solution)/shard_map/ppermute | solution.py:683
  4.1 3.0 %collective-permute-start = (bf16[3,4,128,256]{3,2,1,0:T(8,128)(2,1)S(1)}, bf16[3,4,128,256]{3,2,1,0:T(8,128)(2,1)S(1)}, u32[]{:S(2)}, u32[]{:S(2)}) collective-permute-start(bf16[3,4,128,256]{3,2,1,0:T(8,128)(2,1)S(1)} %shard_map.91), channel_id=1, source_target_pairs={{8,16},{16,8},{9,17},{17,9},{10,18},{18,10},{11,19},{19,11},{12,20... | collective-permute-start | bytes 2359304 | tf_op jit(solution)/shard_map/ppermute | solution.py:682
  7.1 0.0 copy-done.6
  7.1 0.0 copy-done.7
  7.1 0.0 copy-done.4
  7.1 0.0 copy-done.2
  7.1 0.0 copy-done.3
  7.1 1.5 %shard_map.93 = (bf16[4608,256]{1,0:T(8,128)(2,1)S(1)}, bf16[4,48,128]{2,1,0:T(8,128)(2,1)S(1)}, bf16[4,48,128]{2,1,0:T(8,128)(2,1)S(1)}) custom-call(s32[2]{0:T(128)S(1)} %pad_add_fusion.ids_ref, f32[7,7,32]{2,1,0:T(8,128)S(1)} %copy-done.3, bf16[32,32]{1,0:T(8,128)(2,1)S(1)} %copy-done.4, bf16[32,512]{1,0:T(8,128)(2,1)S(1)} %bitcast.13, ...), custom_call_target="tpu_custom_call" | custom-call | flops 1000 | bytes 1000 | tf_op jit(solution)/shard_map/pallas_call | solution.py:447
  8.7 2.4 %collective-permute-start.2 = (bf16[4,48,128]{2,1,0:T(8,128)(2,1)S(1)}, bf16[4,48,128]{2,1,0:T(8,128)(2,1)S(1)}, u32[]{:S(2)}, u32[]{:S(2)}) collective-permute-start(bf16[4,48,128]{2,1,0:T(8,128)(2,1)S(1)} %get-tuple-element.27), channel_id=1, source_target_pairs={{0,4},{1,5},{2,6},{3,7},{4,0},{5,1},{6,2},{7,3},{8,12},{9,13},{10,... | collective-permute-start | bytes 147464 | tf_op jit(solution)/shard_map/ppermute | solution.py:661
  11.0 0.0 collective-permute-done.1.pair_ref
  11.0 0.0 copy-start.8
  11.0 3.3 %shard_map.94.early_ref = f32[2,4,2,128,256]{4,3,2,1,0:T(8,128)S(1)} custom-call(s32[2]{0:T(128)S(1)} %pad_add_fusion.ids_ref, bf16[4,4,128,256]{3,2,1,0:T(8,128)(2,1)S(1)} %get-tuple-element.23.own_ref, bf16[3,4,128,256]{3,2,1,0:T(8,128)(2,1)S(1)} %collective-permute-done.1.pair_ref, bf16[4608,256]{1,0:T(8,128)(2,1)S(1)} %get-tuple-element.25.weight_ref), custom_call_target="tpu_custom_call" | custom-call | flops 1000 | bytes 1000 | tf_op jit(solution)/shard_map/pallas_call | solution.py:286
  14.4 0.0 collective-permute-done.2.rest_1_
  14.4 3.0 %collective-permute-done.cross_ref = bf16[3,4,128,256]{3,2,1,0:T(8,128)(2,1)S(1)} collective-permute-done((bf16[3,4,128,256]{3,2,1,0:T(8,128)(2,1)S(1)}, bf16[3,4,128,256]{3,2,1,0:T(8,128)(2,1)S(1)}, u32[]{:S(2)}, u32[]{:S(2)}) %collective-permute-start) | collective-permute-done | bytes 786464 | tf_op jit(solution)/shard_map/ppermute | solution.py:682
  17.4 0.0 copy-done.8
  17.4 0.0 copy-start.1
  17.4 2.7 %shard_map.95 = (bf16[304,256]{1,0:T(8,128)(2,1)S(1)}, bf16[304,256]{1,0:T(8,128)(2,1)S(1)}, bf16[304,256]{1,0:T(8,128)(2,1)S(1)}, bf16[304,256]{1,0:T(8,128)(2,...) custom-call(s32[2]{0:T(128)S(1)} %pad_add_fusion.ids_ref, ...), custom_call_target="tpu_custom_call" | custom-call | flops 1000 | bytes 1000 | tf_op jit(solution)/shard_map/pallas_call | solution.py:349
  20.1 0.0 copy-start.5
  20.1 1.3 %collective-permute-start.7 = (bf16[304,256]{1,0:T(8,128)(2,1)S(1)}, bf16[304,256]{1,0:T(8,128)(2,1)S(1)}, u32[]{:S(2)}, u32[]{:S(2)}) collective-permute-start(bf16[304,256]{1,0:T(8,128)(2,1)S(1)} %get-tuple-element.33), channel_id=1, source_target_pairs={{0,1},{1,0},{2,3},{3,2},{4,5},{5,4},{6,7},{7,6},{8,9},{9,8},{10,11... | collective-permute-start | bytes 466952 | tf_op jit(solution)/shard_map/ppermute | solution.py:661
  21.4 0.2 collective-permute-start.8
  21.6 1.2 %collective-permute-start.9 = (bf16[304,256]{1,0:T(8,128)(2,1)S(1)}, bf16[304,256]{1,0:T(8,128)(2,1)S(1)}, u32[]{:S(2)}, u32[]{:S(2)}) collective-permute-start(bf16[304,256]{1,0:T(8,128)(2,1)S(1)} %get-tuple-element.35), channel_id=1, source_target_pairs={{0,3},{1,2},{2,1},{3,0},{4,7},{5,6},{6,5},{7,4},{8,11},{9,10},{10,... | collective-permute-start | bytes 466952 | tf_op jit(solution)/shard_map/ppermute | solution.py:661
  22.8 2.3 %collective-permute-start.3 = (bf16[256,256]{1,0:T(8,128)(2,1)S(1)}, bf16[256,256]{1,0:T(8,128)(2,1)S(1)}, u32[]{:S(2)}, u32[]{:S(2)}) collective-permute-start(bf16[256,256]{1,0:T(8,128)(2,1)S(1)} %get-tuple-element.28), channel_id=1, source_target_pairs={{0,4},{1,5},{2,6},{3,7},{4,0},{5,1},{6,2},{7,3},{8,12},{9,13},{10,... | collective-permute-start | bytes 393224 | tf_op jit(solution)/shard_map/ppermute | solution.py:661
  25.1 1.0 %collective-permute-start.4 = (bf16[256,256]{1,0:T(8,128)(2,1)S(1)}, bf16[256,256]{1,0:T(8,128)(2,1)S(1)}, u32[]{:S(2)}, u32[]{:S(2)}) collective-permute-start(bf16[256,256]{1,0:T(8,128)(2,1)S(1)} %get-tuple-element.29), channel_id=1, source_target_pairs={{0,5},{1,4},{2,7},{3,6},{4,1},{5,0},{6,3},{7,2},{8,13},{9,12},{10,... | collective-permute-start | bytes 393224 | tf_op jit(solution)/shard_map/ppermute | solution.py:661
  26.2 0.0 collective-permute-done.7.refs_1_
  26.2 1.6 %collective-permute-start.5 = (bf16[256,256]{1,0:T(8,128)(2,1)S(1)}, bf16[256,256]{1,0:T(8,128)(2,1)S(1)}, u32[]{:S(2)}, u32[]{:S(2)}) collective-permute-start(bf16[256,256]{1,0:T(8,128)(2,1)S(1)} %get-tuple-element.30), channel_id=1, source_target_pairs={{0,6},{1,7},{2,4},{3,5},{4,2},{5,3},{6,0},{7,1},{8,14},{9,15},{10,... | collective-permute-start | bytes 393224 | tf_op jit(solution)/shard_map/ppermute | solution.py:661
  27.8 0.0 collective-permute-done.8.refs_2_
  27.8 1.3 %collective-permute-start.6 = (bf16[256,256]{1,0:T(8,128)(2,1)S(1)}, bf16[256,256]{1,0:T(8,128)(2,1)S(1)}, u32[]{:S(2)}, u32[]{:S(2)}) collective-permute-start(bf16[256,256]{1,0:T(8,128)(2,1)S(1)} %get-tuple-element.31), channel_id=1, source_target_pairs={{0,7},{1,6},{2,5},{3,4},{4,3},{5,2},{6,1},{7,0},{8,15},{9,14},{10,... | collective-permute-start | bytes 393224 | tf_op jit(solution)/shard_map/ppermute | solution.py:661
  29.1 0.0 copy-done.1
  29.1 1.2 %shard_map.97.refs_5_.refs_8_ = bf16[2,768,256]{2,1,0:T(8,128)(2,1)S(1)} custom-call(s32[2]{0:T(128)S(1)} %pad_add_fusion.ids_ref, bf16[2,32,288]{2,1,0:T(8,128)(2,1)S(1)} %bitcast.12), custom_call_target="tpu_custom_call" | custom-call | flops 1000 | bytes 1000 | tf_op jit(solution)/shard_map/pallas_call | solution.py:154
  30.2 0.3 collective-permute-done.9.refs_3_
  30.5 1.9 %shard_map.96.refs_4_.refs_7_ = f32[2048,256]{1,0:T(8,128)S(1)} custom-call(s32[2]{0:T(128)S(1)} %pad_add_fusion.ids_ref, bf16[304,256]{1,0:T(8,128)(2,1)S(1)} %get-tuple-element.32.refs_0_, bf16[304,256]{1,0:T(8,128)(2,1)S(1)} %collective-permute-done.7.refs_1_, bf16[304,256]{1,0:T(8,128)(2,1)S(1)} %collective-permute-done.8.refs_2_, ...), custom_call_target="tpu_custom_call" | custom-call | flops 1000 | bytes 1000 | tf_op jit(solution)/shard_map/pallas_call | solution.py:426
  32.4 0.0 copy-done.5
  32.4 2.0 %shard_map.98 = (bf16[8,8,16,128]{3,2,1,0:T(8,128)(2,1)S(1)}, bf16[512,256]{1,0:T(8,128)(2,1)S(1)}, bf16[512,256]{1,0:T(8,128)(2,1)S(1)}) custom-call(s32[2]{0:T(128)S(1)} %pad_add_fusion.ids_ref, bf16[304,256]{1,0:T(8,128)(2,1)S(1)} %get-tuple-element.32.refs_0_, bf16[304,256]{1,0:T(8,128)(2,1)S(1)} %collective-permute-done.7.refs_1_, ...), custom_call_target="tpu_custom_call" | custom-call | flops 1000 | bytes 1000 | tf_op jit(solution)/shard_map/pallas_call | solution.py:633
  34.4 3.2 %collective-permute-done.3.refs_0_ = bf16[256,256]{1,0:T(8,128)(2,1)S(1)} collective-permute-done((bf16[256,256]{1,0:T(8,128)(2,1)S(1)}, bf16[256,256]{1,0:T(8,128)(2,1)S(1)}, u32[]{:S(2)}, u32[]{:S(2)}) %collective-permute-start.3) | collective-permute-done | bytes 131104 | tf_op jit(solution)/shard_map/ppermute | solution.py:661
  37.6 2.8 %collective-permute-done.4.refs_1_ = bf16[256,256]{1,0:T(8,128)(2,1)S(1)} collective-permute-done((bf16[256,256]{1,0:T(8,128)(2,1)S(1)}, bf16[256,256]{1,0:T(8,128)(2,1)S(1)}, u32[]{:S(2)}, u32[]{:S(2)}) %collective-permute-start.4) | collective-permute-done | bytes 131104 | tf_op jit(solution)/shard_map/ppermute | solution.py:661
  40.4 2.7 %collective-permute-done.5.refs_2_ = bf16[256,256]{1,0:T(8,128)(2,1)S(1)} collective-permute-done((bf16[256,256]{1,0:T(8,128)(2,1)S(1)}, bf16[256,256]{1,0:T(8,128)(2,1)S(1)}, u32[]{:S(2)}, u32[]{:S(2)}) %collective-permute-start.5) | collective-permute-done | bytes 131104 | tf_op jit(solution)/shard_map/ppermute | solution.py:661
  43.1 2.0 %collective-permute-done.6.refs_3_ = bf16[256,256]{1,0:T(8,128)(2,1)S(1)} collective-permute-done((bf16[256,256]{1,0:T(8,128)(2,1)S(1)}, bf16[256,256]{1,0:T(8,128)(2,1)S(1)}, u32[]{:S(2)}, u32[]{:S(2)}) %collective-permute-start.6) | collective-permute-done | bytes 131104 | tf_op jit(solution)/shard_map/ppermute | solution.py:661
  45.1 4.3 %shard_map.99 = bf16[32,8,16,128]{3,2,1,0:T(8,128)(2,1)} custom-call(s32[2]{0:T(128)S(1)} %pad_add_fusion.ids_ref, bf16[256,256]{1,0:T(8,128)(2,1)S(1)} %collective-permute-done.3.refs_0_, bf16[256,256]{1,0:T(8,128)(2,1)S(1)} %collective-permute-done.4.refs_1_, bf16[256,256]{1,0:T(8,128)(2,1)S(1)} %collective-permute-done.5.refs_2_, ...), custom_call_target="tpu_custom_call" | custom-call | flops 1000 | bytes 1000 | tf_op jit(solution)/shard_map/pallas_call | solution.py:642
Async XLA Ops:
  0.0 7.1 %copy-start.6 = (s32[512,1]{0,1:T(1,128)S(1)}, s32[512,1]{0,1:T(1,128)}, u32[]{:S(2)}) copy-start(s32[512,1]{0,1:T(1,128)} %param.16) | copy-start | bytes 6148
  0.0 7.1 %copy-start.7 = (s32[512]{0:T(512)S(1)}, s32[512]{0:T(512)}, u32[]{:S(2)}) copy-start(s32[512]{0:T(512)} %param.17) | copy-start | bytes 6148
  0.0 7.1 %copy-start.4 = (bf16[32,32]{1,0:T(8,128)(2,1)S(1)}, bf16[32,32]{1,0:T(8,128)(2,1)}, u32[]{:S(2)}) copy-start(bf16[32,32]{1,0:T(8,128)(2,1)} %point_ref.1) | copy-start | bytes 6148
  0.1 1.2 %copy-start = (bf16[4,4,32768]{2,1,0:T(4,128)(2,1)S(1)}, bf16[4,4,32768]{2,1,0:T(4,128)(2,1)}, u32[]{:S(2)}) copy-start(bf16[4,4,32768]{2,1,0:T(4,128)(2,1)} %field_ref.3) | copy-start | bytes 3145732
  1.3 5.8 %copy-start.2 = (bf16[512,32]{0,1:T(8,128)(2,1)S(1)}, bf16[512,32]{0,1:T(8,128)(2,1)}, u32[]{:S(2)}) copy-start(bf16[512,32]{0,1:T(8,128)(2,1)} %param.15) | copy-start | bytes 98308
  1.3 5.8 %copy-start.3 = (f32[7,7,32]{2,1,0:T(8,128)S(1)}, f32[7,7,32]{2,1,0:T(8,128)}, u32[]{:S(2)}) copy-start(f32[7,7,32]{2,1,0:T(8,128)} %depth_ref.1) | copy-start | bytes 18820
  3.3 7.7 %collective-permute-start.1 = (bf16[3,4,128,256]{3,2,1,0:T(8,128)(2,1)S(1)}, bf16[3,4,128,256]{3,2,1,0:T(8,128)(2,1)S(1)}, u32[]{:S(2)}, u32[]{:S(2)}) collective-permute-start(bf16[3,4,128,256]{3,2,1,0:T(8,128)(2,1)S(1)} %get-tuple-element.24), channel_id=1, source_target_pairs={{0,8},{8,0},{16,24},{24,16},{1,9},{9,1},{17,25},{25,17},{2,10},{10... | collective-permute-start | bytes 2359304 | tf_op jit(solution)/shard_map/ppermute | solution.py:683
  4.1 13.3 %collective-permute-start = (bf16[3,4,128,256]{3,2,1,0:T(8,128)(2,1)S(1)}, bf16[3,4,128,256]{3,2,1,0:T(8,128)(2,1)S(1)}, u32[]{:S(2)}, u32[]{:S(2)}) collective-permute-start(bf16[3,4,128,256]{3,2,1,0:T(8,128)(2,1)S(1)} %shard_map.91), channel_id=1, source_target_pairs={{8,16},{16,8},{9,17},{17,9},{10,18},{18,10},{11,19},{19,11},{12,20... | collective-permute-start | bytes 2359304 | tf_op jit(solution)/shard_map/ppermute | solution.py:682
  8.7 5.7 %collective-permute-start.2 = (bf16[4,48,128]{2,1,0:T(8,128)(2,1)S(1)}, bf16[4,48,128]{2,1,0:T(8,128)(2,1)S(1)}, u32[]{:S(2)}, u32[]{:S(2)}) collective-permute-start(bf16[4,48,128]{2,1,0:T(8,128)(2,1)S(1)} %get-tuple-element.27), channel_id=1, source_target_pairs={{0,4},{1,5},{2,6},{3,7},{4,0},{5,1},{6,2},{7,3},{8,12},{9,13},{10,... | collective-permute-start | bytes 147464 | tf_op jit(solution)/shard_map/ppermute | solution.py:661
  11.0 6.3 %copy-start.8 = (f32[32]{0:T(128)S(1)}, f32[32]{0:T(128)}, u32[]{:S(2)}) copy-start(f32[32]{0:T(128)} %param.12) | copy-start | bytes 388
  17.4 11.7 %copy-start.1 = (bf16[2,288,32]{1,2,0:T(8,128)(2,1)S(1)}, bf16[2,288,32]{1,2,0:T(8,128)(2,1)}, u32[]{:S(2)}) copy-start(bf16[2,288,32]{1,2,0:T(8,128)(2,1)} %param.13) | copy-start | bytes 110596
  20.1 12.3 %copy-start.5 = (f32[2,32]{1,0:T(2,128)S(1)}, f32[2,32]{1,0:T(2,128)}, u32[]{:S(2)}) copy-start(f32[2,32]{1,0:T(2,128)} %refs_9_.1) | copy-start | bytes 772
  20.1 6.0 %collective-permute-start.7 = (bf16[304,256]{1,0:T(8,128)(2,1)S(1)}, bf16[304,256]{1,0:T(8,128)(2,1)S(1)}, u32[]{:S(2)}, u32[]{:S(2)}) collective-permute-start(bf16[304,256]{1,0:T(8,128)(2,1)S(1)} %get-tuple-element.33), channel_id=1, source_target_pairs={{0,1},{1,0},{2,3},{3,2},{4,5},{5,4},{6,7},{7,6},{8,9},{9,8},{10,11... | collective-permute-start | bytes 466952 | tf_op jit(solution)/shard_map/ppermute | solution.py:661
  21.4 6.3 %collective-permute-start.8 = (bf16[304,256]{1,0:T(8,128)(2,1)S(1)}, bf16[304,256]{1,0:T(8,128)(2,1)S(1)}, u32[]{:S(2)}, u32[]{:S(2)}) collective-permute-start(bf16[304,256]{1,0:T(8,128)(2,1)S(1)} %get-tuple-element.34), channel_id=1, source_target_pairs={{0,2},{1,3},{2,0},{3,1},{4,6},{5,7},{6,4},{7,5},{8,10},{9,11},{10,... | collective-permute-start | bytes 466952 | tf_op jit(solution)/shard_map/ppermute | solution.py:661
  21.6 8.9 %collective-permute-start.9 = (bf16[304,256]{1,0:T(8,128)(2,1)S(1)}, bf16[304,256]{1,0:T(8,128)(2,1)S(1)}, u32[]{:S(2)}, u32[]{:S(2)}) collective-permute-start(bf16[304,256]{1,0:T(8,128)(2,1)S(1)} %get-tuple-element.35), channel_id=1, source_target_pairs={{0,3},{1,2},{2,1},{3,0},{4,7},{5,6},{6,5},{7,4},{8,11},{9,10},{10,... | collective-permute-start | bytes 466952 | tf_op jit(solution)/shard_map/ppermute | solution.py:661
  22.8 14.8 %collective-permute-start.3 = (bf16[256,256]{1,0:T(8,128)(2,1)S(1)}, bf16[256,256]{1,0:T(8,128)(2,1)S(1)}, u32[]{:S(2)}, u32[]{:S(2)}) collective-permute-start(bf16[256,256]{1,0:T(8,128)(2,1)S(1)} %get-tuple-element.28), channel_id=1, source_target_pairs={{0,4},{1,5},{2,6},{3,7},{4,0},{5,1},{6,2},{7,3},{8,12},{9,13},{10,... | collective-permute-start | bytes 393224 | tf_op jit(solution)/shard_map/ppermute | solution.py:661
  25.1 15.3 %collective-permute-start.4 = (bf16[256,256]{1,0:T(8,128)(2,1)S(1)}, bf16[256,256]{1,0:T(8,128)(2,1)S(1)}, u32[]{:S(2)}, u32[]{:S(2)}) collective-permute-start(bf16[256,256]{1,0:T(8,128)(2,1)S(1)} %get-tuple-element.29), channel_id=1, source_target_pairs={{0,5},{1,4},{2,7},{3,6},{4,1},{5,0},{6,3},{7,2},{8,13},{9,12},{10,... | collective-permute-start | bytes 393224 | tf_op jit(solution)/shard_map/ppermute | solution.py:661
  26.2 17.0 %collective-permute-start.5 = (bf16[256,256]{1,0:T(8,128)(2,1)S(1)}, bf16[256,256]{1,0:T(8,128)(2,1)S(1)}, u32[]{:S(2)}, u32[]{:S(2)}) collective-permute-start(bf16[256,256]{1,0:T(8,128)(2,1)S(1)} %get-tuple-element.30), channel_id=1, source_target_pairs={{0,6},{1,7},{2,4},{3,5},{4,2},{5,3},{6,0},{7,1},{8,14},{9,15},{10,... | collective-permute-start | bytes 393224 | tf_op jit(solution)/shard_map/ppermute | solution.py:661
  27.8 17.3 %collective-permute-start.6 = (bf16[256,256]{1,0:T(8,128)(2,1)S(1)}, bf16[256,256]{1,0:T(8,128)(2,1)S(1)}, u32[]{:S(2)}, u32[]{:S(2)}) collective-permute-start(bf16[256,256]{1,0:T(8,128)(2,1)S(1)} %get-tuple-element.31), channel_id=1, source_target_pairs={{0,7},{1,6},{2,5},{3,4},{4,3},{5,2},{6,1},{7,0},{8,15},{9,14},{10,... | collective-permute-start | bytes 393224 | tf_op jit(solution)/shard_map/ppermute | solution.py:661
